TPU v7x, 512 devices: a whole 4x8x8 slice. The times are simulated.
512 devices in a mesh: dp: 32 (over y_hi, z), seqt: 16 (over y_lo, x, core).
Axes of the slice: x: 4, y: 8 (y_hi: 4, y_lo: 2; y = y_hi * 2 + y_lo), z: 8, core: 2. Of those that a mesh axis runs over, the one named last changes fastest.
Arguments:
- latent_tiles: bfloat16 [512, 64, 128], P(('dp', 'seqt')), may hold values from -6 to 6
- tile_route: int32 [512], P(('dp', 'seqt')), may hold values from 0 to 31, as said below
- image_tokens: int32 [32, 2], P('dp'), may hold values from 512 to 1024
- text_lengths: int32 [32, 2], P('dp'), may hold values from 1 to 128
- queries: bfloat16 [65536, 2048], P(('dp', 'seqt')), may hold values from -6 to 6
- key_rows: bfloat16 [65536, 2048], P(('dp', 'seqt')), may hold values from -6 to 6
- values: bfloat16 [65536, 2048], P(('dp', 'seqt')), may hold values from -48 to 48
- text_keys: bfloat16 [8192, 2048], P(('dp', 'seqt')), may hold values from -6 to 6
- text_values: bfloat16 [8192, 2048], P(('dp', 'seqt')), may hold values from -48 to 48
- query_gain: float32 [64], replicated, may hold values from 0.25 to 1.75
- key_gain: float32 [64], replicated, may hold values from 0.25 to 1.75
- residual: bfloat16 [65536, 2432], P(('dp', 'seqt')), may hold values from -6 to 6
- out_weight: bfloat16 [2048, 2432], P('seqt'), may hold values from -0.125 to 0.125
- modulation: float32 [64, 7296], P('dp'), may hold values from -3 to 3
- final_weight: bfloat16 [2432, 64], replicated, may hold values from -0.125 to 0.125
- noise_tiles: bfloat16 [512, 64, 128], P(('dp', 'seqt')), may hold values from -6 to 6
Outputs:
- velocity: float32 [512, 64, 128], P(('dp', 'seqt'))
- attention_grad: bfloat16 [65536, 2048], P(('dp', 'seqt'))
- final_grad: float32 [2432, 64], replicated
- loss_value: float32 [], replicated
Inputs may be any that keep to these rules, and one draw needn't show every extreme that they name: `tile_route`: among the tiles of the encoder ranks of one seqt index, every group is named by exactly 1 tiles.
All inputs are finite; a program needn't handle non-finite values.
Results may differ from a plain program's by a relative error of at most 0.0075.
Values may be sent and summed in bfloat16 or wider, within the bound.
No kernel may reach another device: no remote copies, remote signals or barrier semaphores. Data moves between devices by JAX's collectives and lax.ppermute only.
A program may use at most 64 MiB of HBM per device.

v0:
```python
import jax
import jax.numpy as jnp
from jax import lax
from jax.sharding import PartitionSpec as P

HD = 64
IMGS = 2


EPSILON = 1e-06


def head_norm(rows, gain):
    wide = rows.astype(jnp.float32)
    spread = jnp.mean(wide * wide, axis=-1, keepdims=True)
    return (wide * lax.rsqrt(spread + EPSILON) * gain).astype(jnp.bfloat16)


def token_layout(counts, offset, length_rows, tile_rows):
    first_count = counts[0]
    second_count = counts[1]
    border = (first_count + tile_rows - 1) // tile_rows * tile_rows
    places = offset + jnp.arange(length_rows, dtype=jnp.int32)
    owner = (places >= border).astype(jnp.int32)
    usable = (places < first_count) | (places >= border) & (places < border + second_count)
    return (owner, usable)


def text_layout(lengths, text_slots):
    places = jnp.arange(IMGS * text_slots, dtype=jnp.int32)
    owner = places // text_slots
    limit = jnp.where(owner == 0, lengths[0], lengths[1])
    usable = places % text_slots < limit
    return (owner, usable)


def local_attention(query_heads, key_heads, value_heads, owner, key_owner, key_usable):
    rows_all = query_heads.shape[0]
    heads_here = query_heads.shape[1]
    block_rows = min(512, rows_all)
    block_count = rows_all // block_rows

    def one_block(inputs):
        query_block, owner_block = inputs
        scores = jnp.einsum(
            "qhd,khd->hqk", query_block, key_heads, preferred_element_type=jnp.float32
        ) * HD ** (-0.5)
        allowed = (owner_block[:, None] == key_owner[None, :]) & key_usable[None, :]
        scores = jnp.where(allowed[None], scores, -1e30)
        largest = jnp.max(scores, axis=-1, keepdims=True)
        exponent = jnp.exp(scores - largest)
        weights = (exponent / jnp.sum(exponent, axis=-1, keepdims=True)).astype(jnp.bfloat16)
        return jnp.einsum(
            "hqk,khd->qhd", weights, value_heads, preferred_element_type=jnp.float32
        ).astype(jnp.bfloat16)

    outputs = lax.map(
        one_block,
        (
            query_heads.reshape(block_count, block_rows, heads_here, HD),
            owner.reshape(block_count, block_rows),
        ),
    )
    return outputs.reshape(rows_all, heads_here * HD)


def finish_rows(
    projected,
    owner,
    usable,
    residual_rows,
    modulate,
    final_weight,
    noise_rows,
    latent_rows,
    total_count,
):
    width = residual_rows.shape[1]
    lat_width = final_weight.shape[1]
    first_image = (owner == 0)[:, None]
    gate_rows = jnp.where(first_image, modulate[0, :width], modulate[1, :width])
    shift_rows = jnp.where(
        first_image, modulate[0, width : 2 * width], modulate[1, width : 2 * width]
    )
    scale_rows = jnp.where(first_image, modulate[0, 2 * width :], modulate[1, 2 * width :])
    hidden = residual_rows.astype(jnp.float32) + gate_rows * projected
    average = jnp.mean(hidden, axis=-1, keepdims=True)
    centered = hidden - average
    inverse = lax.rsqrt(jnp.mean(centered * centered, axis=-1, keepdims=True) + EPSILON)
    normed = centered * inverse
    mixed = (normed * (1.0 + scale_rows) + shift_rows).astype(jnp.bfloat16)
    velocity = jnp.dot(mixed, final_weight, preferred_element_type=jnp.float32)
    target = noise_rows.astype(jnp.float32) - latent_rows
    row_weight = usable.astype(jnp.float32)[:, None]
    error_rows = (velocity - target) * row_weight
    loss_part = jnp.sum(error_rows * error_rows)
    grad_velocity = (error_rows * (2.0 / (total_count * lat_width))).astype(jnp.bfloat16)
    final_part = jnp.dot(mixed.T, grad_velocity, preferred_element_type=jnp.float32)
    grad_mixed = jnp.dot(grad_velocity, final_weight.T, preferred_element_type=jnp.float32)
    grad_normed = grad_mixed * (1.0 + scale_rows)
    grad_hidden = inverse * (
        grad_normed
        - jnp.mean(grad_normed, axis=-1, keepdims=True)
        - normed * jnp.mean(grad_normed * normed, axis=-1, keepdims=True)
    )
    grad_projected = (grad_hidden * gate_rows).astype(jnp.bfloat16)
    return (velocity, grad_projected, final_part, loss_part)


def per_device(
    latent_tiles,
    tile_route,
    image_tokens,
    text_lengths,
    queries,
    key_rows,
    values,
    text_keys,
    text_values,
    query_gain,
    key_gain,
    residual,
    out_weight,
    modulation,
    final_weight,
    noise_tiles,
):
    tiles_here = latent_tiles.shape[0]
    lat_width = latent_tiles.shape[1]
    tile_rows = latent_tiles.shape[2]
    group_index = lax.axis_index("dp")
    column_index = lax.axis_index("seqt")
    routes_all = lax.all_gather(tile_route, "dp", axis=0, tiled=True)
    is_mine = (routes_all == group_index).astype(jnp.int32)
    ranked = jnp.cumsum(is_mine) - is_mine
    slot_ids = jnp.arange(tiles_here, dtype=jnp.int32)
    selector = (is_mine[None, :] * (ranked[None, :] == slot_ids[:, None]).astype(jnp.int32)).astype(
        jnp.float32
    )
    landed = jnp.einsum(
        "ik,kct->ict",
        selector,
        lax.all_gather(latent_tiles, "dp", axis=0, tiled=True).astype(jnp.float32),
        precision=lax.Precision.HIGHEST,
    )
    total_count = lax.psum(jnp.sum(image_tokens.astype(jnp.float32)), "dp")
    query_all, key_all, value_all, text_key_all, text_value_all = (
        lax.all_to_all(queries, "seqt", split_axis=1, concat_axis=0, tiled=True),
        lax.all_to_all(key_rows, "seqt", split_axis=1, concat_axis=0, tiled=True),
        lax.all_to_all(values, "seqt", split_axis=1, concat_axis=0, tiled=True),
        lax.all_to_all(text_keys, "seqt", split_axis=1, concat_axis=0, tiled=True),
        lax.all_to_all(text_values, "seqt", split_axis=1, concat_axis=0, tiled=True),
    )
    rows_group = query_all.shape[0]
    heads_here = query_all.shape[1] // HD
    text_slots = text_key_all.shape[0] // IMGS
    counts = image_tokens[0]
    lengths = text_lengths[0]
    owner, usable = token_layout(counts, 0, rows_group, tile_rows)
    text_owner, text_usable = text_layout(lengths, text_slots)
    query_heads = head_norm(query_all.reshape(rows_group, heads_here, HD), query_gain)
    key_heads = jnp.concatenate(
        [
            head_norm(key_all.reshape(rows_group, heads_here, HD), key_gain),
            head_norm(text_key_all.reshape(IMGS * text_slots, heads_here, HD), key_gain),
        ],
        axis=0,
    )
    value_heads = jnp.concatenate(
        [
            value_all.reshape(rows_group, heads_here, HD),
            text_value_all.reshape(IMGS * text_slots, heads_here, HD),
        ],
        axis=0,
    )
    key_owner = jnp.concatenate([owner, text_owner])
    key_usable = jnp.concatenate([usable, text_usable])
    attention_heads = local_attention(
        query_heads, key_heads, value_heads, owner, key_owner, key_usable
    )
    attention = lax.all_to_all(attention_heads, "seqt", split_axis=0, concat_axis=1, tiled=True)
    rows_here = attention.shape[0]
    owner_here, usable_here = token_layout(counts, column_index * rows_here, rows_here, tile_rows)
    gathered = lax.all_gather(out_weight, "seqt", axis=0, tiled=True)
    projected = jnp.dot(attention, gathered, preferred_element_type=jnp.float32)
    noise_rows = noise_tiles.transpose(0, 2, 1).reshape(rows_here, lat_width)
    latent_rows = landed.transpose(0, 2, 1).reshape(rows_here, lat_width)
    velocity, grad_projected, final_part, loss_part = finish_rows(
        projected,
        owner_here,
        usable_here,
        residual,
        modulation,
        final_weight,
        noise_rows,
        latent_rows,
        total_count,
    )
    attention_grad = jnp.dot(grad_projected, gathered.T, preferred_element_type=jnp.float32)
    final_grad, loss_sum = lax.psum((final_part, loss_part), ("dp", "seqt"))
    loss_value = loss_sum / (total_count * lat_width)
    velocity_tiles = velocity.reshape(tiles_here, tile_rows, lat_width).transpose(0, 2, 1)
    return (velocity_tiles, attention_grad.astype(jnp.bfloat16), final_grad, loss_value)


def solution(mesh):
    placed = (
        P(("dp", "seqt"), None, None),
        P(("dp", "seqt")),
        P("dp", None),
        P("dp", None),
        P(("dp", "seqt"), None),
        P(("dp", "seqt"), None),
        P(("dp", "seqt"), None),
        P(("dp", "seqt"), None),
        P(("dp", "seqt"), None),
        P(),
        P(),
        P(("dp", "seqt"), None),
        P("seqt", None),
        P("dp", None),
        P(),
        P(("dp", "seqt"), None, None),
    )
    return jax.shard_map(
        per_device,
        mesh=mesh,
        in_specs=placed,
        out_specs=(P(("dp", "seqt"), None, None), P(("dp", "seqt"), None), P(), P()),
        check_vma=False,
    )
```

profile of v0, /device:TPU:1, one launch (start us, length us, event | category | flops | bytes accessed | tf_op | source)
XLA Modules:
  0.0 626.5 jit_solution(881000691900963373)
XLA Ops:
  7.9 1.5 copy_bitcast_fusion.1
  9.4 10.3 %all-to-all-start.2 = ((bf16[16,16,128]{2,0,1:T(8,128)(2,1)}), bf16[16,16,128]{2,0,1:T(8,128)(2,1)S(1)}, u32[]{:S(2)}, u32[]{:S(2)}) async-start(bf16[16,16,128]{2,0,1:T(8,128)(2,1)} %copy_bitcast_fusion.1), calls=%async_computation.2 | async-start | bytes 131072 | tf_op jit(solution)/shard_map/all_to_all | solution.py:151
  19.7 1.5 copy_bitcast_fusion
  21.2 4.4 all-to-all-done.2
  25.6 3.7 all-to-all-start.4
  29.3 1.0 copy.84
  30.3 4.9 all-to-all-done.4
  35.2 4.3 all-to-all-start.1
  39.6 1.0 copy.89
  40.6 15.0 %all-to-all-done.1 = bf16[128,16,128]{0,2,1:T(8,128)(2,1)S(1)} async-done(((bf16[128,16,128]{0,2,1:T(8,128)(2,1)}), bf16[128,16,128]{0,2,1:T(8,128)(2,1)S(1)}, u32[]{:S(2)}, u32[]{:S(2)}) %all-to-all-start.1) | async-done | bytes 524320 | tf_op jit(solution)/shard_map/all_to_all | solution.py:149
  55.6 4.3 all-to-all-start.3
  60.5 76.0 %psum.21 = f32[]{:T(128)} all-reduce(f32[]{:T(128)} %convert_reduce_fusion), channel_id=1, replica_groups=mesh['dp'=32,'seqt'=16] {'dp'}, use_global_device_ids=true, to_apply=%region_11.12 | all-reduce | flops 1 | bytes 8 | tf_op jit(solution)/shard_map/psum | solution.py:146
  137.7 1.0 copy.81
  140.0 1.3 dynamic-slice
  142.0 13.5 %all-reduce = s32[32]{0:T(128)} all-reduce(s32[32]{0:T(128)S(1)} %dynamic-update-slice), channel_id=1, replica_groups=mesh['dp'=32,'seqt'=16] {'dp'}, use_global_device_ids=true, to_apply=%add | all-reduce | flops 32 | bytes 256
  156.2 1.3 fusion.60
  158.8 22.8 %all-to-all-start = ((bf16[128,16,128]{0,2,1:T(8,128)(2,1)}), bf16[128,16,128]{0,2,1:T(8,128)(2,1)S(1)}, u32[]{:S(2)}, u32[]{:S(2)}) async-start(bf16[128,16,128]{0,2,1:T(8,128)(2,1)} %bitcast.8), calls=%async_computation | async-start | bytes 1048576 | tf_op jit(solution)/shard_map/all_to_all | solution.py:148
  184.7 6.6 %all-to-all-done = bf16[128,16,128]{0,2,1:T(8,128)(2,1)S(1)} async-done(((bf16[128,16,128]{0,2,1:T(8,128)(2,1)}), bf16[128,16,128]{0,2,1:T(8,128)(2,1)S(1)}, u32[]{:S(2)}, u32[]{:S(2)}) %all-to-all-start) | async-done | bytes 524320 | tf_op jit(solution)/shard_map/all_to_all | solution.py:148
  191.5 1.6 copy.83
  193.1 1.4 mul.143
  194.7 1.6 copy.82
  196.3 1.6 reshape.222
  198.2 0.9 copy.93
  200.0 1.1 pad_maximum_fusion
  201.1 46.6 %while.10 = (s32[]{:T(128)}, bf16[4,512,2,64]{1,3,2,0:T(8,128)(2,1)}, s32[4,512]{1,0:T(4,128)}, s32[2304]{0:T(1024)S(1)}, pred[2304]{0:T(1024)(128)(4,1)S(1)}, /...) while((s32[]{:T(128)}, ...), condition=%wide.region_6.7_spmd, body=%wide.region_3.6_spmd.sunk | while | flops 929633792 | bytes 10447769 | solution.py:57
  201.8 0.8 compare_and_fusion.2
  202.6 4.6 fusion.102
  207.3 5.4 fusion.103
  213.4 0.8 compare_and_fusion.2
  214.3 4.6 fusion.102
  218.9 5.4 fusion.103
  225.1 0.8 compare_and_fusion.2
  225.9 4.6 fusion.102
  230.6 5.4 fusion.103
  236.7 0.8 compare_and_fusion.2
  237.6 4.6 fusion.102
  242.2 5.4 fusion.103
  247.6 1.4 copy.94
  249.3 0.9 copy.95
  250.3 4.7 all-to-all-start.5
  256.8 70.3 %all_gather.11 = bf16[32,64,128]{2,1,0:T(8,128)(2,1)S(1)} all-gather(bf16[1,64,128]{2,1,0:T(8,128)(2,1)S(1)} %copy-done.10), channel_id=1, replica_groups=mesh['dp'=32,'seqt'=16] {'dp'}, dimensions={0}, use_global_device_ids=true | all-gather | bytes 540672 | tf_op jit(solution)/shard_map/all_gather | solution.py:143
  327.7 5.5 fusion.77
  334.2 1.6 multiply_reduce_fusion.4
  335.8 1.1 fusion.57
  337.5 8.0 %convolution_convert_fusion = bf16[128,2048]{1,0:T(8,128)(2,1)} fusion(bf16[2048,2432]{1,0:T(8,128)(2,1)} %all-gather.2.cloned.1.call-done, f32[128,2432]{1,0:T(8,128)S(1)} %get-tuple-element.120, f32[128,2432]{1,0:T(8,128)S(1)} %get-tuple-element.118, f32[128]{0:T(128)S(1)} %broadcast_multiply_fusion, f32[128]{0:T(128)S(1)} %broadcast_multiply_fusion.1, ...), kind=kOutput, calls=%fused_computation.33 | convolution fusion | flops 1278132224 | bytes 12997760 | tf_op jit(solution)/shard_map/dot_general | solution.py:199
  345.5 111.2 %psum.23 = f32[]{:T(128)} all-reduce(f32[]{:T(128)} %get-tuple-element.111), channel_id=1, replica_groups=mesh['dp'=32,'seqt'=16] {'dp','seqt'}, use_global_device_ids=true, to_apply=%region_16.17 | all-reduce | flops 1 | bytes 8 | tf_op jit(solution)/shard_map/psum | solution.py:200
  457.3 159.3 %all-reduce.3.cloned.1.call-done = f32[2432,64]{0,1:T(8,128)} async-done(((f32[2432,64]{0,1:T(8,128)}), f32[2432,64]{0,1:T(8,128)}) %all-reduce.3.cloned.1.call-update) | async-done | bytes 622608 | tf_op jit(solution)/shard_map/psum | solution.py:200
  616.6 1.9 copy.115
  (107 shorter events, 15.4 us)
Async XLA Ops:
  7.2 326.9 %copy-start = (bf16[2432,64]{0,1:T(8,128)(2,1)S(1)}, bf16[2432,64]{0,1:T(8,128)(2,1)}, u32[]{:S(2)}) copy-start(bf16[2432,64]{0,1:T(8,128)(2,1)} %param.32) | copy-start | bytes 933892
  7.2 22.2 %copy-start.4 = (bf16[128,2048]{1,0:T(8,128)(2,1)S(1)}, bf16[128,2048]{1,0:T(8,128)(2,1)}, u32[]{:S(2)}) copy-start(bf16[128,2048]{1,0:T(8,128)(2,1)} %param.23) | copy-start | bytes 1572868
  7.2 320.5 %all-gather.2.cloned.1.call-start = ((), (), s32[]{:S(2)}) async-start(), calls=%async_computation.6 | async-start | bytes 10584064 | tf_op jit(solution)/shard_map/all_gather | solution.py:184
  9.4 30.1 %copy-start.5 = (bf16[128,2048]{1,0:T(8,128)(2,1)S(1)}, bf16[128,2048]{1,0:T(8,128)(2,1)}, u32[]{:S(2)}) copy-start(bf16[128,2048]{1,0:T(8,128)(2,1)} %param.24) | copy-start | bytes 1572868
  9.4 16.2 %all-to-all-start.2 = ((bf16[16,16,128]{2,0,1:T(8,128)(2,1)}), bf16[16,16,128]{2,0,1:T(8,128)(2,1)S(1)}, u32[]{:S(2)}, u32[]{:S(2)}) async-start(bf16[16,16,128]{2,0,1:T(8,128)(2,1)} %copy_bitcast_fusion.1), calls=%async_computation.2 | async-start | bytes 131072 | tf_op jit(solution)/shard_map/all_to_all | solution.py:151
  25.6 9.6 %all-to-all-start.4 = ((bf16[16,16,128]{2,0,1:T(8,128)(2,1)}), bf16[16,16,128]{2,0,1:T(8,128)(2,1)S(1)}, u32[]{:S(2)}, u32[]{:S(2)}) async-start(bf16[16,16,128]{2,0,1:T(8,128)(2,1)} %copy_bitcast_fusion), calls=%async_computation.4 | async-start | bytes 131072 | tf_op jit(solution)/shard_map/all_to_all | solution.py:152
  35.2 20.3 %all-to-all-start.1 = ((bf16[128,16,128]{0,2,1:T(8,128)(2,1)}), bf16[128,16,128]{0,2,1:T(8,128)(2,1)S(1)}, u32[]{:S(2)}, u32[]{:S(2)}) async-start(bf16[128,16,128]{0,2,1:T(8,128)(2,1)} %bitcast.11), calls=%async_computation.1 | async-start | bytes 1048576 | tf_op jit(solution)/shard_map/all_to_all | solution.py:149
  39.5 20.3 %copy-start.13 = (s32[1,2]{1,0:T(1,128)S(1)}, s32[1,2]{1,0:T(1,128)}, u32[]{:S(2)}) copy-start(s32[1,2]{1,0:T(1,128)} %param.20) | copy-start | bytes 28
  39.5 98.1 %copy-start.6 = (bf16[128,2048]{1,0:T(8,128)(2,1)S(1)}, bf16[128,2048]{1,0:T(8,128)(2,1)}, u32[]{:S(2)}) copy-start(bf16[128,2048]{1,0:T(8,128)(2,1)} %param.22) | copy-start | bytes 1572868
  40.6 115.0 %copy-start.14 = (s32[1,2]{1,0:T(1,128)S(1)}, s32[1,2]{1,0:T(1,128)}, u32[]{:S(2)}) copy-start(s32[1,2]{1,0:T(1,128)} %param.21) | copy-start | bytes 28
  55.6 103.2 %all-to-all-start.3 = ((bf16[128,16,128]{0,2,1:T(8,128)(2,1)}), bf16[128,16,128]{0,2,1:T(8,128)(2,1)S(1)}, u32[]{:S(2)}, u32[]{:S(2)}) async-start(bf16[128,16,128]{0,2,1:T(8,128)(2,1)} %bitcast.14), calls=%async_computation.3 | async-start | bytes 1048576 | tf_op jit(solution)/shard_map/all_to_all | solution.py:150
  158.8 23.8 %copy-start.11 = (f32[64]{0:T(128)S(1)}, f32[64]{0:T(128)}, u32[]{:S(2)}) copy-start(f32[64]{0:T(128)} %param.28) | copy-start | bytes 772
  158.8 32.6 %all-to-all-start = ((bf16[128,16,128]{0,2,1:T(8,128)(2,1)}), bf16[128,16,128]{0,2,1:T(8,128)(2,1)S(1)}, u32[]{:S(2)}, u32[]{:S(2)}) async-start(bf16[128,16,128]{0,2,1:T(8,128)(2,1)} %bitcast.8), calls=%async_computation | async-start | bytes 1048576 | tf_op jit(solution)/shard_map/all_to_all | solution.py:148
  196.3 1.6 copy-start.15
  198.2 1.1 copy-start.12
  199.1 0.8 copy-start.7
  202.6 4.7 copy-start.2
  202.6 4.7 copy-start.3
  214.2 4.7 copy-start.2
  214.3 4.7 copy-start.3
  225.9 4.7 copy-start.2
  225.9 4.7 copy-start.3
  237.5 4.7 copy-start.2
  237.5 4.7 copy-start.3
  249.3 5.7 copy-start.16
  249.3 7.3 %copy-start.8 = (f32[2,7296]{1,0:T(2,128)S(1)}, f32[2,7296]{1,0:T(2,128)}, u32[]{:S(2)}) copy-start(f32[2,7296]{1,0:T(2,128)} %param.31) | copy-start | bytes 175108
  249.3 7.5 %copy-start.10 = (bf16[1,64,128]{2,1,0:T(8,128)(2,1)S(1)}, bf16[1,64,128]{2,1,0:T(8,128)(2,1)}, u32[]{:S(2)}) copy-start(bf16[1,64,128]{2,1,0:T(8,128)(2,1)} %param.18) | copy-start | bytes 49156
  250.3 77.4 %copy-start.1 = (bf16[128,2432]{1,0:T(8,128)(2,1)S(1)}, bf16[128,2432]{1,0:T(8,128)(2,1)}, u32[]{:S(2)}) copy-start(bf16[128,2432]{1,0:T(8,128)(2,1)} %param.29) | copy-start | bytes 1867780
  250.3 77.4 %all-to-all-start.5 = ((bf16[16,128,128]{1,2,0:T(8,128)(2,1)}), bf16[16,128,128]{1,2,0:T(8,128)(2,1)S(1)}, u32[]{:S(2)}, u32[]{:S(2)}) async-start(bf16[16,128,128]{1,2,0:T(8,128)(2,1)} %copy.95), calls=%async_computation.5 | async-start | bytes 1048576 | tf_op jit(solution)/shard_map/all_to_all | solution.py:181
  254.9 361.7 %all-reduce.3.cloned.1.call-start = ((), (), s32[]{:S(2)}) async-start(), calls=%async_computation.7 | async-start | bytes 1245184 | tf_op jit(solution)/shard_map/psum | solution.py:200
  333.5 0.7 copy-start.9
Sparse Core Ops, SparseCore 0:
  10.2 83.4 all-gather.1
  337.6 278.9 all-reduce.2
where the time goes:
time: 628 us; the launch traced here: 627 us
  blocking collectives  271 us (43%)
  waiting for transfers between devices  191 us (30%)
  matrix products  57.5 us (9%)
  starting transfers between devices  50.1 us (8%)
  local copies, waits for them, and re-layouts  26.6 us (4%)
  between operations  18.9 us (3%)
  other arithmetic  11.2 us (2%)
    psum x1, waiting for transfers between devices, per_device(): final_grad, loss_sum = lax.psum((final_part, loss_part), ('dp', 'seqt'))  159 us
    psum x1, blocking collectives, per_device(): final_grad, loss_sum = lax.psum((final_part, loss_part), ('dp', 'seqt'))  111 us
    psum x1, blocking collectives, per_device(): total_count = lax.psum(jnp.sum(image_tokens.astype(jnp.float32)), 'dp')  76 us
    all_gather x1, blocking collectives, per_device(): lax.all_gather(latent_tiles, 'dp', axis=0, tiled=True).astype(jnp.float32)  70.3 us
    all_to_all x1, starting transfers between devices, per_device(): lax.all_to_all(queries, 'seqt', split_axis=1, concat_axis=0, tiled=True)  22.8 us
    dot_general x4, matrix products, one_block(): jnp.einsum('hqk,khd->qhd', weights, value_heads, preferred_element_type=j...  21.7 us
    sub x4, matrix products, one_block(): exponent = jnp.exp(scores - largest)  18.5 us
    all_to_all x1, waiting for transfers between devices, per_device(): lax.all_to_all(key_rows, 'seqt', split_axis=1, concat_axis=0, tiled=True)  15 us
  transfers between devices with their start and end apart: 8, of which 5 were waited for; matrix products, arithmetic and copies ran while one was open for 13% of the time, Pallas kernels for 0%

commit v1 on v0

v1 whole, which is shorter than its diff:
```python
import functools

import jax
import jax.numpy as jnp
from jax import lax
from jax.experimental import pallas as pl
from jax.experimental.pallas import tpu as pltpu
from jax.sharding import PartitionSpec as P

HD = 64
IMGS = 2
LANES = 128
Q_ROWS = 256
EPSILON = 1e-06
VMEM = pl.BlockSpec(memory_space=pltpu.VMEM)
SMEM = pl.BlockSpec(memory_space=pltpu.SMEM)
NT = (((1,), (1,)), ((), ()))


def params(limit_mib, semantics=None):
    return pltpu.CompilerParams(
        vmem_limit_bytes=limit_mib * 2**20, dimension_semantics=semantics
    )


def pack_kernel(parts, *refs):
    ins, out_ref = refs[:-1], refs[-1]
    block_rows = sum(ref.shape[0] for ref in ins)
    for part in range(parts):
        row = part * block_rows
        for ref in ins:
            rows = ref.shape[0]
            out_ref[row : row + rows, :] = ref[:, part * LANES : (part + 1) * LANES]
            row += rows


def pack(arrays, parts):
    block_rows = sum(array.shape[0] for array in arrays)
    return pl.pallas_call(
        functools.partial(pack_kernel, parts),
        out_shape=jax.ShapeDtypeStruct((parts * block_rows, LANES), arrays[0].dtype),
        in_specs=[VMEM] * len(arrays),
        out_specs=VMEM,
        compiler_params=params(32),
    )(*arrays)


def head_norm(rows, gain, same_head):
    wide = rows.astype(jnp.float32)
    square = wide * wide
    high = square.astype(jnp.bfloat16)
    low = (square - high.astype(jnp.float32)).astype(jnp.bfloat16)
    total = jnp.dot(high, same_head, preferred_element_type=jnp.float32) + jnp.dot(
        low, same_head, preferred_element_type=jnp.float32
    )
    return (wide * lax.rsqrt(total * (1.0 / HD) + EPSILON) * gain).astype(jnp.bfloat16)


def attention_kernel(
    sources, tile, text_rows, counts_ref, lengths_ref, recv_ref, query_gain_ref, key_gain_ref,
    out_ref, query_ref, key_ref, value_ref, window_ref, weigh_ref,
):
    rows_all = sources * tile
    text_slots = sources * text_rows // IMGS
    window = rows_all // IMGS
    block = 3 * tile + 2 * text_rows
    per_image = sources // IMGS
    first_count = counts_ref[0, 0]
    second_count = counts_ref[0, 1]
    border = pl.multiple_of((first_count + tile - 1) // tile * tile, tile)
    head_row = lax.broadcasted_iota(jnp.int32, (LANES, LANES), 0) // HD
    head_column = lax.broadcasted_iota(jnp.int32, (LANES, LANES), 1) // HD
    same_head = (head_row == head_column).astype(jnp.float32).astype(jnp.bfloat16)
    query_gain = query_gain_ref[...]
    key_gain = key_gain_ref[...]
    for source in range(sources):
        at, row = source * block, source * tile
        key = head_norm(recv_ref[at + tile : at + 2 * tile, :], key_gain, same_head)
        key_ref[row : row + tile, :] = key
        if row < window:
            window_ref[0, row : row + tile, :] = key
        value_ref[row : row + tile, :] = recv_ref[at + 2 * tile : at + 3 * tile, :]
        query = head_norm(recv_ref[at : at + tile, :], query_gain, same_head)
        query_ref[row : row + tile, :] = query * jnp.bfloat16(HD**-0.5)
        image, place = source // per_image, window + source % per_image * text_rows
        text = recv_ref[at + 3 * tile : at + 3 * tile + text_rows, :]
        window_ref[image, place : place + text_rows, :] = head_norm(text, key_gain, same_head)
    window_ref[1, :window, :] = key_ref[pl.ds(border, window), :]

    def weighed(values, used, image, start, rows):
        low = lax.broadcasted_iota(jnp.int32, (rows, LANES), 1) < HD
        kept = lax.broadcasted_iota(jnp.int32, (rows, LANES), 0) < used
        wide = jnp.where(kept, values.astype(jnp.float32), 0.0)
        ones = kept.astype(jnp.float32)
        weigh_ref[image, 0, start : start + rows, :] = jnp.where(low, wide, ones).astype(jnp.bfloat16)
        weigh_ref[image, 1, start : start + rows, :] = jnp.where(low, ones, wide).astype(jnp.bfloat16)

    for image in range(IMGS):
        used = counts_ref[0, image]
        for start in range(0, window, tile):
            begin = start if image == 0 else pl.multiple_of(border + start, tile)
            weighed(value_ref[pl.ds(begin, tile), :], used - start, image, start, tile)
        text = jnp.concatenate(
            [
                recv_ref[s * block + 3 * tile + text_rows : (s + 1) * block, :]
                for s in range(image * per_image, (image + 1) * per_image)
            ],
            axis=0,
        )
        weighed(text, lengths_ref[0, image], image, window, text_slots)

    low = lax.broadcasted_iota(jnp.int32, (Q_ROWS, LANES), 1) < HD

    def rows_of(image, start):
        query = query_ref[pl.ds(start, Q_ROWS), :].astype(jnp.float32)
        sums = []
        for head in range(2):
            own = jnp.where(low == (head == 0), query, 0.0).astype(jnp.bfloat16)
            scores = lax.dot_general(own, window_ref[image], NT, preferred_element_type=jnp.float32)
            weights = jnp.exp(scores).astype(jnp.bfloat16)
            sums.append(jnp.dot(weights, weigh_ref[image, head], preferred_element_type=jnp.float32))
        above = jnp.where(low, sums[0], sums[1])
        below = pltpu.roll(jnp.where(low, sums[1], sums[0]), HD, 1)
        out_ref[pl.ds(start, Q_ROWS), :] = (above / below).astype(jnp.bfloat16)

    @pl.loop(0, (border + Q_ROWS - 1) // Q_ROWS)
    def _(step):
        rows_of(0, pl.multiple_of(step * Q_ROWS, tile))

    @pl.loop(0, (rows_all - border + Q_ROWS - 1) // Q_ROWS)
    def _(step):
        rows_of(1, pl.multiple_of(jnp.minimum(border + step * Q_ROWS, rows_all - Q_ROWS), tile))


def attention(recv, counts, lengths, query_gain, key_gain, sources, tile, text_rows):
    rows_all = sources * tile
    keys = rows_all // IMGS + sources * text_rows // IMGS
    twice = lambda gain: jnp.concatenate([gain, gain]).reshape(1, LANES)
    return pl.pallas_call(
        functools.partial(attention_kernel, sources, tile, text_rows),
        out_shape=jax.ShapeDtypeStruct((rows_all, LANES), jnp.bfloat16),
        in_specs=[SMEM, SMEM, VMEM, VMEM, VMEM],
        out_specs=VMEM,
        scratch_shapes=[
            pltpu.VMEM((rows_all, LANES), jnp.bfloat16),
            pltpu.VMEM((rows_all, LANES), jnp.bfloat16),
            pltpu.VMEM((rows_all, LANES), jnp.bfloat16),
            pltpu.VMEM((IMGS, keys, LANES), jnp.bfloat16),
            pltpu.VMEM((IMGS, 2, keys, LANES), jnp.bfloat16),
        ],
        compiler_params=params(48),
    )(counts, lengths, recv, twice(query_gain), twice(key_gain))


def head_kernel(
    steps, layout_ref, total_ref, rows_ref, weight_ref, residual_ref, modulate_ref, final_ref,
    noise_ref, landed_ref, velocity_ref, grad_ref, parts_ref, sum_ref,
):
    step = pl.program_id(0)
    tile, width = residual_ref.shape
    lat = final_ref.shape[0]
    rows = jnp.concatenate([rows_ref[:tile, :], rows_ref[tile:, :]], axis=1)
    product = jnp.dot(rows, weight_ref[...], preferred_element_type=jnp.float32)

    @pl.when(step == 0)
    def _():
        sum_ref[...] = product

    @pl.when(step > 0)
    def _():
        sum_ref[...] += product

    @pl.when(step == steps - 1)
    def _():
        first = layout_ref[0] == 0
        pick = lambda at: jnp.where(
            first,
            modulate_ref[0:1, at * width : (at + 1) * width],
            modulate_ref[1:2, at * width : (at + 1) * width],
        )
        gate, shift, scale = pick(0), pick(1), 1.0 + pick(2)
        mean = lambda array: jnp.sum(array, axis=-1, keepdims=True) * (1.0 / width)
        hidden = residual_ref[...].astype(jnp.float32) + gate * sum_ref[...]
        centered = hidden - mean(hidden)
        inverse = lax.rsqrt(mean(centered * centered) + EPSILON)
        normed = centered * inverse
        mixed = (normed * scale + shift).astype(jnp.bfloat16)
        velocity = lax.dot_general(final_ref[...], mixed, NT, preferred_element_type=jnp.float32)
        velocity_ref[...] = velocity
        target = noise_ref[...].astype(jnp.float32) - landed_ref[...].astype(jnp.float32)
        used = lax.broadcasted_iota(jnp.int32, (lat, tile), 1) < layout_ref[1]
        error = jnp.where(used, velocity - target, 0.0)
        grad_wide = error * (2.0 / (total_ref[0] * lat))
        grad_columns = grad_wide.astype(jnp.bfloat16)
        final_part = jnp.dot(grad_columns, mixed, preferred_element_type=jnp.float32)
        for at in range(width // LANES):
            parts_ref[at] = final_part[:, at * LANES : (at + 1) * LANES]
        parts_ref[width // LANES] = jnp.full((lat, LANES), jnp.sum(error * error))
        grad_rows = grad_wide.T.astype(jnp.bfloat16)
        grad_normed = jnp.dot(grad_rows, final_ref[...], preferred_element_type=jnp.float32) * scale
        grad_hidden = inverse * (
            grad_normed - mean(grad_normed) - normed * mean(grad_normed * normed)
        )
        grad_ref[...] = (grad_hidden * gate).astype(jnp.bfloat16)


def head(layout, total, recv, weight, residual, modulate, final_columns, noise, landed):
    tile, width = residual.shape
    lat = final_columns.shape[0]
    depth = 2 * LANES
    steps = weight.shape[0] // depth
    blocks = width // LANES + 1
    whole = lambda array: pl.BlockSpec(array.shape, lambda i: (0,) * array.ndim)
    return pl.pallas_call(
        functools.partial(head_kernel, steps),
        grid=(steps,),
        out_shape=(
            jax.ShapeDtypeStruct((lat, tile), jnp.float32),
            jax.ShapeDtypeStruct((tile, width), jnp.bfloat16),
            jax.ShapeDtypeStruct((blocks, lat, LANES), jnp.float32),
        ),
        in_specs=[
            SMEM,
            SMEM,
            pl.BlockSpec((2 * tile, LANES), lambda i: (i, 0)),
            pl.BlockSpec((depth, width), lambda i: (i, 0)),
            whole(residual),
            whole(modulate),
            whole(final_columns),
            whole(noise),
            whole(landed),
        ],
        out_specs=(
            pl.BlockSpec((lat, tile), lambda i: (0, 0)),
            pl.BlockSpec((tile, width), lambda i: (0, 0)),
            pl.BlockSpec((blocks, lat, LANES), lambda i: (0, 0, 0)),
        ),
        scratch_shapes=[pltpu.VMEM((tile, width), jnp.float32)],
        compiler_params=params(48, ("arbitrary",)),
    )(layout, total, recv, weight, residual, modulate, final_columns, noise, landed)


def back_kernel(grad_ref, weight_ref, out_ref):
    out_ref[...] = lax.dot_general(
        grad_ref[...], weight_ref[...], NT, preferred_element_type=jnp.float32
    ).astype(jnp.bfloat16)


def back(grad, weight):
    tile, width = grad.shape
    depth = 2 * LANES
    return pl.pallas_call(
        back_kernel,
        grid=(weight.shape[0] // depth,),
        out_shape=jax.ShapeDtypeStruct((tile, weight.shape[0]), jnp.bfloat16),
        in_specs=[
            pl.BlockSpec((tile, width), lambda i: (0, 0)),
            pl.BlockSpec((depth, width), lambda i: (i, 0)),
        ],
        out_specs=pl.BlockSpec((tile, depth), lambda i: (0, i)),
        compiler_params=params(32, ("arbitrary",)),
        cost_estimate=pl.CostEstimate(
            flops=2 * tile * width * weight.shape[0],
            bytes_accessed=2 * width * weight.shape[0],
            transcendentals=0,
        ),
    )(grad, weight)


def unpack_kernel(parts_ref, out_ref):
    for at in range(out_ref.shape[1] // LANES):
        out_ref[:, at * LANES : (at + 1) * LANES] = parts_ref[at]


def unpack(parts, width):
    return pl.pallas_call(
        unpack_kernel,
        out_shape=jax.ShapeDtypeStruct((parts.shape[1], width), jnp.float32),
        in_specs=[VMEM],
        out_specs=VMEM,
        compiler_params=params(32),
    )(parts)


def exchange(array, axis, groups=None):
    return lax.all_to_all(
        array, axis, split_axis=0, concat_axis=0, axis_index_groups=groups, tiled=True
    )


def digits(value, base, rows, lanes):
    places = lax.broadcasted_iota(jnp.int32, (rows, lanes), 0)
    return jnp.where(places == 1, value // base, jnp.where(places == 2, value % base, 0))


def route_near(tile, destination, count, near, groups):
    lat, lanes = tile.shape
    slots = jnp.arange(near, dtype=jnp.int32)[:, None, None]
    hit = destination % near == slots
    notes = digits(count, 16, 16, lanes)[None]
    first = lax.broadcasted_iota(jnp.int32, notes.shape, 1) == 0
    notes = jnp.where(first, jnp.where(hit, destination // near + 1, 0), notes)
    data = jnp.where(hit, tile[None], jnp.zeros_like(tile)[None])
    sent = jnp.concatenate([data, notes.astype(jnp.bfloat16)], axis=1)
    return exchange(sent, "dp", groups)


def route_far(recv, near, far, lat, groups):
    notes = recv[:, lat : lat + 3, 0].astype(jnp.float32).astype(jnp.int32)
    count = jnp.sum(notes[:, 1] * 16 + notes[:, 2])
    slots = jnp.arange(far, dtype=jnp.int32)[:, None]
    hit = (notes[:, 0][None, :] == slots + 1)[:, :, None, None]
    data = jnp.where(hit, recv[None, :, :lat].astype(jnp.float32), 0.0)
    data = jnp.sum(data, axis=1).astype(jnp.bfloat16)
    more = digits(count, 128, 16, recv.shape[2])[None].astype(jnp.bfloat16)
    sent = jnp.concatenate([data, jnp.broadcast_to(more, (far, *more.shape[1:]))], axis=1)
    recv = exchange(sent, "dp", groups)
    landed = jnp.sum(recv[:, :lat].astype(jnp.float32), axis=0).astype(jnp.bfloat16)
    notes = recv[:, lat : lat + 3, 0].astype(jnp.float32)
    return landed, jnp.sum(notes[:, 1] * 128.0 + notes[:, 2])


def sum_over(array, axis, count, groups=None):
    spread = jnp.broadcast_to(array[None], (count, *array.shape))
    return jnp.sum(exchange(spread, axis, groups), axis=0)


def per_device(
    near, latent_tiles, tile_route, image_tokens, text_lengths, queries, key_rows, values,
    text_keys, text_values, query_gain, key_gain, residual, out_weight, modulation, final_weight,
    noise_tiles,
):
    lat_width, tile = latent_tiles.shape[1:]
    rows_here, width = residual.shape
    text_rows = text_keys.shape[0]
    ranks, sources = lax.axis_size("dp"), lax.axis_size("seqt")
    far = ranks // near
    near_groups = [[row * near + at for at in range(near)] for row in range(far)]
    far_groups = [[row * near + at for row in range(far)] for at in range(near)]
    column_index = lax.axis_index("seqt")

    gathered = lax.all_gather(out_weight, "seqt", axis=0, tiled=True)
    sent = pack((queries, key_rows, values, text_keys, text_values), sources)
    recv = exchange(sent, "seqt")
    latent, route, counts, recv = lax.optimization_barrier(
        (latent_tiles, tile_route, image_tokens, recv)
    )
    near_recv = route_near(latent[0], route[0], jnp.sum(counts[0]), near, near_groups)
    heads = attention(
        recv, image_tokens, text_lengths, query_gain, key_gain, sources, tile, text_rows
    )
    heads, near_recv = lax.optimization_barrier((heads, near_recv))
    attended = exchange(heads, "seqt")
    attended, near_recv = lax.optimization_barrier((attended, near_recv))
    landed, total_count = route_far(near_recv, near, far, lat_width, far_groups)

    first_count, second_count = image_tokens[0, 0], image_tokens[0, 1]
    border = (first_count + tile - 1) // tile * tile
    place = column_index * rows_here
    owner = (place >= border).astype(jnp.int32)
    used = jnp.where(owner == 0, first_count, border + second_count) - place
    velocity, grad_projected, parts = head(
        jnp.stack([owner, used]).astype(jnp.int32), total_count.reshape(1), attended, gathered,
        residual, modulation, final_weight.T, noise_tiles[0], landed,
    )
    attention_grad = back(grad_projected, gathered)

    blocks = parts.shape[0]
    mine = exchange(parts.reshape(blocks * lat_width, LANES), "seqt")
    mine = jnp.sum(mine.reshape(sources, blocks * lat_width // sources, LANES), axis=0)
    mine = sum_over(mine, "dp", near, near_groups)
    mine = sum_over(mine, "dp", far, far_groups)
    spread = jnp.broadcast_to(mine[None], (sources, *mine.shape))
    sums = exchange(spread, "seqt").reshape(blocks, lat_width, LANES)
    final_grad = unpack(sums, width).T
    loss_value = sums[blocks - 1, 0, 0] / (total_count * lat_width)
    return velocity[None], attention_grad, final_grad, loss_value


def solution(mesh):
    both = P(("dp", "seqt"), None)
    tiles = P(("dp", "seqt"), None, None)
    placed = (
        tiles, P(("dp", "seqt")), P("dp", None), P("dp", None), both, both, both, both, both,
        P(), P(), both, P("seqt", None), P("dp", None), P(), tiles,
    )
    near = 8 if mesh.shape["dp"] % 8 == 0 else mesh.shape["dp"]
    return jax.shard_map(
        functools.partial(per_device, near),
        mesh=mesh,
        in_specs=placed,
        out_specs=(tiles, both, P(), P()),
        check_vma=False,
    )
```

time: 628 us -> 207 us (0.33)
  blocking collectives: 271 us -> 46 us
  waiting for transfers between devices: 191 us -> 53.4 us
  matrix products: 57.5 us -> 0 us
  Pallas kernels: 0 us -> 28.8 us
  starting transfers between devices: 50.1 us -> 35.4 us
  local copies, waits for them, and re-layouts: 26.6 us -> 12.6 us
  other arithmetic: 11.2 us -> 4.86 us
    psum x2 -> x0, blocking collectives: 187 us -> none  [the longest x1 111 us: per_device(): final_grad, loss_sum = lax.psum((final_part, loss_part), ('dp', 'seqt'))]
    psum x1 -> x0, waiting for transfers between devices: 159 us -> none  [per_device(): final_grad, loss_sum = lax.psum((final_part, loss_part), ('dp', 'seqt'))]
    all_gather x1 -> x0, blocking collectives: 70.3 us -> none  [per_device(): lax.all_gather(latent_tiles, 'dp', axis=0, tiled=True).astype(jnp.float32)]
    all_to_all x0 -> x3, blocking collectives: none -> 46 us  [exchange(): lax.all_to_all(array, axis, split_axis=0, concat_axis=0, axis_index_group...]
    dot_general x10 -> x0, matrix products: 38.9 us -> none  [the longest x4 21.7 us: one_block(): jnp.einsum('hqk,khd->qhd', weights, value_heads, preferred_element_type=j...]
    pallas_call x0 -> x5, Pallas kernels: none -> 28.8 us  [the longest x1 10.8 us: head(): pl.pallas_call(functools.partial(head_kernel, steps), grid=(steps,), out_...]
    all_to_all x6 -> x5, waiting for transfers between devices: 30.9 us -> 52.7 us  [exchange(): lax.all_to_all(array, axis, split_axis=0, concat_axis=0, axis_index_group...]
    sub x4 -> x0, matrix products: 18.5 us -> none  [one_block(): exponent = jnp.exp(scores - largest)]
  transfers between devices with their start and end apart: 8 -> 6, of which waited for: 5 -> 4; matrix products, arithmetic and copies ran while one was open for 13% -> 4% of each run, Pallas kernels for 0% -> 8%
where the time goes in v1:
time: 207 us; the launch traced here: 206 us
  waiting for transfers between devices  53.4 us (26%)
  blocking collectives  46 us (22%)
  starting transfers between devices  35.4 us (17%)
  Pallas kernels  28.8 us (14%)
  between operations  24.6 us (12%)
  local copies, waits for them, and re-layouts  12.6 us (6%)
  other arithmetic  4.86 us (2%)
    all_to_all x5, waiting for transfers between devices, exchange(): lax.all_to_all(array, axis, split_axis=0, concat_axis=0, axis_index_group...  52.7 us
    all_to_all x3, blocking collectives, exchange(): lax.all_to_all(array, axis, split_axis=0, concat_axis=0, axis_index_group...  46 us
    all_to_all x5, starting transfers between devices, exchange(): lax.all_to_all(array, axis, split_axis=0, concat_axis=0, axis_index_group...  35.4 us
    pallas_call x1, Pallas kernels, head(): pl.pallas_call(functools.partial(head_kernel, steps), grid=(steps,), out_...  10.8 us
    pallas_call x1, Pallas kernels, attention(): pl.pallas_call(functools.partial(attention_kernel, sources, tile, text_ro...  10.4 us
    unnamed x31, local copies, waits for them, and re-layouts  8.66 us
    pallas_call x1, Pallas kernels, back(): pl.pallas_call(back_kernel, grid=(weight.shape[0] // depth,), out_shape=j...  5.24 us
  transfers between devices with their start and end apart: 6, of which 4 were waited for; matrix products, arithmetic and copies ran while one was open for 4% of the time, Pallas kernels for 8%

profile of v1, /device:TPU:1, one launch (start us, length us, event | category | flops | bytes accessed | tf_op | source)
XLA Modules:
  0.0 205.7 jit_solution(18325910375990311169)
XLA Ops:
  7.2 0.0 all-gather.2.cloned.1.call-start
  7.2 0.7 all-gather.2.cloned.1.call-update
  7.9 1.0 copy-done.2
  8.9 1.0 copy-done.3
  10.0 1.0 copy-done.4
  11.0 0.8 copy-done.6
  11.9 0.8 copy-done.7
  12.7 1.5 shard_map.183
  14.2 10.5 %all-to-all-start = ((bf16[16,416,128]{2,1,0:T(8,128)(2,1)}), bf16[16,416,128]{2,1,0:T(8,128)(2,1)S(1)}, u32[]{:S(2)}, u32[]{:S(2)}) async-start(bf16[16,416,128]{2,1,0:T(8,128)(2,1)} %bitcast.4), calls=%async_computation | async-start | bytes 3407872 | tf_op jit(solution)/shard_map/all_to_all | solution.py:286
  25.5 35.2 %all-to-all-done = bf16[16,416,128]{2,1,0:T(8,128)(2,1)S(1)} async-done(((bf16[16,416,128]{2,1,0:T(8,128)(2,1)}), bf16[16,416,128]{2,1,0:T(8,128)(2,1)S(1)}, u32[]{:S(2)}, u32[]{:S(2)}) %all-to-all-start) | async-done | bytes 1703968 | tf_op jit(solution)/shard_map/all_to_all | solution.py:286
  60.6 0.6 reduce_sum.75
  63.9 0.1 broadcast_select_fusion.1
  64.0 0.1 select_convert_fusion
  64.1 0.1 broadcast_select_fusion
  64.2 0.7 pad_maximum_fusion
  64.8 7.9 %all-to-all-start.1 = ((bf16[8,80,128]{2,1,0:T(8,128)(2,1)}), bf16[8,80,128]{2,1,0:T(8,128)(2,1)S(1)}, u32[]{:S(2)}, u32[]{:S(2)}) async-start(bf16[8,80,128]{2,1,0:T(8,128)(2,1)} %pad_maximum_fusion), calls=%async_computation.1 | async-start | bytes 327680 | tf_op jit(solution)/shard_map/all_to_all | solution.py:286
  72.7 0.1 maximum_bitcast_fusion
  72.8 10.4 %shard_map.184 = bf16[2048,128]{1,0:T(8,128)(2,1)} custom-call(s32[1,2]{1,0:T(1,128)S(1)} %copy-done.10, s32[1,2]{1,0:T(1,128)S(1)} %copy-done.11, bf16[6656,128]{1,0:T(8,128)(2,1)S(1)} %bitcast.31, f32[1,128]{1,0:T(1,128)S(1)} %get-tuple-element.30.query_gain_ref, f32[1,128]{1,0:T(1,128)S(1)} %get-tuple-element.31.key_gain_ref), custom_call_target="tpu_custom_call" | custom-call | tf_op jit(solution)/shard_map/pallas_call | solution.py:139
  83.3 0.0 all-to-all-done.1
  83.3 5.6 %all-to-all-start.2 = ((bf16[16,128,128]{2,1,0:T(8,128)(2,1)}), bf16[16,128,128]{2,1,0:T(8,128)(2,1)S(1)}, u32[]{:S(2)}, u32[]{:S(2)}) async-start(bf16[16,128,128]{2,1,0:T(8,128)(2,1)} %bitcast.10), calls=%async_computation.2 | async-start | bytes 1048576 | tf_op jit(solution)/shard_map/all_to_all | solution.py:286
  88.9 11.4 %all-to-all-done.2 = bf16[16,128,128]{2,1,0:T(8,128)(2,1)S(1)} async-done(((bf16[16,128,128]{2,1,0:T(8,128)(2,1)}), bf16[16,128,128]{2,1,0:T(8,128)(2,1)S(1)}, u32[]{:S(2)}, u32[]{:S(2)}) %all-to-all-start.2) | async-done | bytes 524320 | tf_op jit(solution)/shard_map/all_to_all | solution.py:286
  100.3 2.0 copy.31
  102.2 0.7 fusion
  102.9 0.6 slice_bitcast_fusion
  106.2 0.1 broadcast_compare_fusion
  106.3 0.1 select_reduce_fusion
  106.4 0.1 select_convert_fusion.1
  106.5 0.6 pad_maximum_fusion.1
  107.2 4.7 %all-to-all-start.3 = ((bf16[4,80,128]{2,1,0:T(8,128)(2,1)}), bf16[4,80,128]{2,1,0:T(8,128)(2,1)S(1)}, u32[]{:S(2)}, u32[]{:S(2)}) async-start(bf16[4,80,128]{2,1,0:T(8,128)(2,1)} %pad_maximum_fusion.1), calls=%async_computation.3 | async-start | bytes 163840 | tf_op jit(solution)/shard_map/all_to_all | solution.py:286
  111.9 0.6 fusion.1
  114.5 0.1 pad_add_fusion.layout_ref
  114.6 4.5 %all-to-all-done.3 = bf16[4,80,128]{2,1,0:T(8,128)(2,1)S(1)} async-done(((bf16[4,80,128]{2,1,0:T(8,128)(2,1)}), bf16[4,80,128]{2,1,0:T(8,128)(2,1)S(1)}, u32[]{:S(2)}, u32[]{:S(2)}) %all-to-all-start.3) | async-done | bytes 81952 | tf_op jit(solution)/shard_map/all_to_all | solution.py:286
  119.0 0.1 convert_reduce_fusion
  119.1 0.7 add_reduce_fusion
  119.8 0.0 all-gather.2.cloned.1.call-done.weight_ref
  119.8 0.0 copy-done.1
  119.9 0.0 copy-done.5
  119.9 10.8 %shard_map.185 = (f32[64,128]{1,0:T(8,128)}, bf16[128,2432]{1,0:T(8,128)(2,1)S(1)}, f32[20,64,128]{2,1,0:T(8,128)S(1)}) custom-call(s32[2]{0:T(128)S(1)} %pad_add_fusion.layout_ref, f32[1]{0:T(128)} %bitcast.13.total_ref, bf16[2048,128]{1,0:T(8,128)(2,1)S(1)} %bitcast.34, bf16[2048,2432]{1,0:T(8,128)(2,1)} %all-gather.2.cloned.1.call-done.weight_ref, ...), custom_call_target="tpu_custom_call" | custom-call | tf_op jit(solution)/shard_map/pallas_call | solution.py:214
  130.7 16.9 %all_to_all.58 = f32[16,80,128]{2,1,0:T(8,128)S(1)} all-to-all(f32[16,80,128]{2,1,0:T(8,128)S(1)} %bitcast.35), channel_id=1, replica_groups=mesh['dp'=32,'seqt'=16] {'seqt'}, dimensions={0} | all-to-all | bytes 1310720 | tf_op jit(solution)/shard_map/all_to_all | solution.py:286
  147.7 18.4 %all_to_all.59 = f32[8,80,128]{2,1,0:T(8,128)S(1)} all-to-all(f32[8,80,128]{2,1,0:T(8,128)S(1)} %broadcast_in_dim.145), channel_id=1, replica_groups={{0,16,32,48,64,80,96,112},{128,144,160,176,192,208,224,240},{256,272,28..., dimensions={0} | all-to-all | bytes 655360 | tf_op jit(solution)/shard_map/all_to_all | solution.py:286
  166.2 10.6 %all_to_all.60 = f32[4,80,128]{2,1,0:T(8,128)S(1)} all-to-all(f32[4,80,128]{2,1,0:T(8,128)S(1)} %broadcast_in_dim.146), channel_id=1, replica_groups={{0,128,256,384},{16,144,272,400},{32,160,288,416},{48,176,304,432},{64,..., dimensions={0} | all-to-all | bytes 327680 | tf_op jit(solution)/shard_map/all_to_all | solution.py:286
  176.8 0.9 broadcast_in_dim.147
  177.7 6.7 %all-to-all-start.7 = ((f32[16,80,128]{2,1,0:T(8,128)}), f32[16,80,128]{2,1,0:T(8,128)S(1)}, u32[]{:S(2)}, u32[]{:S(2)}) async-start(f32[16,80,128]{2,1,0:T(8,128)} %broadcast_in_dim.147), calls=%async_computation.7 | async-start | bytes 1310720 | tf_op jit(solution)/shard_map/all_to_all | solution.py:286
  185.0 3.8 %copy-done = bf16[2048,2432]{1,0:T(8,128)(2,1)S(1)} copy-done((bf16[2048,2432]{1,0:T(8,128)(2,1)S(1)}, bf16[2048,2432]{1,0:T(8,128)(2,1)}, u32[]{:S(2)}) %copy-start) | copy-done | bytes 9961496
  188.9 5.2 %shard_map.186 = bf16[128,2048]{1,0:T(8,128)(2,1)} custom-call(bf16[128,2432]{1,0:T(8,128)(2,1)S(1)} %get-tuple-element.24.grad_ref, bf16[2048,2432]{1,0:T(8,128)(2,1)S(1)} %copy-done), custom_call_target="tpu_custom_call" | custom-call | flops 1275068416 | bytes 9961472 | tf_op jit(solution)/shard_map/pallas_call | solution.py:252
  194.1 1.6 all-to-all-done.7
  195.7 0.9 shard_map.187
  196.6 0.5 slice.51
  (38 shorter events, 0.2 us)
Async XLA Ops:
  7.2 112.7 %all-gather.2.cloned.1.call-start = ((), (), s32[]{:S(2)}) async-start(), calls=%async_computation.8 | async-start | bytes 10584064 | tf_op jit(solution)/shard_map/all_gather | solution.py:342
  7.9 1.0 copy-start.2
  8.9 1.0 copy-start.3
  10.0 1.0 copy-start.4
  11.0 0.8 copy-start.6
  11.9 0.8 copy-start.7
  12.7 47.9 %copy-start.10 = (s32[1,2]{1,0:T(1,128)S(1)}, s32[1,2]{1,0:T(1,128)}, u32[]{:S(2)}) copy-start(s32[1,2]{1,0:T(1,128)} %counts_ref.1) | copy-start | bytes 28
  14.2 49.9 %copy-start.12 = (bf16[1,64,128]{2,1,0:T(8,128)(2,1)S(1)}, bf16[1,64,128]{2,1,0:T(8,128)(2,1)}, u32[]{:S(2)}) copy-start(bf16[1,64,128]{2,1,0:T(8,128)(2,1)} %param.16) | copy-start | bytes 49156
  14.2 58.5 %copy-start.13 = (f32[64]{0:T(128)S(1)}, f32[64]{0:T(128)}, u32[]{:S(2)}) copy-start(f32[64]{0:T(128)} %param.25) | copy-start | bytes 772
  14.2 58.5 %copy-start.14 = (f32[64]{0:T(128)S(1)}, f32[64]{0:T(128)}, u32[]{:S(2)}) copy-start(f32[64]{0:T(128)} %param.26) | copy-start | bytes 772
  14.2 58.6 %copy-start.11 = (s32[1,2]{1,0:T(1,128)S(1)}, s32[1,2]{1,0:T(1,128)}, u32[]{:S(2)}) copy-start(s32[1,2]{1,0:T(1,128)} %lengths_ref.1) | copy-start | bytes 28
  14.2 46.4 %all-to-all-start = ((bf16[16,416,128]{2,1,0:T(8,128)(2,1)}), bf16[16,416,128]{2,1,0:T(8,128)(2,1)S(1)}, u32[]{:S(2)}, u32[]{:S(2)}) async-start(bf16[16,416,128]{2,1,0:T(8,128)(2,1)} %bitcast.4), calls=%async_computation | async-start | bytes 3407872 | tf_op jit(solution)/shard_map/all_to_all | solution.py:286
  64.8 18.4 %all-to-all-start.1 = ((bf16[8,80,128]{2,1,0:T(8,128)(2,1)}), bf16[8,80,128]{2,1,0:T(8,128)(2,1)S(1)}, u32[]{:S(2)}, u32[]{:S(2)}) async-start(bf16[8,80,128]{2,1,0:T(8,128)(2,1)} %pad_maximum_fusion), calls=%async_computation.1 | async-start | bytes 327680 | tf_op jit(solution)/shard_map/all_to_all | solution.py:286
  83.2 36.6 %copy-start.1 = (bf16[128,2432]{1,0:T(8,128)(2,1)S(1)}, bf16[128,2432]{1,0:T(8,128)(2,1)}, u32[]{:S(2)}) copy-start(bf16[128,2432]{1,0:T(8,128)(2,1)} %residual_ref.1) | copy-start | bytes 1867780
  83.2 36.6 %copy-start.5 = (bf16[2432,64]{0,1:T(8,128)(2,1)S(1)}, bf16[2432,64]{0,1:T(8,128)(2,1)}, u32[]{:S(2)}) copy-start(bf16[2432,64]{0,1:T(8,128)(2,1)} %param.30) | copy-start | bytes 933892
  83.2 36.6 %copy-start.8 = (f32[2,7296]{1,0:T(2,128)S(1)}, f32[2,7296]{1,0:T(2,128)}, u32[]{:S(2)}) copy-start(f32[2,7296]{1,0:T(2,128)} %modulate_ref.1) | copy-start | bytes 175108
  83.2 36.6 %copy-start.9 = (bf16[1,64,128]{2,1,0:T(8,128)(2,1)S(1)}, bf16[1,64,128]{2,1,0:T(8,128)(2,1)}, u32[]{:S(2)}) copy-start(bf16[1,64,128]{2,1,0:T(8,128)(2,1)} %param.31) | copy-start | bytes 49156
  83.3 17.0 %all-to-all-start.2 = ((bf16[16,128,128]{2,1,0:T(8,128)(2,1)}), bf16[16,128,128]{2,1,0:T(8,128)(2,1)S(1)}, u32[]{:S(2)}, u32[]{:S(2)}) async-start(bf16[16,128,128]{2,1,0:T(8,128)(2,1)} %bitcast.10), calls=%async_computation.2 | async-start | bytes 1048576 | tf_op jit(solution)/shard_map/all_to_all | solution.py:286
  107.2 11.9 %all-to-all-start.3 = ((bf16[4,80,128]{2,1,0:T(8,128)(2,1)}), bf16[4,80,128]{2,1,0:T(8,128)(2,1)S(1)}, u32[]{:S(2)}, u32[]{:S(2)}) async-start(bf16[4,80,128]{2,1,0:T(8,128)(2,1)} %pad_maximum_fusion.1), calls=%async_computation.3 | async-start | bytes 163840 | tf_op jit(solution)/shard_map/all_to_all | solution.py:286
  177.7 18.0 %all-to-all-start.7 = ((f32[16,80,128]{2,1,0:T(8,128)}), f32[16,80,128]{2,1,0:T(8,128)S(1)}, u32[]{:S(2)}, u32[]{:S(2)}) async-start(f32[16,80,128]{2,1,0:T(8,128)} %broadcast_in_dim.147), calls=%async_computation.7 | async-start | bytes 1310720 | tf_op jit(solution)/shard_map/all_to_all | solution.py:286
  185.0 3.8 %copy-start = (bf16[2048,2432]{1,0:T(8,128)(2,1)S(1)}, bf16[2048,2432]{1,0:T(8,128)(2,1)}, u32[]{:S(2)}) copy-start(bf16[2048,2432]{1,0:T(8,128)(2,1)} %all-gather.2.cloned.1.call-done.weight_ref) | copy-start | bytes 29884420
Sparse Core Ops, SparseCore 0:
  10.1 85.5 all-gather.1

commit v2 on v1

--- a/solution.py
+++ b/solution.py
@@ -11,7 +11,9 @@
 IMGS = 2
 LANES = 128
 Q_ROWS = 256
+NOTES = 16
 EPSILON = 1e-06
+HBM = pl.BlockSpec(memory_space=pltpu.HBM)
 VMEM = pl.BlockSpec(memory_space=pltpu.VMEM)
 SMEM = pl.BlockSpec(memory_space=pltpu.SMEM)
 NT = (((1,), (1,)), ((), ()))
@@ -23,26 +25,92 @@
     )
 
 
-def pack_kernel(parts, *refs):
-    ins, out_ref = refs[:-1], refs[-1]
+def pack_kernel(parts, count, route_ref, counts_ref, tile_ref, *refs):
+    ins, out_ref, tagged_ref, semaphore = refs[:count], refs[count], refs[count + 1], refs[count + 2]
     block_rows = sum(ref.shape[0] for ref in ins)
     for part in range(parts):
         row = part * block_rows
         for ref in ins:
             rows = ref.shape[0]
-            out_ref[row : row + rows, :] = ref[:, part * LANES : (part + 1) * LANES]
+            pltpu.make_async_copy(
+                ref.at[:, pl.ds(part * LANES, LANES)], out_ref.at[pl.ds(row, rows), :], semaphore
+            ).start()
             row += rows
-
-
-def pack(arrays, parts):
+    lat = tile_ref.shape[1]
+    tokens = counts_ref[0, 0] + counts_ref[0, 1]
+    tagged_ref[:lat, :] = tile_ref[0]
+    tagged_ref[lat:, :] = notes(route_ref[0], tokens // 16, tokens % 16)
+    pltpu.make_async_copy(out_ref, out_ref, semaphore).wait()
+
+
+def notes(first, second, third):
+    places = lax.broadcasted_iota(jnp.int32, (NOTES, LANES), 0)
+    third_or_none = jnp.where(places == 2, third, 0)
+    numbers = jnp.where(places == 0, first, jnp.where(places == 1, second, third_or_none))
+    return numbers.astype(jnp.float32).astype(jnp.bfloat16)
+
+
+def pack(arrays, parts, tile, route, counts):
     block_rows = sum(array.shape[0] for array in arrays)
     return pl.pallas_call(
-        functools.partial(pack_kernel, parts),
-        out_shape=jax.ShapeDtypeStruct((parts * block_rows, LANES), arrays[0].dtype),
-        in_specs=[VMEM] * len(arrays),
+        functools.partial(pack_kernel, parts, len(arrays)),
+        out_shape=(
+            jax.ShapeDtypeStruct((parts * block_rows, LANES), arrays[0].dtype),
+            jax.ShapeDtypeStruct((tile.shape[1] + NOTES, LANES), tile.dtype),
+        ),
+        in_specs=[SMEM, SMEM, VMEM] + [HBM] * len(arrays),
+        out_specs=(HBM, VMEM),
+        scratch_shapes=[pltpu.SemaphoreType.DMA],
+        compiler_params=params(60),
+    )(route, counts, tile, *arrays)
+
+
+def select_kernel(me_ref, *refs):
+    ins, out_ref = refs[:-1], refs[-1]
+    rows = out_ref.shape[0] // 2
+    lat = rows - NOTES
+    tokens = jnp.zeros((1, 1), jnp.float32)
+    mine = jnp.zeros((lat, LANES), jnp.float32)
+    other = jnp.zeros((lat, LANES), jnp.float32)
+    me = me_ref[0].astype(jnp.float32)
+    beside = (me_ref[0] ^ 1).astype(jnp.float32)
+    for ref in ins:
+        for at in range(0, ref.shape[0], rows):
+            tile = ref[at : at + lat, :].astype(jnp.float32)
+            note = ref[at + lat : at + rows, :].astype(jnp.float32)
+            route = note[0:1, 0:1]
+            mine += jnp.where(route == me, tile, 0.0)
+            other += jnp.where(route == beside, tile, 0.0)
+            tokens += note[1:2, 0:1] * 16.0 + note[2:3, 0:1]
+    high = jnp.floor(tokens * (1.0 / 128.0))
+    places = lax.broadcasted_iota(jnp.int32, (NOTES, LANES), 0)
+    number = jnp.where(places == 1, high, jnp.where(places == 2, tokens - high * 128.0, 0.0))
+    for half, tile in enumerate((mine, other)):
+        out_ref[half * rows : half * rows + lat, :] = tile.astype(jnp.bfloat16)
+        out_ref[half * rows + lat : (half + 1) * rows, :] = number.astype(jnp.bfloat16)
+
+
+def land(tagged, ranks):
+    held = [tagged]
+    step = ranks // 2
+    while step > 1:
+        have = held[0] if len(held) == 1 else jnp.concatenate(held, axis=0)
+        held = [have, swap(have, ranks, step)]
+        step //= 2
+    rows = tagged.shape[0]
+    chosen = pl.pallas_call(
+        select_kernel,
+        out_shape=jax.ShapeDtypeStruct((2 * rows, LANES), tagged.dtype),
+        in_specs=[SMEM] + [VMEM] * len(held),
         out_specs=VMEM,
         compiler_params=params(32),
-    )(*arrays)
+    )(lax.axis_index("dp").astype(jnp.int32).reshape(1), *held)
+    mine, other = chosen[:rows], chosen[rows:]
+    return mine, swap(other, ranks, 1) if ranks > 1 else jnp.zeros_like(other)
+
+
+def swap(array, ranks, step):
+    return lax.ppermute(array, "dp", [(rank, rank ^ step) for rank in range(ranks)])
 
 
 def head_norm(rows, gain, same_head):
@@ -152,9 +220,17 @@
     )(counts, lengths, recv, twice(query_gain), twice(key_gain))
 
 
+def thirds(number, row):
+    high = number.astype(jnp.bfloat16).astype(jnp.float32)
+    middle = (number - high).astype(jnp.bfloat16).astype(jnp.float32)
+    low = number - high - middle
+    rest = jnp.where(row == 1, middle, jnp.where(row == 2, low, 0.0))
+    return jnp.where(row == 0, high, rest).astype(jnp.bfloat16)
+
+
 def head_kernel(
-    steps, layout_ref, total_ref, rows_ref, weight_ref, residual_ref, modulate_ref, final_ref,
-    noise_ref, landed_ref, velocity_ref, grad_ref, parts_ref, sum_ref,
+    steps, place_ref, counts_ref, rows_ref, weight_ref, residual_ref, modulate_ref, final_ref,
+    noise_ref, near_ref, far_ref, velocity_ref, grad_ref, parts_ref, total_ref, sum_ref,
 ):
     step = pl.program_id(0)
     tile, width = residual_ref.shape
@@ -172,7 +248,15 @@
 
     @pl.when(step == steps - 1)
     def _():
-        first = layout_ref[0] == 0
+        place = place_ref[0] * tile
+        border = (counts_ref[0, 0] + tile - 1) // tile * tile
+        first = place < border
+        used_rows = jnp.where(first, counts_ref[0, 0], border + counts_ref[0, 1]) - place
+        total = jnp.zeros((1, 1), jnp.float32)
+        for ref in (near_ref, far_ref):
+            note = ref[lat:, :].astype(jnp.float32)
+            total += note[1:2, 0:1] * 128.0 + note[2:3, 0:1]
+        total_ref[...] = jnp.broadcast_to(total, total_ref.shape)
         pick = lambda at: jnp.where(
             first,
             modulate_ref[0:1, at * width : (at + 1) * width],
@@ -187,15 +271,17 @@
         mixed = (normed * scale + shift).astype(jnp.bfloat16)
         velocity = lax.dot_general(final_ref[...], mixed, NT, preferred_element_type=jnp.float32)
         velocity_ref[...] = velocity
-        target = noise_ref[...].astype(jnp.float32) - landed_ref[...].astype(jnp.float32)
-        used = lax.broadcasted_iota(jnp.int32, (lat, tile), 1) < layout_ref[1]
+        landed = near_ref[:lat, :].astype(jnp.float32) + far_ref[:lat, :].astype(jnp.float32)
+        target = noise_ref[...].astype(jnp.float32) - landed
+        used = lax.broadcasted_iota(jnp.int32, (lat, tile), 1) < used_rows
         error = jnp.where(used, velocity - target, 0.0)
-        grad_wide = error * (2.0 / (total_ref[0] * lat))
+        grad_wide = error * (2.0 / (total * lat))
         grad_columns = grad_wide.astype(jnp.bfloat16)
         final_part = jnp.dot(grad_columns, mixed, preferred_element_type=jnp.float32)
         for at in range(width // LANES):
-            parts_ref[at] = final_part[:, at * LANES : (at + 1) * LANES]
-        parts_ref[width // LANES] = jnp.full((lat, LANES), jnp.sum(error * error))
+            parts_ref[at] = final_part[:, at * LANES : (at + 1) * LANES].astype(jnp.bfloat16)
+        squares = jnp.sum(error * error, axis=(0, 1), keepdims=True)
+        parts_ref[width // LANES] = thirds(squares, lax.broadcasted_iota(jnp.int32, (lat, LANES), 0))
         grad_rows = grad_wide.T.astype(jnp.bfloat16)
         grad_normed = jnp.dot(grad_rows, final_ref[...], preferred_element_type=jnp.float32) * scale
         grad_hidden = inverse * (
@@ -204,7 +290,7 @@
         grad_ref[...] = (grad_hidden * gate).astype(jnp.bfloat16)
 
 
-def head(layout, total, recv, weight, residual, modulate, final_columns, noise, landed):
+def head(place, counts, recv, weight, residual, modulate, final_columns, noise, near, far):
     tile, width = residual.shape
     lat = final_columns.shape[0]
     depth = 2 * LANES
@@ -217,7 +303,8 @@
         out_shape=(
             jax.ShapeDtypeStruct((lat, tile), jnp.float32),
             jax.ShapeDtypeStruct((tile, width), jnp.bfloat16),
-            jax.ShapeDtypeStruct((blocks, lat, LANES), jnp.float32),
+            jax.ShapeDtypeStruct((blocks, lat, LANES), jnp.bfloat16),
+            jax.ShapeDtypeStruct((8, LANES), jnp.float32),
         ),
         in_specs=[
             SMEM,
@@ -228,16 +315,18 @@
             whole(modulate),
             whole(final_columns),
             whole(noise),
-            whole(landed),
+            whole(near),
+            whole(far),
         ],
         out_specs=(
             pl.BlockSpec((lat, tile), lambda i: (0, 0)),
             pl.BlockSpec((tile, width), lambda i: (0, 0)),
             pl.BlockSpec((blocks, lat, LANES), lambda i: (0, 0, 0)),
+            pl.BlockSpec((8, LANES), lambda i: (0, 0)),
         ),
         scratch_shapes=[pltpu.VMEM((tile, width), jnp.float32)],
         compiler_params=params(48, ("arbitrary",)),
-    )(layout, total, recv, weight, residual, modulate, final_columns, noise, landed)
+    )(place, counts, recv, weight, residual, modulate, final_columns, noise, near, far)
 
 
 def back_kernel(grad_ref, weight_ref, out_ref):
@@ -267,62 +356,59 @@
     )(grad, weight)
 
 
-def unpack_kernel(parts_ref, out_ref):
-    for at in range(out_ref.shape[1] // LANES):
-        out_ref[:, at * LANES : (at + 1) * LANES] = parts_ref[at]
-
-
-def unpack(parts, width):
+def sum_kernel(ranks, loss_row, last_ref, recv_ref, out_ref):
+    rows = out_ref.shape[1]
+    total = recv_ref[:rows, :].astype(jnp.float32)
+    for rank in range(1, ranks):
+        total += recv_ref[rank * rows : (rank + 1) * rows, :].astype(jnp.float32)
+    loss = total[loss_row : loss_row + 1] + total[loss_row + 1 : loss_row + 2] + total[loss_row + 2 : loss_row + 3]
+    row = lax.broadcasted_iota(jnp.int32, (rows, LANES), 0) - loss_row
+    kept = thirds(loss, row)
+    inside = jnp.logical_and(row >= 0, row < 3)
+    changed = jnp.where(inside, kept.astype(jnp.float32), total)
+    result = jnp.where(last_ref[0] == 1, changed, total).astype(jnp.bfloat16)
+    for rank in range(out_ref.shape[0]):
+        out_ref[rank] = result
+
+
+def sum_out(recv, ranks, copies, loss_row, last):
+    rows = recv.shape[0] // ranks
+    result = pl.pallas_call(
+        functools.partial(sum_kernel, ranks, loss_row),
+        out_shape=jax.ShapeDtypeStruct((copies, rows, LANES), jnp.bfloat16),
+        in_specs=[SMEM, VMEM],
+        out_specs=VMEM,
+        compiler_params=params(32),
+    )(last, recv)
+    return result.reshape(copies * rows, LANES)
+
+
+def unpack_kernel(parts_ref, total_ref, out_ref, loss_ref):
+    blocks, lat = parts_ref.shape[:2]
+    for at in range(blocks - 1):
+        out_ref[:, at * LANES : (at + 1) * LANES] = parts_ref[at].astype(jnp.float32)
+    last = parts_ref[blocks - 1, :16, :].astype(jnp.float32)
+    loss = last[0:1] + last[1:2] + last[2:3]
+    loss_ref[...] = jnp.broadcast_to(loss, loss_ref.shape) / (total_ref[...] * lat)
+
+
+def unpack(parts, total, width):
     return pl.pallas_call(
         unpack_kernel,
-        out_shape=jax.ShapeDtypeStruct((parts.shape[1], width), jnp.float32),
-        in_specs=[VMEM],
-        out_specs=VMEM,
+        out_shape=(
+            jax.ShapeDtypeStruct((parts.shape[1], width), jnp.float32),
+            jax.ShapeDtypeStruct((8, LANES), jnp.float32),
+        ),
+        in_specs=[VMEM, VMEM],
+        out_specs=(VMEM, VMEM),
         compiler_params=params(32),
-    )(parts)
+    )(parts, total)
 
 
 def exchange(array, axis, groups=None):
     return lax.all_to_all(
         array, axis, split_axis=0, concat_axis=0, axis_index_groups=groups, tiled=True
     )
-
-
-def digits(value, base, rows, lanes):
-    places = lax.broadcasted_iota(jnp.int32, (rows, lanes), 0)
-    return jnp.where(places == 1, value // base, jnp.where(places == 2, value % base, 0))
-
-
-def route_near(tile, destination, count, near, groups):
-    lat, lanes = tile.shape
-    slots = jnp.arange(near, dtype=jnp.int32)[:, None, None]
-    hit = destination % near == slots
-    notes = digits(count, 16, 16, lanes)[None]
-    first = lax.broadcasted_iota(jnp.int32, notes.shape, 1) == 0
-    notes = jnp.where(first, jnp.where(hit, destination // near + 1, 0), notes)
-    data = jnp.where(hit, tile[None], jnp.zeros_like(tile)[None])
-    sent = jnp.concatenate([data, notes.astype(jnp.bfloat16)], axis=1)
-    return exchange(sent, "dp", groups)
-
-
-def route_far(recv, near, far, lat, groups):
-    notes = recv[:, lat : lat + 3, 0].astype(jnp.float32).astype(jnp.int32)
-    count = jnp.sum(notes[:, 1] * 16 + notes[:, 2])
-    slots = jnp.arange(far, dtype=jnp.int32)[:, None]
-    hit = (notes[:, 0][None, :] == slots + 1)[:, :, None, None]
-    data = jnp.where(hit, recv[None, :, :lat].astype(jnp.float32), 0.0)
-    data = jnp.sum(data, axis=1).astype(jnp.bfloat16)
-    more = digits(count, 128, 16, recv.shape[2])[None].astype(jnp.bfloat16)
-    sent = jnp.concatenate([data, jnp.broadcast_to(more, (far, *more.shape[1:]))], axis=1)
-    recv = exchange(sent, "dp", groups)
-    landed = jnp.sum(recv[:, :lat].astype(jnp.float32), axis=0).astype(jnp.bfloat16)
-    notes = recv[:, lat : lat + 3, 0].astype(jnp.float32)
-    return landed, jnp.sum(notes[:, 1] * 128.0 + notes[:, 2])
-
-
-def sum_over(array, axis, count, groups=None):
-    spread = jnp.broadcast_to(array[None], (count, *array.shape))
-    return jnp.sum(exchange(spread, axis, groups), axis=0)
 
 
 def per_device(
@@ -337,44 +423,35 @@
     far = ranks // near
     near_groups = [[row * near + at for at in range(near)] for row in range(far)]
     far_groups = [[row * near + at for row in range(far)] for at in range(near)]
-    column_index = lax.axis_index("seqt")
+    column_index = lax.axis_index("seqt").astype(jnp.int32)
 
     gathered = lax.all_gather(out_weight, "seqt", axis=0, tiled=True)
-    sent = pack((queries, key_rows, values, text_keys, text_values), sources)
+    sent, tagged = pack(
+        (queries, key_rows, values, text_keys, text_values), sources, latent_tiles, tile_route, image_tokens
+    )
     recv = exchange(sent, "seqt")
-    latent, route, counts, recv = lax.optimization_barrier(
-        (latent_tiles, tile_route, image_tokens, recv)
-    )
-    near_recv = route_near(latent[0], route[0], jnp.sum(counts[0]), near, near_groups)
+    mine, other = land(tagged, ranks)
+    recv, mine, other = lax.optimization_barrier((recv, mine, other))
     heads = attention(
         recv, image_tokens, text_lengths, query_gain, key_gain, sources, tile, text_rows
     )
-    heads, near_recv = lax.optimization_barrier((heads, near_recv))
     attended = exchange(heads, "seqt")
-    attended, near_recv = lax.optimization_barrier((attended, near_recv))
-    landed, total_count = route_far(near_recv, near, far, lat_width, far_groups)
-
-    first_count, second_count = image_tokens[0, 0], image_tokens[0, 1]
-    border = (first_count + tile - 1) // tile * tile
-    place = column_index * rows_here
-    owner = (place >= border).astype(jnp.int32)
-    used = jnp.where(owner == 0, first_count, border + second_count) - place
-    velocity, grad_projected, parts = head(
-        jnp.stack([owner, used]).astype(jnp.int32), total_count.reshape(1), attended, gathered,
-        residual, modulation, final_weight.T, noise_tiles[0], landed,
+    velocity, grad_projected, parts, total = head(
+        column_index.reshape(1), image_tokens, attended, gathered, residual, modulation,
+        final_weight.T, noise_tiles[0], mine, other,
     )
     attention_grad = back(grad_projected, gathered)
 
     blocks = parts.shape[0]
-    mine = exchange(parts.reshape(blocks * lat_width, LANES), "seqt")
-    mine = jnp.sum(mine.reshape(sources, blocks * lat_width // sources, LANES), axis=0)
-    mine = sum_over(mine, "dp", near, near_groups)
-    mine = sum_over(mine, "dp", far, far_groups)
-    spread = jnp.broadcast_to(mine[None], (sources, *mine.shape))
-    sums = exchange(spread, "seqt").reshape(blocks, lat_width, LANES)
-    final_grad = unpack(sums, width).T
-    loss_value = sums[blocks - 1, 0, 0] / (total_count * lat_width)
-    return velocity[None], attention_grad, final_grad, loss_value
+    share = blocks * lat_width // sources
+    loss_row = (blocks - 1) * lat_width - (sources - 1) * share
+    last = (column_index == sources - 1).astype(jnp.int32).reshape(1)
+    sums = exchange(parts.reshape(blocks * lat_width, LANES), "seqt")
+    sums = exchange(sum_out(sums, sources, near, loss_row, last), "dp", near_groups)
+    sums = exchange(sum_out(sums, near, far, loss_row, last), "dp", far_groups)
+    sums = exchange(sum_out(sums, far, sources, loss_row, last), "seqt")
+    final_columns, loss = unpack(sums.reshape(blocks, lat_width, LANES), total, width)
+    return velocity[None], attention_grad, final_columns.T, loss[0, 0]
 
 
 def solution(mesh):

time: 207 us -> 236 us (1.14)
  Pallas kernels: 28.8 us -> 81.9 us
  blocking collectives: 46 us -> 24.8 us
  starting transfers between devices: 35.4 us -> 52.5 us
  between operations: 24.6 us -> 14.9 us
  local copies, waits for them, and re-layouts: 12.6 us -> 4.44 us
  other arithmetic: 4.86 us -> 0.09 us
  waiting for transfers between devices: 53.4 us -> 56.6 us
    pallas_call x2 -> x6, Pallas kernels: 2.35 us -> 55.9 us  [the longest x1 54.1 us: pack(): pl.pallas_call(functools.partial(pack_kernel, parts, len(arrays)), out_sh...]
    ppermute x0 -> x5, waiting for transfers between devices: none -> 38.4 us  [swap(): lax.ppermute(array, 'dp', [(rank, rank ^ step) for rank in range(ranks)])]
    all_to_all x5 -> x4, waiting for transfers between devices: 52.7 us -> 17.6 us  [exchange(): lax.all_to_all(array, axis, split_axis=0, concat_axis=0, axis_index_group...]
    all_to_all x3 -> x2, blocking collectives: 46 us -> 24.8 us  [exchange(): lax.all_to_all(array, axis, split_axis=0, concat_axis=0, axis_index_group...]
    ppermute x0 -> x5, starting transfers between devices: none -> 19.8 us  [swap(): lax.ppermute(array, 'dp', [(rank, rank ^ step) for rank in range(ranks)])]
    unnamed x31 -> x23, local copies, waits for them, and re-layouts: 8.66 us -> 3.91 us
    all_to_all x5 -> x4, starting transfers between devices: 35.4 us -> 32.6 us  [exchange(): lax.all_to_all(array, axis, split_axis=0, concat_axis=0, axis_index_group...]
  transfers between devices with their start and end apart: 6 -> 10, of which waited for: 4 -> 7; matrix products, arithmetic and copies ran while one was open for 4% -> 0% of each run, Pallas kernels for 8% -> 30%
where the time goes in v2:
time: 236 us; the launch traced here: 235 us
  Pallas kernels  81.9 us (35%)
  waiting for transfers between devices  56.6 us (24%)
  starting transfers between devices  52.5 us (22%)
  blocking collectives  24.8 us (11%)
  between operations  14.9 us (6%)
  local copies, waits for them, and re-layouts  4.44 us (2%)
    pallas_call x1, Pallas kernels, pack(): pl.pallas_call(functools.partial(pack_kernel, parts, len(arrays)), out_sh...  54.1 us
    ppermute x5, waiting for transfers between devices, swap(): lax.ppermute(array, 'dp', [(rank, rank ^ step) for rank in range(ranks)])  38.4 us
    all_to_all x4, starting transfers between devices, exchange(): lax.all_to_all(array, axis, split_axis=0, concat_axis=0, axis_index_group...  32.6 us
    all_to_all x2, blocking collectives, exchange(): lax.all_to_all(array, axis, split_axis=0, concat_axis=0, axis_index_group...  24.8 us
    ppermute x5, starting transfers between devices, swap(): lax.ppermute(array, 'dp', [(rank, rank ^ step) for rank in range(ranks)])  19.8 us
    all_to_all x4, waiting for transfers between devices, exchange(): lax.all_to_all(array, axis, split_axis=0, concat_axis=0, axis_index_group...  17.6 us
    pallas_call x1, Pallas kernels, attention(): pl.pallas_call(functools.partial(attention_kernel, sources, tile, text_ro...  10.4 us
    pallas_call x1, Pallas kernels, head(): pl.pallas_call(functools.partial(head_kernel, steps), grid=(steps,), out_...  10.4 us
  transfers between devices with their start and end apart: 10, of which 7 were waited for; matrix products, arithmetic and copies ran while one was open for 0% of the time, Pallas kernels for 30%

profile of v2, /device:TPU:1, one launch (start us, length us, event | category | flops | bytes accessed | tf_op | source)
XLA Modules:
  0.0 235.1 jit_solution(4200857100906891568)
XLA Ops:
  7.2 0.0 all-gather.2.cloned.1.call-start
  7.2 0.7 all-gather.2.cloned.1.call-update
  8.5 54.1 %shard_map.183 = (bf16[6656,128]{1,0:T(8,128)(2,1)}, bf16[80,128]{1,0:T(8,128)(2,1)}) custom-call(s32[1]{0:T(128)S(6)} %copy.23.route_ref, s32[1,2]{1,0:T(1,128)} %counts_ref.5, bf16[1,64,128]{2,1,0:T(8,128)(2,1)} %tile_ref.1, bf16[128,2048]{1,0:T(8,128)(2,1)} %refs_0_.1, bf16[128,2048]{1,0:T(8,128)(2,1)} %refs_1_.1, bf16[128,2048]{1,0:T(8,128)(2,1)} %refs_2_.1, ...), custom_call_target="tpu_custom_call" | custom-call | tf_op jit(solution)/shard_map/pallas_call | solution.py:55
  62.6 0.0 copy-start.7
  62.6 0.0 copy-start.8
  62.6 0.0 copy-start.9
  62.7 0.0 copy-start.5
  62.7 0.0 copy-start.6
  62.7 10.5 %all-to-all-start = ((bf16[16,416,128]{2,1,0:T(8,128)(2,1)}), bf16[16,416,128]{2,1,0:T(8,128)(2,1)S(1)}, u32[]{:S(2)}, u32[]{:S(2)}) async-start(bf16[16,416,128]{2,1,0:T(8,128)(2,1)} %bitcast.29), calls=%async_computation | async-start | bytes 3407872 | tf_op jit(solution)/shard_map/all_to_all | solution.py:409
  73.2 0.0 copy-done.7
  73.2 3.0 %collective-permute-start = (bf16[80,128]{1,0:T(8,128)(2,1)S(1)}, bf16[80,128]{1,0:T(8,128)(2,1)S(1)}, u32[]{:S(2)}, u32[]{:S(2)}) collective-permute-start(bf16[80,128]{1,0:T(8,128)(2,1)S(1)} %copy-done.7), channel_id=1, source_target_pairs={{0,256},{16,272},{32,288},{48,304},{64,320},{80,336},{96,352},{112... | collective-permute-start | bytes 61448 | tf_op jit(solution)/shard_map/ppermute | solution.py:113
  76.3 25.5 %collective-permute-done = bf16[80,128]{1,0:T(8,128)(2,1)S(1)} collective-permute-done((bf16[80,128]{1,0:T(8,128)(2,1)S(1)}, bf16[80,128]{1,0:T(8,128)(2,1)S(1)}, u32[]{:S(2)}, u32[]{:S(2)}) %collective-permute-start) | collective-permute-done | bytes 20512 | tf_op jit(solution)/shard_map/ppermute | solution.py:113
  101.8 2.2 collective-permute-start.1
  104.0 3.4 %collective-permute-done.1 = bf16[160,128]{1,0:T(8,128)(2,1)S(1)} collective-permute-done((bf16[160,128]{1,0:T(8,128)(2,1)S(1)}, bf16[160,128]{1,0:T(8,128)(2,1)S(1)}, u32[]{:S(2)}, u32[]{:S(2)}) %collective-permute-start.1) | collective-permute-done | bytes 40992 | tf_op jit(solution)/shard_map/ppermute | solution.py:113
  107.4 7.7 %collective-permute-start.2 = (bf16[320,128]{1,0:T(8,128)(2,1)S(1)}, bf16[320,128]{1,0:T(8,128)(2,1)S(1)}, u32[]{:S(2)}, u32[]{:S(2)}) collective-permute-start(bf16[320,128]{1,0:T(8,128)(2,1)S(1)} %pad_maximum_fusion), channel_id=1, source_target_pairs={{0,64},{16,80},{32,96},{48,112},{64,0},{80,16},{96,32},{112,48},{1... | collective-permute-start | bytes 245768 | tf_op jit(solution)/shard_map/ppermute | solution.py:113
  115.1 1.9 collective-permute-done.2
  117.1 4.8 %collective-permute-start.3 = (bf16[640,128]{1,0:T(8,128)(2,1)S(1)}, bf16[640,128]{1,0:T(8,128)(2,1)S(1)}, u32[]{:S(2)}, u32[]{:S(2)}) collective-permute-start(bf16[640,128]{1,0:T(8,128)(2,1)S(1)} %constant_dynamic-update-slice_fusion.refs_0_), channel_id=1, source_target_pairs={{0,32},{16,48},{32,0},{48,16},{64,96},{80,112},{96,64},{112,80},{1... | collective-permute-start | bytes 491528 | tf_op jit(solution)/shard_map/ppermute | solution.py:113
  121.8 5.1 %collective-permute-done.3.refs_1_ = bf16[640,128]{1,0:T(8,128)(2,1)S(1)} collective-permute-done((bf16[640,128]{1,0:T(8,128)(2,1)S(1)}, bf16[640,128]{1,0:T(8,128)(2,1)S(1)}, u32[]{:S(2)}, u32[]{:S(2)}) %collective-permute-start.3) | collective-permute-done | bytes 163872 | tf_op jit(solution)/shard_map/ppermute | solution.py:113
  126.9 0.1 shard_map.184
  127.1 0.0 copy-start.1
  127.1 0.0 copy-start.2
  127.1 0.0 copy-start.3
  127.1 0.0 copy-start.4
  127.1 2.1 collective-permute-start.4
  129.2 0.0 copy-done.8
  129.2 0.0 copy-done.9
  129.2 0.1 maximum_bitcast_fusion
  129.3 2.5 %collective-permute-done.4.far_ref = bf16[80,128]{1,0:T(8,128)(2,1)S(1)} collective-permute-done((bf16[80,128]{1,0:T(8,128)(2,1)S(1)}, bf16[80,128]{1,0:T(8,128)(2,1)S(1)}, u32[]{:S(2)}, u32[]{:S(2)}) %collective-permute-start.4) | collective-permute-done | bytes 20512 | tf_op jit(solution)/shard_map/ppermute | solution.py:113
  131.8 0.0 all-to-all-done
  131.8 0.0 copy-done.6
  131.8 10.4 %shard_map.185 = bf16[2048,128]{1,0:T(8,128)(2,1)} custom-call(s32[1,2]{1,0:T(1,128)S(1)} %copy-done.5, s32[1,2]{1,0:T(1,128)S(1)} %copy-done.6, bf16[6656,128]{1,0:T(8,128)(2,1)S(1)} %bitcast.21, f32[1,128]{1,0:T(1,128)S(1)} %get-tuple-element.28.query_gain_ref, f32[1,128]{1,0:T(1,128)S(1)} %get-tuple-element.29.key_gain_ref), custom_call_target="tpu_custom_call" | custom-call | tf_op jit(solution)/shard_map/pallas_call | solution.py:207
  142.2 10.0 %all-to-all-start.1 = ((bf16[16,128,128]{2,1,0:T(8,128)(2,1)}), bf16[16,128,128]{2,1,0:T(8,128)(2,1)S(1)}, u32[]{:S(2)}, u32[]{:S(2)}) async-start(bf16[16,128,128]{2,1,0:T(8,128)(2,1)} %bitcast.6), calls=%async_computation.1 | async-start | bytes 1048576 | tf_op jit(solution)/shard_map/all_to_all | solution.py:409
  152.2 9.8 %all-to-all-done.1 = bf16[16,128,128]{2,1,0:T(8,128)(2,1)S(1)} async-done(((bf16[16,128,128]{2,1,0:T(8,128)(2,1)}), bf16[16,128,128]{2,1,0:T(8,128)(2,1)S(1)}, u32[]{:S(2)}, u32[]{:S(2)}) %all-to-all-start.1) | async-done | bytes 524320 | tf_op jit(solution)/shard_map/all_to_all | solution.py:409
  162.0 0.0 copy-done.2
  162.0 0.0 copy-done.4
  162.0 10.4 %shard_map.186 = (f32[64,128]{1,0:T(8,128)}, bf16[128,2432]{1,0:T(8,128)(2,1)S(1)}, bf16[20,64,128]{2,1,0:T(8,128)(2,1)}, f32[8,128]{1,0:T(8,128)S(1)}) custom-call(s32[1]{0:T(128)} %bitcast.place_ref, s32[1,2]{1,0:T(1,128)S(1)} %copy-done.5, bf16[2048,128]{1,0:T(8,128)(2,1)S(1)} %bitcast.22, bf16[2048,2432]{1,0:T(8,128)(2,1)} %all-gather.2.cloned.1.call-done.weight_ref, ...), custom_call_target="tpu_custom_call" | custom-call | tf_op jit(solution)/shard_map/pallas_call | solution.py:300
  172.4 4.5 %all-to-all-start.2 = ((bf16[16,80,128]{2,1,0:T(8,128)(2,1)}), bf16[16,80,128]{2,1,0:T(8,128)(2,1)S(1)}, u32[]{:S(2)}, u32[]{:S(2)}) async-start(bf16[16,80,128]{2,1,0:T(8,128)(2,1)} %bitcast.12), calls=%async_computation.2 | async-start | bytes 655360 | tf_op jit(solution)/shard_map/all_to_all | solution.py:409
  176.9 7.8 %all-to-all-done.2 = bf16[16,80,128]{2,1,0:T(8,128)(2,1)S(1)} async-done(((bf16[16,80,128]{2,1,0:T(8,128)(2,1)}), bf16[16,80,128]{2,1,0:T(8,128)(2,1)S(1)}, u32[]{:S(2)}, u32[]{:S(2)}) %all-to-all-start.2) | async-done | bytes 327712 | tf_op jit(solution)/shard_map/all_to_all | solution.py:409
  184.6 0.1 shard_map.188
  184.7 14.2 %all_to_all.56 = bf16[8,80,128]{2,1,0:T(8,128)(2,1)S(1)} all-to-all(bf16[8,80,128]{2,1,0:T(8,128)(2,1)S(1)} %shard_map.188), channel_id=1, replica_groups={{0,16,32,48,64,80,96,112},{128,144,160,176,192,208,224,240},{256,272,28..., dimensions={0} | all-to-all | bytes 327680 | tf_op jit(solution)/shard_map/all_to_all | solution.py:409
  199.0 10.5 %all_to_all.57 = bf16[4,80,128]{2,1,0:T(8,128)(2,1)S(1)} all-to-all(bf16[4,80,128]{2,1,0:T(8,128)(2,1)S(1)} %shard_map.189), channel_id=1, replica_groups={{0,128,256,384},{16,144,272,400},{32,160,288,416},{48,176,304,432},{64,..., dimensions={0} | all-to-all | bytes 163840 | tf_op jit(solution)/shard_map/all_to_all | solution.py:409
  209.5 0.8 shard_map.190
  210.2 7.6 %all-to-all-start.5 = ((bf16[16,80,128]{2,1,0:T(8,128)(2,1)}), bf16[16,80,128]{2,1,0:T(8,128)(2,1)S(1)}, u32[]{:S(2)}, u32[]{:S(2)}) async-start(bf16[16,80,128]{2,1,0:T(8,128)(2,1)} %shard_map.190), calls=%async_computation.5 | async-start | bytes 655360 | tf_op jit(solution)/shard_map/all_to_all | solution.py:409
  217.8 3.8 %copy-done = bf16[2048,2432]{1,0:T(8,128)(2,1)S(1)} copy-done((bf16[2048,2432]{1,0:T(8,128)(2,1)S(1)}, bf16[2048,2432]{1,0:T(8,128)(2,1)}, u32[]{:S(2)}) %copy-start) | copy-done | bytes 9961496
  221.7 5.2 %shard_map.187 = bf16[128,2048]{1,0:T(8,128)(2,1)} custom-call(bf16[128,2432]{1,0:T(8,128)(2,1)S(1)} %get-tuple-element.21.grad_ref, bf16[2048,2432]{1,0:T(8,128)(2,1)S(1)} %copy-done), custom_call_target="tpu_custom_call" | custom-call | flops 1275068416 | bytes 9961472 | tf_op jit(solution)/shard_map/pallas_call | solution.py:341
  226.9 0.0 all-to-all-done.5
  226.9 0.9 shard_map.191
  227.8 0.5 slice.11
  (13 shorter events, 0.1 us)
Async XLA Ops:
  7.2 154.8 %all-gather.2.cloned.1.call-start = ((), (), s32[]{:S(2)}) async-start(), calls=%async_computation.6 | async-start | bytes 10584064 | tf_op jit(solution)/shard_map/all_gather | solution.py:428
  62.6 10.6 %copy-start.7 = (bf16[80,128]{1,0:T(8,128)(2,1)S(1)}, bf16[80,128]{1,0:T(8,128)(2,1)}, u32[]{:S(2)}) copy-start(bf16[80,128]{1,0:T(8,128)(2,1)} %get-tuple-element.16) | copy-start | bytes 61444
  62.6 66.6 %copy-start.8 = (f32[64]{0:T(128)S(1)}, f32[64]{0:T(128)}, u32[]{:S(2)}) copy-start(f32[64]{0:T(128)} %param.25) | copy-start | bytes 772
  62.6 66.6 %copy-start.9 = (f32[64]{0:T(128)S(1)}, f32[64]{0:T(128)}, u32[]{:S(2)}) copy-start(f32[64]{0:T(128)} %param.26) | copy-start | bytes 772
  62.7 69.1 %copy-start.5 = (s32[1,2]{1,0:T(1,128)S(1)}, s32[1,2]{1,0:T(1,128)}, u32[]{:S(2)}) copy-start(s32[1,2]{1,0:T(1,128)} %counts_ref.5) | copy-start | bytes 28
  62.7 69.1 %copy-start.6 = (s32[1,2]{1,0:T(1,128)S(1)}, s32[1,2]{1,0:T(1,128)}, u32[]{:S(2)}) copy-start(s32[1,2]{1,0:T(1,128)} %lengths_ref.1) | copy-start | bytes 28
  62.7 69.1 %all-to-all-start = ((bf16[16,416,128]{2,1,0:T(8,128)(2,1)}), bf16[16,416,128]{2,1,0:T(8,128)(2,1)S(1)}, u32[]{:S(2)}, u32[]{:S(2)}) async-start(bf16[16,416,128]{2,1,0:T(8,128)(2,1)} %bitcast.29), calls=%async_computation | async-start | bytes 3407872 | tf_op jit(solution)/shard_map/all_to_all | solution.py:409
  73.2 28.6 %collective-permute-start = (bf16[80,128]{1,0:T(8,128)(2,1)S(1)}, bf16[80,128]{1,0:T(8,128)(2,1)S(1)}, u32[]{:S(2)}, u32[]{:S(2)}) collective-permute-start(bf16[80,128]{1,0:T(8,128)(2,1)S(1)} %copy-done.7), channel_id=1, source_target_pairs={{0,256},{16,272},{32,288},{48,304},{64,320},{80,336},{96,352},{112... | collective-permute-start | bytes 61448 | tf_op jit(solution)/shard_map/ppermute | solution.py:113
  101.8 5.6 %collective-permute-start.1 = (bf16[160,128]{1,0:T(8,128)(2,1)S(1)}, bf16[160,128]{1,0:T(8,128)(2,1)S(1)}, u32[]{:S(2)}, u32[]{:S(2)}) collective-permute-start(bf16[160,128]{1,0:T(8,128)(2,1)S(1)} %pad_maximum_fusion.1), channel_id=1, source_target_pairs={{0,128},{16,144},{32,160},{48,176},{64,192},{80,208},{96,224},{112... | collective-permute-start | bytes 122888 | tf_op jit(solution)/shard_map/ppermute | solution.py:113
  107.4 9.6 %collective-permute-start.2 = (bf16[320,128]{1,0:T(8,128)(2,1)S(1)}, bf16[320,128]{1,0:T(8,128)(2,1)S(1)}, u32[]{:S(2)}, u32[]{:S(2)}) collective-permute-start(bf16[320,128]{1,0:T(8,128)(2,1)S(1)} %pad_maximum_fusion), channel_id=1, source_target_pairs={{0,64},{16,80},{32,96},{48,112},{64,0},{80,16},{96,32},{112,48},{1... | collective-permute-start | bytes 245768 | tf_op jit(solution)/shard_map/ppermute | solution.py:113
  117.1 9.8 %collective-permute-start.3 = (bf16[640,128]{1,0:T(8,128)(2,1)S(1)}, bf16[640,128]{1,0:T(8,128)(2,1)S(1)}, u32[]{:S(2)}, u32[]{:S(2)}) collective-permute-start(bf16[640,128]{1,0:T(8,128)(2,1)S(1)} %constant_dynamic-update-slice_fusion.refs_0_), channel_id=1, source_target_pairs={{0,32},{16,48},{32,0},{48,16},{64,96},{80,112},{96,64},{112,80},{1... | collective-permute-start | bytes 491528 | tf_op jit(solution)/shard_map/ppermute | solution.py:113
  127.1 34.9 %copy-start.1 = (bf16[128,2432]{1,0:T(8,128)(2,1)S(1)}, bf16[128,2432]{1,0:T(8,128)(2,1)}, u32[]{:S(2)}) copy-start(bf16[128,2432]{1,0:T(8,128)(2,1)} %residual_ref.1) | copy-start | bytes 1867780
  127.1 34.9 %copy-start.2 = (bf16[2432,64]{0,1:T(8,128)(2,1)S(1)}, bf16[2432,64]{0,1:T(8,128)(2,1)}, u32[]{:S(2)}) copy-start(bf16[2432,64]{0,1:T(8,128)(2,1)} %param.30) | copy-start | bytes 933892
  127.1 34.9 %copy-start.3 = (f32[2,7296]{1,0:T(2,128)S(1)}, f32[2,7296]{1,0:T(2,128)}, u32[]{:S(2)}) copy-start(f32[2,7296]{1,0:T(2,128)} %modulate_ref.1) | copy-start | bytes 175108
  127.1 34.9 %copy-start.4 = (bf16[1,64,128]{2,1,0:T(8,128)(2,1)S(1)}, bf16[1,64,128]{2,1,0:T(8,128)(2,1)}, u32[]{:S(2)}) copy-start(bf16[1,64,128]{2,1,0:T(8,128)(2,1)} %param.31) | copy-start | bytes 49156
  127.1 4.7 %collective-permute-start.4 = (bf16[80,128]{1,0:T(8,128)(2,1)S(1)}, bf16[80,128]{1,0:T(8,128)(2,1)S(1)}, u32[]{:S(2)}, u32[]{:S(2)}) collective-permute-start(bf16[80,128]{1,0:T(8,128)(2,1)S(1)} %get-tuple-element.26), channel_id=1, source_target_pairs={{0,16},{16,0},{32,48},{48,32},{64,80},{80,64},{96,112},{112,96},{1... | collective-permute-start | bytes 61448 | tf_op jit(solution)/shard_map/ppermute | solution.py:113
  142.2 19.8 %all-to-all-start.1 = ((bf16[16,128,128]{2,1,0:T(8,128)(2,1)}), bf16[16,128,128]{2,1,0:T(8,128)(2,1)S(1)}, u32[]{:S(2)}, u32[]{:S(2)}) async-start(bf16[16,128,128]{2,1,0:T(8,128)(2,1)} %bitcast.6), calls=%async_computation.1 | async-start | bytes 1048576 | tf_op jit(solution)/shard_map/all_to_all | solution.py:409
  172.4 12.3 %all-to-all-start.2 = ((bf16[16,80,128]{2,1,0:T(8,128)(2,1)}), bf16[16,80,128]{2,1,0:T(8,128)(2,1)S(1)}, u32[]{:S(2)}, u32[]{:S(2)}) async-start(bf16[16,80,128]{2,1,0:T(8,128)(2,1)} %bitcast.12), calls=%async_computation.2 | async-start | bytes 655360 | tf_op jit(solution)/shard_map/all_to_all | solution.py:409
  210.2 16.7 %all-to-all-start.5 = ((bf16[16,80,128]{2,1,0:T(8,128)(2,1)}), bf16[16,80,128]{2,1,0:T(8,128)(2,1)S(1)}, u32[]{:S(2)}, u32[]{:S(2)}) async-start(bf16[16,80,128]{2,1,0:T(8,128)(2,1)} %shard_map.190), calls=%async_computation.5 | async-start | bytes 655360 | tf_op jit(solution)/shard_map/all_to_all | solution.py:409
  217.8 3.8 %copy-start = (bf16[2048,2432]{1,0:T(8,128)(2,1)S(1)}, bf16[2048,2432]{1,0:T(8,128)(2,1)}, u32[]{:S(2)}) copy-start(bf16[2048,2432]{1,0:T(8,128)(2,1)} %all-gather.2.cloned.1.call-done.weight_ref) | copy-start | bytes 29884420
Sparse Core Ops, SparseCore 0:
  10.1 80.4 all-gather.1

commit v3 on v2

--- a/solution.py
+++ b/solution.py
@@ -59,21 +59,21 @@
             jax.ShapeDtypeStruct((tile.shape[1] + NOTES, LANES), tile.dtype),
         ),
         in_specs=[SMEM, SMEM, VMEM] + [HBM] * len(arrays),
-        out_specs=(HBM, VMEM),
+        out_specs=(VMEM, VMEM),
         scratch_shapes=[pltpu.SemaphoreType.DMA],
         compiler_params=params(60),
     )(route, counts, tile, *arrays)
 
 
-def select_kernel(me_ref, *refs):
+def select_kernel(last, me_ref, *refs):
     ins, out_ref = refs[:-1], refs[-1]
-    rows = out_ref.shape[0] // 2
+    rows = out_ref.shape[1]
     lat = rows - NOTES
     tokens = jnp.zeros((1, 1), jnp.float32)
     mine = jnp.zeros((lat, LANES), jnp.float32)
     other = jnp.zeros((lat, LANES), jnp.float32)
     me = me_ref[0].astype(jnp.float32)
-    beside = (me_ref[0] ^ 1).astype(jnp.float32)
+    beside = (me_ref[0] ^ last).astype(jnp.float32)
     for ref in ins:
         for at in range(0, ref.shape[0], rows):
             tile = ref[at : at + lat, :].astype(jnp.float32)
@@ -86,27 +86,26 @@
     places = lax.broadcasted_iota(jnp.int32, (NOTES, LANES), 0)
     number = jnp.where(places == 1, high, jnp.where(places == 2, tokens - high * 128.0, 0.0))
     for half, tile in enumerate((mine, other)):
-        out_ref[half * rows : half * rows + lat, :] = tile.astype(jnp.bfloat16)
-        out_ref[half * rows + lat : (half + 1) * rows, :] = number.astype(jnp.bfloat16)
-
-
-def land(tagged, ranks):
-    held = [tagged]
-    step = ranks // 2
-    while step > 1:
-        have = held[0] if len(held) == 1 else jnp.concatenate(held, axis=0)
-        held = [have, swap(have, ranks, step)]
-        step //= 2
-    rows = tagged.shape[0]
+        out_ref[half, :lat, :] = tile.astype(jnp.bfloat16)
+        out_ref[half, lat:, :] = number.astype(jnp.bfloat16)
+
+
+def gather(held, ranks, bits):
+    for bit in bits:
+        held = jnp.concatenate([held, swap(held, ranks, bit)], axis=0)
+    return held
+
+
+def land(held, rows, ranks):
+    bit = max(ranks // 2, 1)
     chosen = pl.pallas_call(
-        select_kernel,
-        out_shape=jax.ShapeDtypeStruct((2 * rows, LANES), tagged.dtype),
-        in_specs=[SMEM] + [VMEM] * len(held),
+        functools.partial(select_kernel, bit),
+        out_shape=jax.ShapeDtypeStruct((2, rows, LANES), held.dtype),
+        in_specs=[SMEM, VMEM],
         out_specs=VMEM,
         compiler_params=params(32),
-    )(lax.axis_index("dp").astype(jnp.int32).reshape(1), *held)
-    mine, other = chosen[:rows], chosen[rows:]
-    return mine, swap(other, ranks, 1) if ranks > 1 else jnp.zeros_like(other)
+    )(lax.axis_index("dp").astype(jnp.int32).reshape(1), held)
+    return chosen[0], swap(chosen[1], ranks, bit) if bit < ranks else jnp.zeros_like(chosen[1])
 
 
 def swap(array, ranks, step):
@@ -217,6 +216,11 @@
             pltpu.VMEM((IMGS, 2, keys, LANES), jnp.bfloat16),
         ],
         compiler_params=params(48),
+        cost_estimate=pl.CostEstimate(
+            flops=16 * rows_all * keys * LANES,
+            bytes_accessed=4 * rows_all * LANES * 4,
+            transcendentals=2 * rows_all * keys,
+        ),
     )(counts, lengths, recv, twice(query_gain), twice(key_gain))
 
 
@@ -430,12 +434,16 @@
         (queries, key_rows, values, text_keys, text_values), sources, latent_tiles, tile_route, image_tokens
     )
     recv = exchange(sent, "seqt")
-    mine, other = land(tagged, ranks)
-    recv, mine, other = lax.optimization_barrier((recv, mine, other))
+    bits = [1 << at for at in range(ranks.bit_length() - 1)]
+    held = gather(tagged, ranks, [bit for bit in reversed(bits) if bit < near])
+    recv, held = lax.optimization_barrier((recv, held))
+    held = gather(held, ranks, [bit for bit in bits[:-1] if bit >= near])
     heads = attention(
         recv, image_tokens, text_lengths, query_gain, key_gain, sources, tile, text_rows
     )
+    heads, held = lax.optimization_barrier((heads, held))
     attended = exchange(heads, "seqt")
+    mine, other = land(held, tagged.shape[0], ranks)
     velocity, grad_projected, parts, total = head(
         column_index.reshape(1), image_tokens, attended, gathered, residual, modulation,
         final_weight.T, noise_tiles[0], mine, other,

time: 236 us -> 179 us (0.76)
  Pallas kernels: 81.9 us -> 31.3 us
  starting transfers between devices: 52.5 us -> 45.2 us
  blocking collectives: 24.8 us -> 27.2 us
    pallas_call x1, Pallas kernels: 54.1 us -> 3.42 us  [pack(): pl.pallas_call(functools.partial(pack_kernel, parts, len(arrays)), out_sh...]
    ppermute x5, waiting for transfers between devices: 38.4 us -> 17.3 us  [swap(): lax.ppermute(array, 'dp', [(rank, rank ^ step) for rank in range(ranks)])]
    all_gather x1, waiting for transfers between devices: 0.01 us -> 12.3 us  [per_device(): gathered = lax.all_gather(out_weight, 'seqt', axis=0, tiled=True)]
    all_to_all x4, waiting for transfers between devices: 17.6 us -> 24.3 us  [exchange(): lax.all_to_all(array, axis, split_axis=0, concat_axis=0, axis_index_group...]
    all_to_all x4, starting transfers between devices: 32.6 us -> 27.6 us  [exchange(): lax.all_to_all(array, axis, split_axis=0, concat_axis=0, axis_index_group...]
    all_to_all x2, blocking collectives: 24.8 us -> 27.2 us  [exchange(): lax.all_to_all(array, axis, split_axis=0, concat_axis=0, axis_index_group...]
  transfers between devices with their start and end apart: 10 -> 10, of which waited for: 7 -> 8; matrix products, arithmetic and copies ran while one was open for 0% -> 0% of each run, Pallas kernels for 30% -> 11%
where the time goes in v3:
time: 179 us; the launch traced here: 178 us
  waiting for transfers between devices  54.5 us (30%)
  starting transfers between devices  45.2 us (25%)
  Pallas kernels  31.3 us (17%)
  blocking collectives  27.2 us (15%)
  between operations  14.9 us (8%)
  local copies, waits for them, and re-layouts  4.39 us (2%)
    all_to_all x4, starting transfers between devices, exchange(): lax.all_to_all(array, axis, split_axis=0, concat_axis=0, axis_index_group...  27.6 us
    all_to_all x2, blocking collectives, exchange(): lax.all_to_all(array, axis, split_axis=0, concat_axis=0, axis_index_group...  27.2 us
    all_to_all x4, waiting for transfers between devices, exchange(): lax.all_to_all(array, axis, split_axis=0, concat_axis=0, axis_index_group...  24.3 us
    ppermute x5, starting transfers between devices, swap(): lax.ppermute(array, 'dp', [(rank, rank ^ step) for rank in range(ranks)])  17.5 us
    ppermute x5, waiting for transfers between devices, swap(): lax.ppermute(array, 'dp', [(rank, rank ^ step) for rank in range(ranks)])  17.3 us
    all_gather x1, waiting for transfers between devices, per_device(): gathered = lax.all_gather(out_weight, 'seqt', axis=0, tiled=True)  12.3 us
    pallas_call x1, Pallas kernels, head(): pl.pallas_call(functools.partial(head_kernel, steps), grid=(steps,), out_...  10.4 us
    pallas_call x1, Pallas kernels, attention(): pl.pallas_call(functools.partial(attention_kernel, sources, tile, text_ro...  10.4 us
  transfers between devices with their start and end apart: 10, of which 8 were waited for; matrix products, arithmetic and copies ran while one was open for 0% of the time, Pallas kernels for 11%

profile of v3, /device:TPU:1, one launch (start us, length us, event | category | flops | bytes accessed | tf_op | source)
XLA Modules:
  0.0 177.5 jit_solution(10293731271681914602)
XLA Ops:
  7.2 0.0 all-gather.2.cloned.1.call-start
  7.2 0.7 all-gather.2.cloned.1.call-update
  8.5 3.4 %shard_map.183 = (bf16[6656,128]{1,0:T(8,128)(2,1)}, bf16[80,128]{1,0:T(8,128)(2,1)}) custom-call(s32[1]{0:T(128)S(6)} %copy.20.route_ref, s32[1,2]{1,0:T(1,128)} %counts_ref.5, bf16[1,64,128]{2,1,0:T(8,128)(2,1)} %tile_ref.1, bf16[128,2048]{1,0:T(8,128)(2,1)} %refs_0_.1, bf16[128,2048]{1,0:T(8,128)(2,1)} %refs_1_.1, bf16[128,2048]{1,0:T(8,128)(2,1)} %refs_2_.1, ...), custom_call_target="tpu_custom_call" | custom-call | tf_op jit(solution)/shard_map/pallas_call | solution.py:55
  12.0 0.0 copy-start.7
  12.0 0.0 copy-start.8
  12.0 0.0 copy-start.9
  12.0 0.0 copy-start.5
  12.0 0.0 copy-start.6
  12.0 10.5 %all-to-all-start = ((bf16[16,416,128]{2,1,0:T(8,128)(2,1)}), bf16[16,416,128]{2,1,0:T(8,128)(2,1)S(1)}, u32[]{:S(2)}, u32[]{:S(2)}) async-start(bf16[16,416,128]{2,1,0:T(8,128)(2,1)} %bitcast.33), calls=%async_computation | async-start | bytes 3407872 | tf_op jit(solution)/shard_map/all_to_all | solution.py:413
  22.6 0.0 copy-done.7
  22.6 7.1 %collective-permute-start = (bf16[80,128]{1,0:T(8,128)(2,1)S(1)}, bf16[80,128]{1,0:T(8,128)(2,1)S(1)}, u32[]{:S(2)}, u32[]{:S(2)}) collective-permute-start(bf16[80,128]{1,0:T(8,128)(2,1)S(1)} %copy-done.7), channel_id=1, source_target_pairs={{0,64},{16,80},{32,96},{48,112},{64,0},{80,16},{96,32},{112,48},{1... | collective-permute-start | bytes 61448 | tf_op jit(solution)/shard_map/ppermute | solution.py:112
  29.7 1.4 collective-permute-done
  31.1 3.8 %collective-permute-start.1 = (bf16[160,128]{1,0:T(8,128)(2,1)S(1)}, bf16[160,128]{1,0:T(8,128)(2,1)S(1)}, u32[]{:S(2)}, u32[]{:S(2)}) collective-permute-start(bf16[160,128]{1,0:T(8,128)(2,1)S(1)} %pad_maximum_fusion.3), channel_id=1, source_target_pairs={{0,32},{16,48},{32,0},{48,16},{64,96},{80,112},{96,64},{112,80},{1... | collective-permute-start | bytes 122888 | tf_op jit(solution)/shard_map/ppermute | solution.py:112
  34.8 2.2 %collective-permute-done.1 = bf16[160,128]{1,0:T(8,128)(2,1)S(1)} collective-permute-done((bf16[160,128]{1,0:T(8,128)(2,1)S(1)}, bf16[160,128]{1,0:T(8,128)(2,1)S(1)}, u32[]{:S(2)}, u32[]{:S(2)}) %collective-permute-start.1) | collective-permute-done | bytes 40992 | tf_op jit(solution)/shard_map/ppermute | solution.py:112
  37.0 2.8 %collective-permute-start.2 = (bf16[320,128]{1,0:T(8,128)(2,1)S(1)}, bf16[320,128]{1,0:T(8,128)(2,1)S(1)}, u32[]{:S(2)}, u32[]{:S(2)}) collective-permute-start(bf16[320,128]{1,0:T(8,128)(2,1)S(1)} %pad_maximum_fusion.2), channel_id=1, source_target_pairs={{0,16},{16,0},{32,48},{48,32},{64,80},{80,64},{96,112},{112,96},{1... | collective-permute-start | bytes 245768 | tf_op jit(solution)/shard_map/ppermute | solution.py:112
  39.9 0.0 copy-done.8
  39.9 0.0 copy-done.9
  39.9 0.1 maximum_bitcast_fusion
  39.9 2.6 %collective-permute-done.2 = bf16[320,128]{1,0:T(8,128)(2,1)S(1)} collective-permute-done((bf16[320,128]{1,0:T(8,128)(2,1)S(1)}, bf16[320,128]{1,0:T(8,128)(2,1)S(1)}, u32[]{:S(2)}, u32[]{:S(2)}) %collective-permute-start.2) | collective-permute-done | bytes 81952 | tf_op jit(solution)/shard_map/ppermute | solution.py:112
  42.6 13.7 %all-to-all-done = bf16[16,416,128]{2,1,0:T(8,128)(2,1)S(1)} async-done(((bf16[16,416,128]{2,1,0:T(8,128)(2,1)}), bf16[16,416,128]{2,1,0:T(8,128)(2,1)S(1)}, u32[]{:S(2)}, u32[]{:S(2)}) %all-to-all-start) | async-done | bytes 1703968 | tf_op jit(solution)/shard_map/all_to_all | solution.py:413
  56.3 1.9 %collective-permute-start.3 = (bf16[640,128]{1,0:T(8,128)(2,1)S(1)}, bf16[640,128]{1,0:T(8,128)(2,1)S(1)}, u32[]{:S(2)}, u32[]{:S(2)}) collective-permute-start(bf16[640,128]{1,0:T(8,128)(2,1)S(1)} %pad_maximum_fusion.1), channel_id=1, source_target_pairs={{0,128},{16,144},{32,160},{48,176},{64,192},{80,208},{96,224},{112... | collective-permute-start | bytes 491528 | tf_op jit(solution)/shard_map/ppermute | solution.py:112
  58.2 0.0 copy-done.5
  58.2 0.0 copy-done.6
  58.2 10.4 %shard_map.184 = bf16[2048,128]{1,0:T(8,128)(2,1)} custom-call(s32[1,2]{1,0:T(1,128)S(1)} %copy-done.5, s32[1,2]{1,0:T(1,128)S(1)} %copy-done.6, bf16[6656,128]{1,0:T(8,128)(2,1)S(1)} %bitcast.26, f32[1,128]{1,0:T(1,128)S(1)} %get-tuple-element.30.query_gain_ref, f32[1,128]{1,0:T(1,128)S(1)} %get-tuple-element.31.key_gain_ref), custom_call_target="tpu_custom_call" | custom-call | flops 4831838208 | bytes 4194304 | tf_op jit(solution)/shard_map/pallas_call | solution.py:206
  68.6 0.0 collective-permute-done.3
  68.7 5.3 %all-to-all-start.1 = ((bf16[16,128,128]{2,1,0:T(8,128)(2,1)}), bf16[16,128,128]{2,1,0:T(8,128)(2,1)S(1)}, u32[]{:S(2)}, u32[]{:S(2)}) async-start(bf16[16,128,128]{2,1,0:T(8,128)(2,1)} %bitcast.5), calls=%async_computation.1 | async-start | bytes 1048576 | tf_op jit(solution)/shard_map/all_to_all | solution.py:413
  74.0 0.1 shard_map.185
  74.1 1.9 %collective-permute-start.4 = (bf16[80,128]{1,0:T(8,128)(2,1)S(1)}, bf16[80,128]{1,0:T(8,128)(2,1)S(1)}, u32[]{:S(2)}, u32[]{:S(2)}) collective-permute-start(bf16[80,128]{1,0:T(8,128)(2,1)S(1)} %get-tuple-element.28), channel_id=1, source_target_pairs={{0,256},{16,272},{32,288},{48,304},{64,320},{80,336},{96,352},{112... | collective-permute-start | bytes 61448 | tf_op jit(solution)/shard_map/ppermute | solution.py:112
  76.1 11.1 %collective-permute-done.4.far_ref = bf16[80,128]{1,0:T(8,128)(2,1)S(1)} collective-permute-done((bf16[80,128]{1,0:T(8,128)(2,1)S(1)}, bf16[80,128]{1,0:T(8,128)(2,1)S(1)}, u32[]{:S(2)}, u32[]{:S(2)}) %collective-permute-start.4) | collective-permute-done | bytes 20512 | tf_op jit(solution)/shard_map/ppermute | solution.py:112
  87.2 2.9 %all-to-all-done.1 = bf16[16,128,128]{2,1,0:T(8,128)(2,1)S(1)} async-done(((bf16[16,128,128]{2,1,0:T(8,128)(2,1)}), bf16[16,128,128]{2,1,0:T(8,128)(2,1)S(1)}, u32[]{:S(2)}, u32[]{:S(2)}) %all-to-all-start.1) | async-done | bytes 524320 | tf_op jit(solution)/shard_map/all_to_all | solution.py:413
  90.0 12.3 %all-gather.2.cloned.1.call-done.weight_ref = bf16[2048,2432]{1,0:T(8,128)(2,1)} async-done(((bf16[128,2432]{1,0:T(8,128)(2,1)}), bf16[2048,2432]{1,0:T(8,128)(2,1)}) %all-gather.2.cloned.1.call-update) | async-done | bytes 9961488 | tf_op jit(solution)/shard_map/all_gather | solution.py:432
  102.3 0.0 copy-done.1
  102.3 0.0 copy-done.2
  102.3 0.0 copy-done.3
  102.3 0.0 copy-done.4
  102.3 10.4 %shard_map.186 = (f32[64,128]{1,0:T(8,128)}, bf16[128,2432]{1,0:T(8,128)(2,1)S(1)}, bf16[20,64,128]{2,1,0:T(8,128)(2,1)}, f32[8,128]{1,0:T(8,128)S(1)}) custom-call(s32[1]{0:T(128)} %bitcast.place_ref, s32[1,2]{1,0:T(1,128)S(1)} %copy-done.5, bf16[2048,128]{1,0:T(8,128)(2,1)S(1)} %bitcast.25, bf16[2048,2432]{1,0:T(8,128)(2,1)} %all-gather.2.cloned.1.call-done.weight_ref, ...), custom_call_target="tpu_custom_call" | custom-call | tf_op jit(solution)/shard_map/pallas_call | solution.py:304
  112.7 4.2 %all-to-all-start.2 = ((bf16[16,80,128]{2,1,0:T(8,128)(2,1)}), bf16[16,80,128]{2,1,0:T(8,128)(2,1)S(1)}, u32[]{:S(2)}, u32[]{:S(2)}) async-start(bf16[16,80,128]{2,1,0:T(8,128)(2,1)} %bitcast.14), calls=%async_computation.2 | async-start | bytes 655360 | tf_op jit(solution)/shard_map/all_to_all | solution.py:413
  117.0 7.7 %all-to-all-done.2 = bf16[16,80,128]{2,1,0:T(8,128)(2,1)S(1)} async-done(((bf16[16,80,128]{2,1,0:T(8,128)(2,1)}), bf16[16,80,128]{2,1,0:T(8,128)(2,1)S(1)}, u32[]{:S(2)}, u32[]{:S(2)}) %all-to-all-start.2) | async-done | bytes 327712 | tf_op jit(solution)/shard_map/all_to_all | solution.py:413
  124.7 0.1 shard_map.188
  124.7 14.5 %all_to_all.56 = bf16[8,80,128]{2,1,0:T(8,128)(2,1)S(1)} all-to-all(bf16[8,80,128]{2,1,0:T(8,128)(2,1)S(1)} %shard_map.188), channel_id=1, replica_groups={{0,16,32,48,64,80,96,112},{128,144,160,176,192,208,224,240},{256,272,28..., dimensions={0} | all-to-all | bytes 327680 | tf_op jit(solution)/shard_map/all_to_all | solution.py:413
  139.3 12.7 %all_to_all.57 = bf16[4,80,128]{2,1,0:T(8,128)(2,1)S(1)} all-to-all(bf16[4,80,128]{2,1,0:T(8,128)(2,1)S(1)} %shard_map.189), channel_id=1, replica_groups={{0,128,256,384},{16,144,272,400},{32,160,288,416},{48,176,304,432},{64,..., dimensions={0} | all-to-all | bytes 163840 | tf_op jit(solution)/shard_map/all_to_all | solution.py:413
  151.9 0.8 shard_map.190
  152.7 7.5 %all-to-all-start.5 = ((bf16[16,80,128]{2,1,0:T(8,128)(2,1)}), bf16[16,80,128]{2,1,0:T(8,128)(2,1)S(1)}, u32[]{:S(2)}, u32[]{:S(2)}) async-start(bf16[16,80,128]{2,1,0:T(8,128)(2,1)} %shard_map.190), calls=%async_computation.5 | async-start | bytes 655360 | tf_op jit(solution)/shard_map/all_to_all | solution.py:413
  160.2 3.8 %copy-done = bf16[2048,2432]{1,0:T(8,128)(2,1)S(1)} copy-done((bf16[2048,2432]{1,0:T(8,128)(2,1)S(1)}, bf16[2048,2432]{1,0:T(8,128)(2,1)}, u32[]{:S(2)}) %copy-start) | copy-done | bytes 9961496
  164.0 5.2 %shard_map.187 = bf16[128,2048]{1,0:T(8,128)(2,1)} custom-call(bf16[128,2432]{1,0:T(8,128)(2,1)S(1)} %get-tuple-element.23.grad_ref, bf16[2048,2432]{1,0:T(8,128)(2,1)S(1)} %copy-done), custom_call_target="tpu_custom_call" | custom-call | flops 1275068416 | bytes 9961472 | tf_op jit(solution)/shard_map/pallas_call | solution.py:345
  169.3 0.0 all-to-all-done.5
  169.3 0.9 shard_map.191
  170.2 0.5 slice.11
  (11 shorter events, 0.1 us)
Async XLA Ops:
  7.2 95.2 %all-gather.2.cloned.1.call-start = ((), (), s32[]{:S(2)}) async-start(), calls=%async_computation.6 | async-start | bytes 10584064 | tf_op jit(solution)/shard_map/all_gather | solution.py:432
  12.0 10.6 %copy-start.7 = (bf16[80,128]{1,0:T(8,128)(2,1)S(1)}, bf16[80,128]{1,0:T(8,128)(2,1)}, u32[]{:S(2)}) copy-start(bf16[80,128]{1,0:T(8,128)(2,1)} %get-tuple-element.17) | copy-start | bytes 61444
  12.0 27.9 %copy-start.8 = (f32[64]{0:T(128)S(1)}, f32[64]{0:T(128)}, u32[]{:S(2)}) copy-start(f32[64]{0:T(128)} %param.25) | copy-start | bytes 772
  12.0 27.9 %copy-start.9 = (f32[64]{0:T(128)S(1)}, f32[64]{0:T(128)}, u32[]{:S(2)}) copy-start(f32[64]{0:T(128)} %param.26) | copy-start | bytes 772
  12.0 46.2 %copy-start.5 = (s32[1,2]{1,0:T(1,128)S(1)}, s32[1,2]{1,0:T(1,128)}, u32[]{:S(2)}) copy-start(s32[1,2]{1,0:T(1,128)} %counts_ref.5) | copy-start | bytes 28
  12.0 46.2 %copy-start.6 = (s32[1,2]{1,0:T(1,128)S(1)}, s32[1,2]{1,0:T(1,128)}, u32[]{:S(2)}) copy-start(s32[1,2]{1,0:T(1,128)} %lengths_ref.1) | copy-start | bytes 28
  12.0 44.3 %all-to-all-start = ((bf16[16,416,128]{2,1,0:T(8,128)(2,1)}), bf16[16,416,128]{2,1,0:T(8,128)(2,1)S(1)}, u32[]{:S(2)}, u32[]{:S(2)}) async-start(bf16[16,416,128]{2,1,0:T(8,128)(2,1)} %bitcast.33), calls=%async_computation | async-start | bytes 3407872 | tf_op jit(solution)/shard_map/all_to_all | solution.py:413
  22.6 8.5 %collective-permute-start = (bf16[80,128]{1,0:T(8,128)(2,1)S(1)}, bf16[80,128]{1,0:T(8,128)(2,1)S(1)}, u32[]{:S(2)}, u32[]{:S(2)}) collective-permute-start(bf16[80,128]{1,0:T(8,128)(2,1)S(1)} %copy-done.7), channel_id=1, source_target_pairs={{0,64},{16,80},{32,96},{48,112},{64,0},{80,16},{96,32},{112,48},{1... | collective-permute-start | bytes 61448 | tf_op jit(solution)/shard_map/ppermute | solution.py:112
  31.1 5.9 %collective-permute-start.1 = (bf16[160,128]{1,0:T(8,128)(2,1)S(1)}, bf16[160,128]{1,0:T(8,128)(2,1)S(1)}, u32[]{:S(2)}, u32[]{:S(2)}) collective-permute-start(bf16[160,128]{1,0:T(8,128)(2,1)S(1)} %pad_maximum_fusion.3), channel_id=1, source_target_pairs={{0,32},{16,48},{32,0},{48,16},{64,96},{80,112},{96,64},{112,80},{1... | collective-permute-start | bytes 122888 | tf_op jit(solution)/shard_map/ppermute | solution.py:112
  37.0 5.6 %collective-permute-start.2 = (bf16[320,128]{1,0:T(8,128)(2,1)S(1)}, bf16[320,128]{1,0:T(8,128)(2,1)S(1)}, u32[]{:S(2)}, u32[]{:S(2)}) collective-permute-start(bf16[320,128]{1,0:T(8,128)(2,1)S(1)} %pad_maximum_fusion.2), channel_id=1, source_target_pairs={{0,16},{16,0},{32,48},{48,32},{64,80},{80,64},{96,112},{112,96},{1... | collective-permute-start | bytes 245768 | tf_op jit(solution)/shard_map/ppermute | solution.py:112
  56.3 12.3 %collective-permute-start.3 = (bf16[640,128]{1,0:T(8,128)(2,1)S(1)}, bf16[640,128]{1,0:T(8,128)(2,1)S(1)}, u32[]{:S(2)}, u32[]{:S(2)}) collective-permute-start(bf16[640,128]{1,0:T(8,128)(2,1)S(1)} %pad_maximum_fusion.1), channel_id=1, source_target_pairs={{0,128},{16,144},{32,160},{48,176},{64,192},{80,208},{96,224},{112... | collective-permute-start | bytes 491528 | tf_op jit(solution)/shard_map/ppermute | solution.py:112
  68.6 33.7 %copy-start.1 = (bf16[128,2432]{1,0:T(8,128)(2,1)S(1)}, bf16[128,2432]{1,0:T(8,128)(2,1)}, u32[]{:S(2)}) copy-start(bf16[128,2432]{1,0:T(8,128)(2,1)} %residual_ref.1) | copy-start | bytes 1867780
  68.6 33.7 %copy-start.2 = (bf16[2432,64]{0,1:T(8,128)(2,1)S(1)}, bf16[2432,64]{0,1:T(8,128)(2,1)}, u32[]{:S(2)}) copy-start(bf16[2432,64]{0,1:T(8,128)(2,1)} %param.30) | copy-start | bytes 933892
  68.6 33.7 %copy-start.3 = (f32[2,7296]{1,0:T(2,128)S(1)}, f32[2,7296]{1,0:T(2,128)}, u32[]{:S(2)}) copy-start(f32[2,7296]{1,0:T(2,128)} %modulate_ref.1) | copy-start | bytes 175108
  68.6 33.7 %copy-start.4 = (bf16[1,64,128]{2,1,0:T(8,128)(2,1)S(1)}, bf16[1,64,128]{2,1,0:T(8,128)(2,1)}, u32[]{:S(2)}) copy-start(bf16[1,64,128]{2,1,0:T(8,128)(2,1)} %param.31) | copy-start | bytes 49156
  68.7 21.4 %all-to-all-start.1 = ((bf16[16,128,128]{2,1,0:T(8,128)(2,1)}), bf16[16,128,128]{2,1,0:T(8,128)(2,1)S(1)}, u32[]{:S(2)}, u32[]{:S(2)}) async-start(bf16[16,128,128]{2,1,0:T(8,128)(2,1)} %bitcast.5), calls=%async_computation.1 | async-start | bytes 1048576 | tf_op jit(solution)/shard_map/all_to_all | solution.py:413
  74.1 13.0 %collective-permute-start.4 = (bf16[80,128]{1,0:T(8,128)(2,1)S(1)}, bf16[80,128]{1,0:T(8,128)(2,1)S(1)}, u32[]{:S(2)}, u32[]{:S(2)}) collective-permute-start(bf16[80,128]{1,0:T(8,128)(2,1)S(1)} %get-tuple-element.28), channel_id=1, source_target_pairs={{0,256},{16,272},{32,288},{48,304},{64,320},{80,336},{96,352},{112... | collective-permute-start | bytes 61448 | tf_op jit(solution)/shard_map/ppermute | solution.py:112
  112.7 11.9 %all-to-all-start.2 = ((bf16[16,80,128]{2,1,0:T(8,128)(2,1)}), bf16[16,80,128]{2,1,0:T(8,128)(2,1)S(1)}, u32[]{:S(2)}, u32[]{:S(2)}) async-start(bf16[16,80,128]{2,1,0:T(8,128)(2,1)} %bitcast.14), calls=%async_computation.2 | async-start | bytes 655360 | tf_op jit(solution)/shard_map/all_to_all | solution.py:413
  152.7 16.6 %all-to-all-start.5 = ((bf16[16,80,128]{2,1,0:T(8,128)(2,1)}), bf16[16,80,128]{2,1,0:T(8,128)(2,1)S(1)}, u32[]{:S(2)}, u32[]{:S(2)}) async-start(bf16[16,80,128]{2,1,0:T(8,128)(2,1)} %shard_map.190), calls=%async_computation.5 | async-start | bytes 655360 | tf_op jit(solution)/shard_map/all_to_all | solution.py:413
  160.2 3.8 %copy-start = (bf16[2048,2432]{1,0:T(8,128)(2,1)S(1)}, bf16[2048,2432]{1,0:T(8,128)(2,1)}, u32[]{:S(2)}) copy-start(bf16[2048,2432]{1,0:T(8,128)(2,1)} %all-gather.2.cloned.1.call-done.weight_ref) | copy-start | bytes 29884420
Sparse Core Ops, SparseCore 0:
  10.1 92.1 all-gather.1

commit v4 on v3

--- a/solution.py
+++ b/solution.py
@@ -103,13 +103,13 @@
         out_shape=jax.ShapeDtypeStruct((2, rows, LANES), held.dtype),
         in_specs=[SMEM, VMEM],
         out_specs=VMEM,
-        compiler_params=params(32),
+        compiler_params=params(16),
     )(lax.axis_index("dp").astype(jnp.int32).reshape(1), held)
     return chosen[0], swap(chosen[1], ranks, bit) if bit < ranks else jnp.zeros_like(chosen[1])
 
 
-def swap(array, ranks, step):
-    return lax.ppermute(array, "dp", [(rank, rank ^ step) for rank in range(ranks)])
+def swap(array, ranks, step, axis="dp"):
+    return lax.ppermute(array, axis, [(rank, rank ^ step) for rank in range(ranks)])
 
 
 def head_norm(rows, gain, same_head):
@@ -188,7 +188,11 @@
             sums.append(jnp.dot(weights, weigh_ref[image, head], preferred_element_type=jnp.float32))
         above = jnp.where(low, sums[0], sums[1])
         below = pltpu.roll(jnp.where(low, sums[1], sums[0]), HD, 1)
-        out_ref[pl.ds(start, Q_ROWS), :] = (above / below).astype(jnp.bfloat16)
+        result = (above / below).astype(jnp.bfloat16)
+        for part in range(Q_ROWS // tile):
+            at = start // tile + part
+            place = (lax.rem(at, per_image) * IMGS + lax.div(at, per_image)) * tile
+            out_ref[pl.ds(pl.multiple_of(place, tile), tile), :] = result[part * tile : (part + 1) * tile]
 
     @pl.loop(0, (border + Q_ROWS - 1) // Q_ROWS)
     def _(step):
@@ -215,7 +219,7 @@
             pltpu.VMEM((IMGS, keys, LANES), jnp.bfloat16),
             pltpu.VMEM((IMGS, 2, keys, LANES), jnp.bfloat16),
         ],
-        compiler_params=params(48),
+        compiler_params=params(32),
         cost_estimate=pl.CostEstimate(
             flops=16 * rows_all * keys * LANES,
             bytes_accessed=4 * rows_all * LANES * 4,
@@ -232,14 +236,26 @@
     return jnp.where(row == 0, high, rest).astype(jnp.bfloat16)
 
 
-def head_kernel(
-    steps, place_ref, counts_ref, rows_ref, weight_ref, residual_ref, modulate_ref, final_ref,
-    noise_ref, near_ref, far_ref, velocity_ref, grad_ref, parts_ref, total_ref, sum_ref,
-):
+def pick_rows(first, modulate_ref, at, width):
+    columns = pl.ds(at * width, width)
+    return jnp.where(first, modulate_ref[0:1, columns], modulate_ref[1:2, columns])
+
+
+def row_mean(array):
+    return jnp.sum(array, axis=-1, keepdims=True) * (1.0 / array.shape[1])
+
+
+def layout(place_ref, counts_ref, tile):
+    place = place_ref[0] * tile
+    border = (counts_ref[0, 0] + tile - 1) // tile * tile
+    first = place < border
+    return first, jnp.where(first, counts_ref[0, 0], border + counts_ref[0, 1]) - place
+
+
+def project_kernel(steps, half_ref, rows_ref, weight_ref, own_ref, other_ref, sum_ref):
     step = pl.program_id(0)
-    tile, width = residual_ref.shape
-    lat = final_ref.shape[0]
-    rows = jnp.concatenate([rows_ref[:tile, :], rows_ref[tile:, :]], axis=1)
+    tile = own_ref.shape[0]
+    rows = jnp.concatenate([rows_ref[: 2 * tile, :], rows_ref[2 * tile :, :]], axis=1)
     product = jnp.dot(rows, weight_ref[...], preferred_element_type=jnp.float32)
 
     @pl.when(step == 0)
@@ -252,112 +268,171 @@
 
     @pl.when(step == steps - 1)
     def _():
-        place = place_ref[0] * tile
-        border = (counts_ref[0, 0] + tile - 1) // tile * tile
-        first = place < border
-        used_rows = jnp.where(first, counts_ref[0, 0], border + counts_ref[0, 1]) - place
-        total = jnp.zeros((1, 1), jnp.float32)
-        for ref in (near_ref, far_ref):
-            note = ref[lat:, :].astype(jnp.float32)
-            total += note[1:2, 0:1] * 128.0 + note[2:3, 0:1]
-        total_ref[...] = jnp.broadcast_to(total, total_ref.shape)
-        pick = lambda at: jnp.where(
-            first,
-            modulate_ref[0:1, at * width : (at + 1) * width],
-            modulate_ref[1:2, at * width : (at + 1) * width],
-        )
-        gate, shift, scale = pick(0), pick(1), 1.0 + pick(2)
-        mean = lambda array: jnp.sum(array, axis=-1, keepdims=True) * (1.0 / width)
-        hidden = residual_ref[...].astype(jnp.float32) + gate * sum_ref[...]
-        centered = hidden - mean(hidden)
-        inverse = lax.rsqrt(mean(centered * centered) + EPSILON)
-        normed = centered * inverse
-        mixed = (normed * scale + shift).astype(jnp.bfloat16)
-        velocity = lax.dot_general(final_ref[...], mixed, NT, preferred_element_type=jnp.float32)
-        velocity_ref[...] = velocity
-        landed = near_ref[:lat, :].astype(jnp.float32) + far_ref[:lat, :].astype(jnp.float32)
-        target = noise_ref[...].astype(jnp.float32) - landed
-        used = lax.broadcasted_iota(jnp.int32, (lat, tile), 1) < used_rows
-        error = jnp.where(used, velocity - target, 0.0)
-        grad_wide = error * (2.0 / (total * lat))
-        grad_columns = grad_wide.astype(jnp.bfloat16)
-        final_part = jnp.dot(grad_columns, mixed, preferred_element_type=jnp.float32)
-        for at in range(width // LANES):
-            parts_ref[at] = final_part[:, at * LANES : (at + 1) * LANES].astype(jnp.bfloat16)
-        squares = jnp.sum(error * error, axis=(0, 1), keepdims=True)
-        parts_ref[width // LANES] = thirds(squares, lax.broadcasted_iota(jnp.int32, (lat, LANES), 0))
-        grad_rows = grad_wide.T.astype(jnp.bfloat16)
-        grad_normed = jnp.dot(grad_rows, final_ref[...], preferred_element_type=jnp.float32) * scale
-        grad_hidden = inverse * (
-            grad_normed - mean(grad_normed) - normed * mean(grad_normed * normed)
-        )
-        grad_ref[...] = (grad_hidden * gate).astype(jnp.bfloat16)
-
-
-def head(place, counts, recv, weight, residual, modulate, final_columns, noise, near, far):
-    tile, width = residual.shape
-    lat = final_columns.shape[0]
+        for half in range(2):
+
+            @pl.when(half_ref[0] == half)
+            def _():
+                own_ref[...] = sum_ref[half * tile : (half + 1) * tile, :]
+                other = sum_ref[(1 - half) * tile : (2 - half) * tile, :]
+                other_ref[...] = other.astype(jnp.bfloat16)
+
+
+def project(half, recv, weight, tile):
     depth = 2 * LANES
     steps = weight.shape[0] // depth
-    blocks = width // LANES + 1
-    whole = lambda array: pl.BlockSpec(array.shape, lambda i: (0,) * array.ndim)
-    return pl.pallas_call(
-        functools.partial(head_kernel, steps),
+    width = weight.shape[1]
+    return pl.pallas_call(
+        functools.partial(project_kernel, steps),
         grid=(steps,),
         out_shape=(
-            jax.ShapeDtypeStruct((lat, tile), jnp.float32),
+            jax.ShapeDtypeStruct((tile, width), jnp.float32),
             jax.ShapeDtypeStruct((tile, width), jnp.bfloat16),
-            jax.ShapeDtypeStruct((blocks, lat, LANES), jnp.bfloat16),
-            jax.ShapeDtypeStruct((8, LANES), jnp.float32),
         ),
         in_specs=[
             SMEM,
-            SMEM,
-            pl.BlockSpec((2 * tile, LANES), lambda i: (i, 0)),
+            pl.BlockSpec((4 * tile, LANES), lambda i: (i, 0)),
             pl.BlockSpec((depth, width), lambda i: (i, 0)),
-            whole(residual),
-            whole(modulate),
-            whole(final_columns),
-            whole(noise),
-            whole(near),
-            whole(far),
         ],
-        out_specs=(
-            pl.BlockSpec((lat, tile), lambda i: (0, 0)),
-            pl.BlockSpec((tile, width), lambda i: (0, 0)),
-            pl.BlockSpec((blocks, lat, LANES), lambda i: (0, 0, 0)),
-            pl.BlockSpec((8, LANES), lambda i: (0, 0)),
+        out_specs=(VMEM, VMEM),
+        scratch_shapes=[pltpu.VMEM((2 * tile, width), jnp.float32)],
+        compiler_params=params(52, ("arbitrary",)),
+    )(half, recv, weight)
+
+
+def head_kernel(
+    place_ref, counts_ref, own_ref, other_ref, residual_ref, modulate_ref, final_ref, noise_ref,
+    near_ref, far_ref, velocity_ref, parts_ref, total_ref, normed_ref, inverse_ref, grad_ref,
+):
+    tile, width = residual_ref.shape
+    lat = final_ref.shape[0]
+    first, used_rows = layout(place_ref, counts_ref, tile)
+    total = jnp.zeros((1, 1), jnp.float32)
+    for ref in (near_ref, far_ref):
+        note = ref[lat:, :].astype(jnp.float32)
+        total += note[1:2, 0:1] * 128.0 + note[2:3, 0:1]
+    total_ref[...] = jnp.broadcast_to(total, total_ref.shape)
+    gate, shift, scale = (pick_rows(first, modulate_ref, at, width) for at in range(3))
+    projected = own_ref[...] + other_ref[...].astype(jnp.float32)
+    hidden = residual_ref[...].astype(jnp.float32) + gate * projected
+    centered = hidden - row_mean(hidden)
+    inverse = lax.rsqrt(row_mean(centered * centered) + EPSILON)
+    normed = centered * inverse
+    normed_ref[...] = normed
+    inverse_ref[...] = jnp.broadcast_to(inverse, inverse_ref.shape)
+    mixed = (normed * (1.0 + scale) + shift).astype(jnp.bfloat16)
+    velocity = lax.dot_general(final_ref[...], mixed, NT, preferred_element_type=jnp.float32)
+    velocity_ref[...] = velocity
+    landed = near_ref[:lat, :].astype(jnp.float32) + far_ref[:lat, :].astype(jnp.float32)
+    target = noise_ref[...].astype(jnp.float32) - landed
+    used = lax.broadcasted_iota(jnp.int32, (lat, tile), 1) < used_rows
+    error = jnp.where(used, velocity - target, 0.0)
+    grad_wide = error * (2.0 / (total * lat))
+    grad_columns = grad_wide.astype(jnp.bfloat16)
+    grad_ref[...] = grad_wide
+    final_part = jnp.dot(grad_columns, mixed, preferred_element_type=jnp.float32)
+    for at in range(width // LANES):
+        parts_ref[at] = final_part[:, at * LANES : (at + 1) * LANES].astype(jnp.bfloat16)
+    squares = jnp.sum(error * error, axis=(0, 1), keepdims=True)
+    parts_ref[width // LANES] = thirds(squares, lax.broadcasted_iota(jnp.int32, (lat, LANES), 0))
+
+
+def head(place, counts, own, other, residual, modulate, final_columns, noise, near, far):
+    tile, width = residual.shape
+    lat = final_columns.shape[0]
+    blocks = width // LANES + 1
+    return pl.pallas_call(
+        head_kernel,
+        out_shape=(
+            jax.ShapeDtypeStruct((lat, tile), jnp.float32),
+            jax.ShapeDtypeStruct((blocks, lat, LANES), jnp.bfloat16),
+            jax.ShapeDtypeStruct((8, LANES), jnp.float32),
+            jax.ShapeDtypeStruct((tile, width), jnp.float32),
+            jax.ShapeDtypeStruct((tile, LANES), jnp.float32),
+            jax.ShapeDtypeStruct((lat, tile), jnp.float32),
         ),
-        scratch_shapes=[pltpu.VMEM((tile, width), jnp.float32)],
-        compiler_params=params(48, ("arbitrary",)),
-    )(place, counts, recv, weight, residual, modulate, final_columns, noise, near, far)
-
-
-def back_kernel(grad_ref, weight_ref, out_ref):
-    out_ref[...] = lax.dot_general(
-        grad_ref[...], weight_ref[...], NT, preferred_element_type=jnp.float32
-    ).astype(jnp.bfloat16)
-
-
-def back(grad, weight):
-    tile, width = grad.shape
+        in_specs=[SMEM] * 2 + [VMEM] * 8,
+        out_specs=(VMEM,) * 6,
+        compiler_params=params(20),
+    )(place, counts, own, other, residual, modulate, final_columns, noise, near, far)
+
+
+def grad_kernel(
+    place_ref, counts_ref, grad_columns_ref, normed_ref, inverse_ref, modulate_ref, final_ref, out_ref
+):
+    tile, width = normed_ref.shape
+    first, _ = layout(place_ref, counts_ref, tile)
+    gate, scale = (pick_rows(first, modulate_ref, at, width) for at in (0, 2))
+    normed = normed_ref[...]
+    grad_rows = grad_columns_ref[...].T.astype(jnp.bfloat16)
+    grad_mixed = jnp.dot(grad_rows, final_ref[...], preferred_element_type=jnp.float32)
+    grad_normed = grad_mixed * (1.0 + scale)
+    across = normed * row_mean(grad_normed * normed)
+    grad_hidden = inverse_ref[:, 0:1] * (grad_normed - row_mean(grad_normed) - across)
+    out_ref[...] = (grad_hidden * gate).astype(jnp.bfloat16)
+
+
+def grad_projected_of(place, counts, grad_columns, normed, inverse, modulate, final_columns):
+    return pl.pallas_call(
+        grad_kernel,
+        out_shape=jax.ShapeDtypeStruct(normed.shape, jnp.bfloat16),
+        in_specs=[SMEM] * 2 + [VMEM] * 5,
+        out_specs=VMEM,
+        compiler_params=params(20),
+    )(place, counts, grad_columns, normed, inverse, modulate, final_columns)
+
+
+def back_kernel(own_ref, other_ref, weight_ref, own_out_ref, other_out_ref, both_ref):
+    tile = own_ref.shape[0]
+
+    @pl.when(pl.program_id(0) == 0)
+    def _():
+        both_ref[:tile, :] = own_ref[...]
+        both_ref[tile:, :] = other_ref[...]
+
+    product = lax.dot_general(both_ref[...], weight_ref[...], NT, preferred_element_type=jnp.float32)
+    own_out_ref[...] = product[:tile].astype(jnp.bfloat16)
+    other_out_ref[...] = product[tile:].astype(jnp.bfloat16)
+
+
+def back(own, other, weight):
+    tile, width = own.shape
     depth = 2 * LANES
+    out = jax.ShapeDtypeStruct((tile, weight.shape[0]), jnp.bfloat16)
+    out_spec = pl.BlockSpec((tile, depth), lambda i: (0, i))
     return pl.pallas_call(
         back_kernel,
         grid=(weight.shape[0] // depth,),
-        out_shape=jax.ShapeDtypeStruct((tile, weight.shape[0]), jnp.bfloat16),
-        in_specs=[
-            pl.BlockSpec((tile, width), lambda i: (0, 0)),
-            pl.BlockSpec((depth, width), lambda i: (i, 0)),
-        ],
-        out_specs=pl.BlockSpec((tile, depth), lambda i: (0, i)),
-        compiler_params=params(32, ("arbitrary",)),
+        out_shape=(out, out),
+        in_specs=[VMEM, VMEM, pl.BlockSpec((depth, width), lambda i: (i, 0))],
+        out_specs=(out_spec, out_spec),
+        scratch_shapes=[pltpu.VMEM((2 * tile, width), jnp.bfloat16)],
+        compiler_params=params(24, ("arbitrary",)),
         cost_estimate=pl.CostEstimate(
-            flops=2 * tile * width * weight.shape[0],
+            flops=4 * tile * width * weight.shape[0],
             bytes_accessed=2 * width * weight.shape[0],
             transcendentals=0,
         ),
-    )(grad, weight)
+    )(own, other, weight)
+
+
+def join_kernel(half_ref, own_ref, other_ref, out_ref):
+    depth = own_ref.shape[1]
+    for half in range(2):
+
+        @pl.when(half_ref[0] == half)
+        def _():
+            out_ref[:, half * depth : (half + 1) * depth] = own_ref[...]
+            out_ref[:, (1 - half) * depth : (2 - half) * depth] = other_ref[...]
+
+
+def join(half, own, other):
+    return pl.pallas_call(
+        join_kernel,
+        out_shape=jax.ShapeDtypeStruct((own.shape[0], 2 * own.shape[1]), own.dtype),
+        in_specs=[SMEM, VMEM, VMEM],
+        out_specs=VMEM,
+        compiler_params=params(16),
+    )(half, own, other)
 
 
 def sum_kernel(ranks, loss_row, last_ref, recv_ref, out_ref):
@@ -382,7 +457,7 @@
         out_shape=jax.ShapeDtypeStruct((copies, rows, LANES), jnp.bfloat16),
         in_specs=[SMEM, VMEM],
         out_specs=VMEM,
-        compiler_params=params(32),
+        compiler_params=params(16),
     )(last, recv)
     return result.reshape(copies * rows, LANES)
 
@@ -405,7 +480,7 @@
         ),
         in_specs=[VMEM, VMEM],
         out_specs=(VMEM, VMEM),
-        compiler_params=params(32),
+        compiler_params=params(16),
     )(parts, total)
 
 
@@ -429,7 +504,12 @@
     far_groups = [[row * near + at for row in range(far)] for at in range(near)]
     column_index = lax.axis_index("seqt").astype(jnp.int32)
 
-    gathered = lax.all_gather(out_weight, "seqt", axis=0, tiled=True)
+    per_half = sources // 2
+    halves = [[half * per_half + at for at in range(per_half)] for half in range(2)]
+    place = column_index.reshape(1)
+    half = (column_index // per_half).reshape(1)
+
+    gathered = lax.all_gather(out_weight, "seqt", axis=0, axis_index_groups=halves, tiled=True)
     sent, tagged = pack(
         (queries, key_rows, values, text_keys, text_values), sources, latent_tiles, tile_route, image_tokens
     )
@@ -442,24 +522,34 @@
         recv, image_tokens, text_lengths, query_gain, key_gain, sources, tile, text_rows
     )
     heads, held = lax.optimization_barrier((heads, held))
-    attended = exchange(heads, "seqt")
+    attended = exchange(heads, "seqt", halves)
     mine, other = land(held, tagged.shape[0], ranks)
-    velocity, grad_projected, parts, total = head(
-        column_index.reshape(1), image_tokens, attended, gathered, residual, modulation,
-        final_weight.T, noise_tiles[0], mine, other,
-    )
-    attention_grad = back(grad_projected, gathered)
-
+    final_columns = final_weight.T
+    own, across = project(half, attended, gathered, tile)
+    across = swap(across, sources, per_half, "seqt")
+    velocity, parts, total, normed, inverse, grad_columns = head(
+        place, image_tokens, own, across, residual, modulation, final_columns, noise_tiles[0],
+        mine, other,
+    )
+    grad_projected = grad_projected_of(
+        place, image_tokens, grad_columns, normed, inverse, modulation, final_columns
+    )
     blocks = parts.shape[0]
     share = blocks * lat_width // sources
     loss_row = (blocks - 1) * lat_width - (sources - 1) * share
     last = (column_index == sources - 1).astype(jnp.int32).reshape(1)
     sums = exchange(parts.reshape(blocks * lat_width, LANES), "seqt")
+    sums, grad_projected = lax.optimization_barrier((sums, grad_projected))
+    partner_grad = swap(grad_projected, sources, per_half, "seqt")
     sums = exchange(sum_out(sums, sources, near, loss_row, last), "dp", near_groups)
+    sums, partner_grad = lax.optimization_barrier((sums, partner_grad))
+    own_grad, across_grad = back(grad_projected, partner_grad, gathered)
     sums = exchange(sum_out(sums, near, far, loss_row, last), "dp", far_groups)
+    sums, own_grad, across_grad = lax.optimization_barrier((sums, own_grad, across_grad))
+    attention_grad = join(half, own_grad, swap(across_grad, sources, per_half, "seqt"))
     sums = exchange(sum_out(sums, far, sources, loss_row, last), "seqt")
-    final_columns, loss = unpack(sums.reshape(blocks, lat_width, LANES), total, width)
-    return velocity[None], attention_grad, final_columns.T, loss[0, 0]
+    final_sums, loss = unpack(sums.reshape(blocks, lat_width, LANES), total, width)
+    return velocity[None], attention_grad, final_sums.T, loss[0, 0]
 
 
 def solution(mesh):

time: 179 us -> 182 us (1.017)
  starting transfers between devices: 45.2 us -> 58.9 us
  blocking collectives: 27.2 us -> 20.9 us
  waiting for transfers between devices: 54.5 us -> 50.7 us
  Pallas kernels: 31.3 us -> 29.4 us
    all_gather x1, waiting for transfers between devices: 12.3 us -> 0.01 us  [per_device(): lax.all_gather(out_weight, 'seqt', axis=0, axis_index_groups=halves, tile...]
    ppermute x5 -> x8, starting transfers between devices: 17.5 us -> 27.5 us  [swap(): lax.ppermute(array, axis, [(rank, rank ^ step) for rank in range(ranks)])]
    ppermute x5 -> x8, waiting for transfers between devices: 17.3 us -> 25.6 us  [swap(): lax.ppermute(array, axis, [(rank, rank ^ step) for rank in range(ranks)])]
    all_to_all x2 -> x1, blocking collectives: 27.2 us -> 20.9 us  [exchange(): lax.all_to_all(array, axis, split_axis=0, concat_axis=0, axis_index_group...]
    all_to_all x4 -> x5, starting transfers between devices: 27.6 us -> 31.3 us  [exchange(): lax.all_to_all(array, axis, split_axis=0, concat_axis=0, axis_index_group...]
    pallas_call x2 -> x5, Pallas kernels: 15.6 us -> 13.1 us  [the longest x1 6.16 us: project(): pl.pallas_call(functools.partial(project_kernel, steps), grid=(steps,), o...]
    unnamed x20 -> x26, local copies, waits for them, and re-layouts: 3.87 us -> 5.64 us
    all_to_all x4 -> x5, waiting for transfers between devices: 24.3 us -> 24.4 us  [exchange(): lax.all_to_all(array, axis, split_axis=0, concat_axis=0, axis_index_group...]
  transfers between devices with their start and end apart: 10 -> 14, of which waited for: 8 -> 9; matrix products, arithmetic and copies ran while one was open for 0% -> 0% of each run, Pallas kernels for 11% -> 10%
where the time goes in v4:
time: 182 us; the launch traced here: 181 us
  starting transfers between devices  58.9 us (32%)
  waiting for transfers between devices  50.7 us (28%)
  Pallas kernels  29.4 us (16%)
  blocking collectives  20.9 us (11%)
  between operations  14.9 us (8%)
  local copies, waits for them, and re-layouts  6.16 us (3%)
    all_to_all x5, starting transfers between devices, exchange(): lax.all_to_all(array, axis, split_axis=0, concat_axis=0, axis_index_group...  31.3 us
    ppermute x8, starting transfers between devices, swap(): lax.ppermute(array, axis, [(rank, rank ^ step) for rank in range(ranks)])  27.5 us
    ppermute x8, waiting for transfers between devices, swap(): lax.ppermute(array, axis, [(rank, rank ^ step) for rank in range(ranks)])  25.6 us
    all_to_all x5, waiting for transfers between devices, exchange(): lax.all_to_all(array, axis, split_axis=0, concat_axis=0, axis_index_group...  24.4 us
    all_to_all x1, blocking collectives, exchange(): lax.all_to_all(array, axis, split_axis=0, concat_axis=0, axis_index_group...  20.9 us
    pallas_call x1, Pallas kernels, attention(): pl.pallas_call(functools.partial(attention_kernel, sources, tile, text_ro...  10.4 us
    pallas_call x1, Pallas kernels, project(): pl.pallas_call(functools.partial(project_kernel, steps), grid=(steps,), o...  6.16 us
    unnamed x26, local copies, waits for them, and re-layouts  5.64 us
  transfers between devices with their start and end apart: 14, of which 9 were waited for; matrix products, arithmetic and copies ran while one was open for 0% of the time, Pallas kernels for 10%

profile of v4, /device:TPU:1, one launch (start us, length us, event | category | flops | bytes accessed | tf_op | source)
XLA Modules:
  0.0 181.1 jit_solution(4601249084745291531)
XLA Ops:
  7.2 0.0 all-gather.2.cloned.1.call-start
  7.2 0.7 all-gather.2.cloned.1.call-update
  8.5 3.5 %shard_map.183 = (bf16[6656,128]{1,0:T(8,128)(2,1)}, bf16[80,128]{1,0:T(8,128)(2,1)}) custom-call(s32[1]{0:T(128)S(6)} %copy.20.route_ref, s32[1,2]{1,0:T(1,128)} %counts_ref.7, bf16[1,64,128]{2,1,0:T(8,128)(2,1)} %tile_ref.1, bf16[128,2048]{1,0:T(8,128)(2,1)} %refs_0_.1, bf16[128,2048]{1,0:T(8,128)(2,1)} %refs_1_.1, bf16[128,2048]{1,0:T(8,128)(2,1)} %refs_2_.1, ...), custom_call_target="tpu_custom_call" | custom-call | tf_op jit(solution)/shard_map/pallas_call | solution.py:55
  12.0 0.0 copy-start.10
  12.0 0.0 copy-start.11
  12.0 0.0 copy-start.12
  12.1 0.0 copy-start.8
  12.1 10.5 %all-to-all-start = ((bf16[16,416,128]{2,1,0:T(8,128)(2,1)}), bf16[16,416,128]{2,1,0:T(8,128)(2,1)S(1)}, u32[]{:S(2)}, u32[]{:S(2)}) async-start(bf16[16,416,128]{2,1,0:T(8,128)(2,1)} %bitcast.35), calls=%async_computation | async-start | bytes 3407872 | tf_op jit(solution)/shard_map/all_to_all | solution.py:488
  22.6 7.1 %collective-permute-start = (bf16[80,128]{1,0:T(8,128)(2,1)S(1)}, bf16[80,128]{1,0:T(8,128)(2,1)S(1)}, u32[]{:S(2)}, u32[]{:S(2)}) collective-permute-start(bf16[80,128]{1,0:T(8,128)(2,1)S(1)} %copy-done.10), channel_id=1, source_target_pairs={{0,64},{16,80},{32,96},{48,112},{64,0},{80,16},{96,32},{112,48},{1... | collective-permute-start | bytes 61448 | tf_op jit(solution)/shard_map/ppermute | solution.py:112
  29.7 1.4 collective-permute-done
  31.1 3.8 %collective-permute-start.1 = (bf16[160,128]{1,0:T(8,128)(2,1)S(1)}, bf16[160,128]{1,0:T(8,128)(2,1)S(1)}, u32[]{:S(2)}, u32[]{:S(2)}) collective-permute-start(bf16[160,128]{1,0:T(8,128)(2,1)S(1)} %pad_maximum_fusion.3), channel_id=1, source_target_pairs={{0,32},{16,48},{32,0},{48,16},{64,96},{80,112},{96,64},{112,80},{1... | collective-permute-start | bytes 122888 | tf_op jit(solution)/shard_map/ppermute | solution.py:112
  34.9 2.2 %collective-permute-done.1 = bf16[160,128]{1,0:T(8,128)(2,1)S(1)} collective-permute-done((bf16[160,128]{1,0:T(8,128)(2,1)S(1)}, bf16[160,128]{1,0:T(8,128)(2,1)S(1)}, u32[]{:S(2)}, u32[]{:S(2)}) %collective-permute-start.1) | collective-permute-done | bytes 40992 | tf_op jit(solution)/shard_map/ppermute | solution.py:112
  37.1 2.8 %collective-permute-start.2 = (bf16[320,128]{1,0:T(8,128)(2,1)S(1)}, bf16[320,128]{1,0:T(8,128)(2,1)S(1)}, u32[]{:S(2)}, u32[]{:S(2)}) collective-permute-start(bf16[320,128]{1,0:T(8,128)(2,1)S(1)} %pad_maximum_fusion.2), channel_id=1, source_target_pairs={{0,16},{16,0},{32,48},{48,32},{64,80},{80,64},{96,112},{112,96},{1... | collective-permute-start | bytes 245768 | tf_op jit(solution)/shard_map/ppermute | solution.py:112
  39.9 0.1 maximum_bitcast_fusion
  40.0 2.6 %collective-permute-done.2 = bf16[320,128]{1,0:T(8,128)(2,1)S(1)} collective-permute-done((bf16[320,128]{1,0:T(8,128)(2,1)S(1)}, bf16[320,128]{1,0:T(8,128)(2,1)S(1)}, u32[]{:S(2)}, u32[]{:S(2)}) %collective-permute-start.2) | collective-permute-done | bytes 81952 | tf_op jit(solution)/shard_map/ppermute | solution.py:112
  42.6 6.3 %all-to-all-done = bf16[16,416,128]{2,1,0:T(8,128)(2,1)S(1)} async-done(((bf16[16,416,128]{2,1,0:T(8,128)(2,1)}), bf16[16,416,128]{2,1,0:T(8,128)(2,1)S(1)}, u32[]{:S(2)}, u32[]{:S(2)}) %all-to-all-start) | async-done | bytes 1703968 | tf_op jit(solution)/shard_map/all_to_all | solution.py:488
  48.9 1.9 %collective-permute-start.3 = (bf16[640,128]{1,0:T(8,128)(2,1)S(1)}, bf16[640,128]{1,0:T(8,128)(2,1)S(1)}, u32[]{:S(2)}, u32[]{:S(2)}) collective-permute-start(bf16[640,128]{1,0:T(8,128)(2,1)S(1)} %pad_maximum_fusion.1), channel_id=1, source_target_pairs={{0,128},{16,144},{32,160},{48,176},{64,192},{80,208},{96,224},{112... | collective-permute-start | bytes 491528 | tf_op jit(solution)/shard_map/ppermute | solution.py:112
  50.9 10.4 %shard_map.184 = bf16[2048,128]{1,0:T(8,128)(2,1)} custom-call(s32[1,2]{1,0:T(1,128)S(1)} %copy-done.8, s32[1,2]{1,0:T(1,128)S(1)} %copy-done.9, bf16[6656,128]{1,0:T(8,128)(2,1)S(1)} %bitcast.27, f32[1,128]{1,0:T(1,128)S(1)} %get-tuple-element.56.query_gain_ref, f32[1,128]{1,0:T(1,128)S(1)} %get-tuple-element.57.key_gain_ref), custom_call_target="tpu_custom_call" | custom-call | flops 4831838208 | bytes 4194304 | tf_op jit(solution)/shard_map/pallas_call | solution.py:210
  61.3 4.5 %all-to-all-start.1 = ((bf16[8,256,128]{2,1,0:T(8,128)(2,1)}), bf16[8,256,128]{2,1,0:T(8,128)(2,1)S(1)}, u32[]{:S(2)}, u32[]{:S(2)}) async-start(bf16[8,256,128]{2,1,0:T(8,128)(2,1)} %bitcast.6), calls=%async_computation.1 | async-start | bytes 1048576 | tf_op jit(solution)/shard_map/all_to_all | solution.py:488
  65.8 9.5 %all-to-all-done.1 = bf16[8,256,128]{2,1,0:T(8,128)(2,1)S(1)} async-done(((bf16[8,256,128]{2,1,0:T(8,128)(2,1)}), bf16[8,256,128]{2,1,0:T(8,128)(2,1)S(1)}, u32[]{:S(2)}, u32[]{:S(2)}) %all-to-all-start.1) | async-done | bytes 524320 | tf_op jit(solution)/shard_map/all_to_all | solution.py:488
  75.3 0.0 copy-start.7
  75.3 6.2 %shard_map.185 = (f32[128,2432]{1,0:T(8,128)}, bf16[128,2432]{1,0:T(8,128)(2,1)S(1)}) custom-call(s32[1]{0:T(128)} %bitcast.1.half_ref, bf16[2048,128]{1,0:T(8,128)(2,1)S(1)} %bitcast.26, bf16[1024,2432]{1,0:T(8,128)(2,1)} %all-gather.2.cloned.1.call-done.weight_ref), custom_call_target="tpu_custom_call" | custom-call | tf_op jit(solution)/shard_map/pallas_call | solution.py:284
  81.4 3.4 %collective-permute-start.4 = (bf16[128,2432]{1,0:T(8,128)(2,1)S(1)}, bf16[128,2432]{1,0:T(8,128)(2,1)S(1)}, u32[]{:S(2)}, u32[]{:S(2)}) collective-permute-start(bf16[128,2432]{1,0:T(8,128)(2,1)S(1)} %get-tuple-element.35), channel_id=1, source_target_pairs={{0,8},{1,9},{2,10},{3,11},{4,12},{5,13},{6,14},{7,15},{8,0},{9,1},... | collective-permute-start | bytes 1867784 | tf_op jit(solution)/shard_map/ppermute | solution.py:112
  84.9 0.1 shard_map.186
  85.0 2.5 %collective-permute-start.5 = (bf16[80,128]{1,0:T(8,128)(2,1)S(1)}, bf16[80,128]{1,0:T(8,128)(2,1)S(1)}, u32[]{:S(2)}, u32[]{:S(2)}) collective-permute-start(bf16[80,128]{1,0:T(8,128)(2,1)S(1)} %get-tuple-element.54), channel_id=1, source_target_pairs={{0,256},{16,272},{32,288},{48,304},{64,320},{80,336},{96,352},{112... | collective-permute-start | bytes 61448 | tf_op jit(solution)/shard_map/ppermute | solution.py:112
  87.5 11.3 %collective-permute-done.5.far_ref = bf16[80,128]{1,0:T(8,128)(2,1)S(1)} collective-permute-done((bf16[80,128]{1,0:T(8,128)(2,1)S(1)}, bf16[80,128]{1,0:T(8,128)(2,1)S(1)}, u32[]{:S(2)}, u32[]{:S(2)}) %collective-permute-start.5) | collective-permute-done | bytes 20512 | tf_op jit(solution)/shard_map/ppermute | solution.py:112
  98.7 0.8 copy-done.4
  99.6 1.3 copy-done.1
  100.9 1.1 copy-done.5
  102.0 2.5 %shard_map.187 = (f32[64,128]{1,0:T(8,128)}, bf16[20,64,128]{2,1,0:T(8,128)(2,1)}, f32[8,128]{1,0:T(8,128)S(1)}, f32[128,2432]{1,0:T(8,128)S(1)}, f32[128,128]{1,0:T(8,128)S(1)}, /*index=5*/f32[64,128]{1,0:T(8,128)S(1)}) custom-call(s32[1]{0:T(128)} %bitcast.place_ref, s32[1,2]{1,0:T(1,128)S(1)} %copy-done.8, f32[128,2432]{1,0:T(8,128)S(1)} %copy-done.1, ...), custom_call_target="tpu_custom_call" | custom-call | tf_op jit(solution)/shard_map/pallas_call | solution.py:343
  104.4 5.5 %all-to-all-start.2 = ((bf16[16,80,128]{2,1,0:T(8,128)(2,1)}), bf16[16,80,128]{2,1,0:T(8,128)(2,1)S(1)}, u32[]{:S(2)}, u32[]{:S(2)}) async-start(bf16[16,80,128]{2,1,0:T(8,128)(2,1)} %bitcast.15), calls=%async_computation.2 | async-start | bytes 655360 | tf_op jit(solution)/shard_map/all_to_all | solution.py:488
  109.9 1.3 shard_map.188.own_ref
  111.2 6.4 %all-to-all-done.2 = bf16[16,80,128]{2,1,0:T(8,128)(2,1)S(1)} async-done(((bf16[16,80,128]{2,1,0:T(8,128)(2,1)}), bf16[16,80,128]{2,1,0:T(8,128)(2,1)S(1)}, u32[]{:S(2)}, u32[]{:S(2)}) %all-to-all-start.2) | async-done | bytes 327712 | tf_op jit(solution)/shard_map/all_to_all | solution.py:488
  117.7 2.7 %collective-permute-start.6 = (bf16[128,2432]{1,0:T(8,128)(2,1)S(1)}, bf16[128,2432]{1,0:T(8,128)(2,1)S(1)}, u32[]{:S(2)}, u32[]{:S(2)}) collective-permute-start(bf16[128,2432]{1,0:T(8,128)(2,1)S(1)} %shard_map.188.own_ref), channel_id=1, source_target_pairs={{0,8},{1,9},{2,10},{3,11},{4,12},{5,13},{6,14},{7,15},{8,0},{9,1},... | collective-permute-start | bytes 1867784 | tf_op jit(solution)/shard_map/ppermute | solution.py:112
  120.4 0.1 shard_map.189
  120.5 20.9 %all_to_all.59 = bf16[8,80,128]{2,1,0:T(8,128)(2,1)S(1)} all-to-all(bf16[8,80,128]{2,1,0:T(8,128)(2,1)S(1)} %shard_map.189), channel_id=1, replica_groups={{0,16,32,48,64,80,96,112},{128,144,160,176,192,208,224,240},{256,272,28..., dimensions={0} | all-to-all | bytes 327680 | tf_op jit(solution)/shard_map/all_to_all | solution.py:488
  141.4 0.7 shard_map.190
  142.0 3.3 %all-to-all-start.4 = ((bf16[4,80,128]{2,1,0:T(8,128)(2,1)}), bf16[4,80,128]{2,1,0:T(8,128)(2,1)S(1)}, u32[]{:S(2)}, u32[]{:S(2)}) async-start(bf16[4,80,128]{2,1,0:T(8,128)(2,1)} %shard_map.190), calls=%async_computation.4 | async-start | bytes 163840 | tf_op jit(solution)/shard_map/all_to_all | solution.py:488
  145.3 2.4 %copy-done = bf16[1024,2432]{1,0:T(8,128)(2,1)S(1)} copy-done((bf16[1024,2432]{1,0:T(8,128)(2,1)S(1)}, bf16[1024,2432]{1,0:T(8,128)(2,1)}, u32[]{:S(2)}) %copy-start) | copy-done | bytes 4980760
  147.8 2.3 %shard_map.191 = (bf16[128,1024]{1,0:T(8,128)(2,1)S(1)}, bf16[128,1024]{1,0:T(8,128)(2,1)S(1)}) custom-call(bf16[128,2432]{1,0:T(8,128)(2,1)S(1)} %shard_map.188.own_ref, bf16[128,2432]{1,0:T(8,128)(2,1)S(1)} %collective-permute-done.6.other_ref, bf16[1024,2432]{1,0:T(8,128)(2,1)S(1)} %copy-done), custom_call_target="tpu_custom_call" | custom-call | flops 1275068416 | bytes 4980736 | tf_op jit(solution)/shard_map/pallas_call | solution.py:402
  150.1 2.2 %all-to-all-done.4 = bf16[4,80,128]{2,1,0:T(8,128)(2,1)S(1)} async-done(((bf16[4,80,128]{2,1,0:T(8,128)(2,1)}), bf16[4,80,128]{2,1,0:T(8,128)(2,1)S(1)}, u32[]{:S(2)}, u32[]{:S(2)}) %all-to-all-start.4) | async-done | bytes 81952 | tf_op jit(solution)/shard_map/all_to_all | solution.py:488
  152.3 0.8 shard_map.193
  153.0 7.5 %all-to-all-start.5 = ((bf16[16,80,128]{2,1,0:T(8,128)(2,1)}), bf16[16,80,128]{2,1,0:T(8,128)(2,1)S(1)}, u32[]{:S(2)}, u32[]{:S(2)}) async-start(bf16[16,80,128]{2,1,0:T(8,128)(2,1)} %shard_map.193), calls=%async_computation.5 | async-start | bytes 655360 | tf_op jit(solution)/shard_map/all_to_all | solution.py:488
  160.6 3.3 %collective-permute-start.7 = (bf16[128,1024]{1,0:T(8,128)(2,1)S(1)}, bf16[128,1024]{1,0:T(8,128)(2,1)S(1)}, u32[]{:S(2)}, u32[]{:S(2)}) collective-permute-start(bf16[128,1024]{1,0:T(8,128)(2,1)S(1)} %get-tuple-element.49), channel_id=1, source_target_pairs={{0,8},{1,9},{2,10},{3,11},{4,12},{5,13},{6,14},{7,15},{8,0},{9,1},... | collective-permute-start | bytes 786440 | tf_op jit(solution)/shard_map/ppermute | solution.py:112
  163.9 8.2 %collective-permute-done.7.other_ref = bf16[128,1024]{1,0:T(8,128)(2,1)S(1)} collective-permute-done((bf16[128,1024]{1,0:T(8,128)(2,1)S(1)}, bf16[128,1024]{1,0:T(8,128)(2,1)S(1)}, u32[]{:S(2)}, u32[]{:S(2)}) %collective-permute-start.7) | collective-permute-done | bytes 262176 | tf_op jit(solution)/shard_map/ppermute | solution.py:112
  172.1 0.8 shard_map.192
  172.9 0.9 shard_map.194
  173.8 0.5 slice.11
  (27 shorter events, 0.1 us)
Async XLA Ops:
  7.2 68.1 %all-gather.2.cloned.1.call-start = ((), (), s32[]{:S(2)}) async-start(), calls=%async_computation.6 | async-start | bytes 5603328 | tf_op jit(solution)/shard_map/all_gather | solution.py:512
  12.0 10.6 %copy-start.10 = (bf16[80,128]{1,0:T(8,128)(2,1)S(1)}, bf16[80,128]{1,0:T(8,128)(2,1)}, u32[]{:S(2)}) copy-start(bf16[80,128]{1,0:T(8,128)(2,1)} %get-tuple-element.30) | copy-start | bytes 61444
  12.0 27.9 %copy-start.11 = (f32[64]{0:T(128)S(1)}, f32[64]{0:T(128)}, u32[]{:S(2)}) copy-start(f32[64]{0:T(128)} %param.25) | copy-start | bytes 772
  12.0 27.9 %copy-start.12 = (f32[64]{0:T(128)S(1)}, f32[64]{0:T(128)}, u32[]{:S(2)}) copy-start(f32[64]{0:T(128)} %param.26) | copy-start | bytes 772
  12.1 38.8 %copy-start.8 = (s32[1,2]{1,0:T(1,128)S(1)}, s32[1,2]{1,0:T(1,128)}, u32[]{:S(2)}) copy-start(s32[1,2]{1,0:T(1,128)} %counts_ref.7) | copy-start | bytes 28
  12.1 38.8 %copy-start.9 = (s32[1,2]{1,0:T(1,128)S(1)}, s32[1,2]{1,0:T(1,128)}, u32[]{:S(2)}) copy-start(s32[1,2]{1,0:T(1,128)} %lengths_ref.1) | copy-start | bytes 28
  12.1 36.8 %all-to-all-start = ((bf16[16,416,128]{2,1,0:T(8,128)(2,1)}), bf16[16,416,128]{2,1,0:T(8,128)(2,1)S(1)}, u32[]{:S(2)}, u32[]{:S(2)}) async-start(bf16[16,416,128]{2,1,0:T(8,128)(2,1)} %bitcast.35), calls=%async_computation | async-start | bytes 3407872 | tf_op jit(solution)/shard_map/all_to_all | solution.py:488
  22.6 8.5 %collective-permute-start = (bf16[80,128]{1,0:T(8,128)(2,1)S(1)}, bf16[80,128]{1,0:T(8,128)(2,1)S(1)}, u32[]{:S(2)}, u32[]{:S(2)}) collective-permute-start(bf16[80,128]{1,0:T(8,128)(2,1)S(1)} %copy-done.10), channel_id=1, source_target_pairs={{0,64},{16,80},{32,96},{48,112},{64,0},{80,16},{96,32},{112,48},{1... | collective-permute-start | bytes 61448 | tf_op jit(solution)/shard_map/ppermute | solution.py:112
  31.1 5.9 %collective-permute-start.1 = (bf16[160,128]{1,0:T(8,128)(2,1)S(1)}, bf16[160,128]{1,0:T(8,128)(2,1)S(1)}, u32[]{:S(2)}, u32[]{:S(2)}) collective-permute-start(bf16[160,128]{1,0:T(8,128)(2,1)S(1)} %pad_maximum_fusion.3), channel_id=1, source_target_pairs={{0,32},{16,48},{32,0},{48,16},{64,96},{80,112},{96,64},{112,80},{1... | collective-permute-start | bytes 122888 | tf_op jit(solution)/shard_map/ppermute | solution.py:112
  37.1 5.6 %collective-permute-start.2 = (bf16[320,128]{1,0:T(8,128)(2,1)S(1)}, bf16[320,128]{1,0:T(8,128)(2,1)S(1)}, u32[]{:S(2)}, u32[]{:S(2)}) collective-permute-start(bf16[320,128]{1,0:T(8,128)(2,1)S(1)} %pad_maximum_fusion.2), channel_id=1, source_target_pairs={{0,16},{16,0},{32,48},{48,32},{64,80},{80,64},{96,112},{112,96},{1... | collective-permute-start | bytes 245768 | tf_op jit(solution)/shard_map/ppermute | solution.py:112
  48.9 12.4 %collective-permute-start.3 = (bf16[640,128]{1,0:T(8,128)(2,1)S(1)}, bf16[640,128]{1,0:T(8,128)(2,1)S(1)}, u32[]{:S(2)}, u32[]{:S(2)}) collective-permute-start(bf16[640,128]{1,0:T(8,128)(2,1)S(1)} %pad_maximum_fusion.1), channel_id=1, source_target_pairs={{0,128},{16,144},{32,160},{48,176},{64,192},{80,208},{96,224},{112... | collective-permute-start | bytes 491528 | tf_op jit(solution)/shard_map/ppermute | solution.py:112
  61.3 13.9 %all-to-all-start.1 = ((bf16[8,256,128]{2,1,0:T(8,128)(2,1)}), bf16[8,256,128]{2,1,0:T(8,128)(2,1)S(1)}, u32[]{:S(2)}, u32[]{:S(2)}) async-start(bf16[8,256,128]{2,1,0:T(8,128)(2,1)} %bitcast.6), calls=%async_computation.1 | async-start | bytes 1048576 | tf_op jit(solution)/shard_map/all_to_all | solution.py:488
  75.3 24.3 %copy-start.2 = (bf16[2432,64]{0,1:T(8,128)(2,1)S(1)}, bf16[2432,64]{0,1:T(8,128)(2,1)}, u32[]{:S(2)}) copy-start(bf16[2432,64]{0,1:T(8,128)(2,1)} %param.30) | copy-start | bytes 933892
  75.3 24.3 %copy-start.3 = (bf16[128,2432]{1,0:T(8,128)(2,1)S(1)}, bf16[128,2432]{1,0:T(8,128)(2,1)}, u32[]{:S(2)}) copy-start(bf16[128,2432]{1,0:T(8,128)(2,1)} %residual_ref.1) | copy-start | bytes 1867780
  75.3 24.3 %copy-start.6 = (f32[2,7296]{1,0:T(2,128)S(1)}, f32[2,7296]{1,0:T(2,128)}, u32[]{:S(2)}) copy-start(f32[2,7296]{1,0:T(2,128)} %modulate_ref.3) | copy-start | bytes 175108
  75.3 24.3 %copy-start.7 = (bf16[1,64,128]{2,1,0:T(8,128)(2,1)S(1)}, bf16[1,64,128]{2,1,0:T(8,128)(2,1)}, u32[]{:S(2)}) copy-start(bf16[1,64,128]{2,1,0:T(8,128)(2,1)} %param.31) | copy-start | bytes 49156
  81.4 17.3 %collective-permute-start.4 = (bf16[128,2432]{1,0:T(8,128)(2,1)S(1)}, bf16[128,2432]{1,0:T(8,128)(2,1)S(1)}, u32[]{:S(2)}, u32[]{:S(2)}) collective-permute-start(bf16[128,2432]{1,0:T(8,128)(2,1)S(1)} %get-tuple-element.35), channel_id=1, source_target_pairs={{0,8},{1,9},{2,10},{3,11},{4,12},{5,13},{6,14},{7,15},{8,0},{9,1},... | collective-permute-start | bytes 1867784 | tf_op jit(solution)/shard_map/ppermute | solution.py:112
  85.0 13.7 %collective-permute-start.5 = (bf16[80,128]{1,0:T(8,128)(2,1)S(1)}, bf16[80,128]{1,0:T(8,128)(2,1)S(1)}, u32[]{:S(2)}, u32[]{:S(2)}) collective-permute-start(bf16[80,128]{1,0:T(8,128)(2,1)S(1)} %get-tuple-element.54), channel_id=1, source_target_pairs={{0,256},{16,272},{32,288},{48,304},{64,320},{80,336},{96,352},{112... | collective-permute-start | bytes 61448 | tf_op jit(solution)/shard_map/ppermute | solution.py:112
  98.7 0.8 copy-start.4
  99.6 1.3 copy-start.1
  100.9 1.1 copy-start.5
  104.4 13.3 %all-to-all-start.2 = ((bf16[16,80,128]{2,1,0:T(8,128)(2,1)}), bf16[16,80,128]{2,1,0:T(8,128)(2,1)S(1)}, u32[]{:S(2)}, u32[]{:S(2)}) async-start(bf16[16,80,128]{2,1,0:T(8,128)(2,1)} %bitcast.15), calls=%async_computation.2 | async-start | bytes 655360 | tf_op jit(solution)/shard_map/all_to_all | solution.py:488
  117.7 23.7 %collective-permute-start.6 = (bf16[128,2432]{1,0:T(8,128)(2,1)S(1)}, bf16[128,2432]{1,0:T(8,128)(2,1)S(1)}, u32[]{:S(2)}, u32[]{:S(2)}) collective-permute-start(bf16[128,2432]{1,0:T(8,128)(2,1)S(1)} %shard_map.188.own_ref), channel_id=1, source_target_pairs={{0,8},{1,9},{2,10},{3,11},{4,12},{5,13},{6,14},{7,15},{8,0},{9,1},... | collective-permute-start | bytes 1867784 | tf_op jit(solution)/shard_map/ppermute | solution.py:112
  142.0 10.2 %all-to-all-start.4 = ((bf16[4,80,128]{2,1,0:T(8,128)(2,1)}), bf16[4,80,128]{2,1,0:T(8,128)(2,1)S(1)}, u32[]{:S(2)}, u32[]{:S(2)}) async-start(bf16[4,80,128]{2,1,0:T(8,128)(2,1)} %shard_map.190), calls=%async_computation.4 | async-start | bytes 163840 | tf_op jit(solution)/shard_map/all_to_all | solution.py:488
  145.3 2.4 %copy-start = (bf16[1024,2432]{1,0:T(8,128)(2,1)S(1)}, bf16[1024,2432]{1,0:T(8,128)(2,1)}, u32[]{:S(2)}) copy-start(bf16[1024,2432]{1,0:T(8,128)(2,1)} %all-gather.2.cloned.1.call-done.weight_ref) | copy-start | bytes 14942212
  153.0 19.9 %all-to-all-start.5 = ((bf16[16,80,128]{2,1,0:T(8,128)(2,1)}), bf16[16,80,128]{2,1,0:T(8,128)(2,1)S(1)}, u32[]{:S(2)}, u32[]{:S(2)}) async-start(bf16[16,80,128]{2,1,0:T(8,128)(2,1)} %shard_map.193), calls=%async_computation.5 | async-start | bytes 655360 | tf_op jit(solution)/shard_map/all_to_all | solution.py:488
  160.6 11.5 %collective-permute-start.7 = (bf16[128,1024]{1,0:T(8,128)(2,1)S(1)}, bf16[128,1024]{1,0:T(8,128)(2,1)S(1)}, u32[]{:S(2)}, u32[]{:S(2)}) collective-permute-start(bf16[128,1024]{1,0:T(8,128)(2,1)S(1)} %get-tuple-element.49), channel_id=1, source_target_pairs={{0,8},{1,9},{2,10},{3,11},{4,12},{5,13},{6,14},{7,15},{8,0},{9,1},... | collective-permute-start | bytes 786440 | tf_op jit(solution)/shard_map/ppermute | solution.py:112
Sparse Core Ops, SparseCore 0:
  10.1 56.8 all-gather.1

commit v5 on v4

--- a/solution.py
+++ b/solution.py
@@ -26,21 +26,28 @@
 
 
 def pack_kernel(parts, count, route_ref, counts_ref, tile_ref, *refs):
-    ins, out_ref, tagged_ref, semaphore = refs[:count], refs[count], refs[count + 1], refs[count + 2]
+    ins, (out_ref, tagged_ref, lined_ref, in_semaphores, out_semaphore) = refs[:count], refs[count:]
     block_rows = sum(ref.shape[0] for ref in ins)
     for part in range(parts):
         row = part * block_rows
         for ref in ins:
             rows = ref.shape[0]
             pltpu.make_async_copy(
-                ref.at[:, pl.ds(part * LANES, LANES)], out_ref.at[pl.ds(row, rows), :], semaphore
+                ref.at[:, pl.ds(part * LANES, LANES)],
+                lined_ref.at[pl.ds(row, rows), :],
+                in_semaphores.at[part],
             ).start()
             row += rows
     lat = tile_ref.shape[1]
     tokens = counts_ref[0, 0] + counts_ref[0, 1]
     tagged_ref[:lat, :] = tile_ref[0]
     tagged_ref[lat:, :] = notes(route_ref[0], tokens // 16, tokens % 16)
-    pltpu.make_async_copy(out_ref, out_ref, semaphore).wait()
+    for part in range(parts):
+        here = lined_ref.at[pl.ds(part * block_rows, block_rows), :]
+        pltpu.make_async_copy(here, here, in_semaphores.at[part]).wait()
+        there = out_ref.at[pl.ds(part * block_rows, block_rows), :]
+        pltpu.make_async_copy(here, there, out_semaphore).start()
+    pltpu.make_async_copy(lined_ref, out_ref, out_semaphore).wait()
 
 
 def notes(first, second, third):
@@ -59,8 +66,12 @@
             jax.ShapeDtypeStruct((tile.shape[1] + NOTES, LANES), tile.dtype),
         ),
         in_specs=[SMEM, SMEM, VMEM] + [HBM] * len(arrays),
-        out_specs=(VMEM, VMEM),
-        scratch_shapes=[pltpu.SemaphoreType.DMA],
+        out_specs=(HBM, VMEM),
+        scratch_shapes=[
+            pltpu.VMEM((parts * block_rows, LANES), arrays[0].dtype),
+            pltpu.SemaphoreType.DMA((parts,)),
+            pltpu.SemaphoreType.DMA,
+        ],
         compiler_params=params(60),
     )(route, counts, tile, *arrays)
 
@@ -252,49 +263,35 @@
     return first, jnp.where(first, counts_ref[0, 0], border + counts_ref[0, 1]) - place
 
 
-def project_kernel(steps, half_ref, rows_ref, weight_ref, own_ref, other_ref, sum_ref):
-    step = pl.program_id(0)
+def project_kernel(half_ref, rows_ref, weight_ref, own_ref, other_ref, lined_ref):
     tile = own_ref.shape[0]
-    rows = jnp.concatenate([rows_ref[: 2 * tile, :], rows_ref[2 * tile :, :]], axis=1)
-    product = jnp.dot(rows, weight_ref[...], preferred_element_type=jnp.float32)
-
-    @pl.when(step == 0)
+
+    @pl.when(pl.program_id(0) == 0)
     def _():
-        sum_ref[...] = product
-
-    @pl.when(step > 0)
-    def _():
-        sum_ref[...] += product
-
-    @pl.when(step == steps - 1)
-    def _():
-        for half in range(2):
-
-            @pl.when(half_ref[0] == half)
-            def _():
-                own_ref[...] = sum_ref[half * tile : (half + 1) * tile, :]
-                other = sum_ref[(1 - half) * tile : (2 - half) * tile, :]
-                other_ref[...] = other.astype(jnp.bfloat16)
+        for at in range(lined_ref.shape[1] // LANES):
+            rows = rows_ref[at * 2 * tile : (at + 1) * 2 * tile, :]
+            lined_ref[:, at * LANES : (at + 1) * LANES] = rows
+
+    product = jnp.dot(lined_ref[...], weight_ref[...], preferred_element_type=jnp.float32)
+    first = half_ref[0] == 0
+    own_ref[...] = jnp.where(first, product[:tile], product[tile:])
+    other_ref[...] = jnp.where(first, product[tile:], product[:tile]).astype(jnp.bfloat16)
 
 
 def project(half, recv, weight, tile):
-    depth = 2 * LANES
-    steps = weight.shape[0] // depth
-    width = weight.shape[1]
-    return pl.pallas_call(
-        functools.partial(project_kernel, steps),
-        grid=(steps,),
+    depth, width = weight.shape
+    block = 4 * LANES
+    out_spec = pl.BlockSpec((tile, block), lambda i: (0, i))
+    return pl.pallas_call(
+        project_kernel,
+        grid=(pl.cdiv(width, block),),
         out_shape=(
             jax.ShapeDtypeStruct((tile, width), jnp.float32),
             jax.ShapeDtypeStruct((tile, width), jnp.bfloat16),
         ),
-        in_specs=[
-            SMEM,
-            pl.BlockSpec((4 * tile, LANES), lambda i: (i, 0)),
-            pl.BlockSpec((depth, width), lambda i: (i, 0)),
-        ],
-        out_specs=(VMEM, VMEM),
-        scratch_shapes=[pltpu.VMEM((2 * tile, width), jnp.float32)],
+        in_specs=[SMEM, VMEM, pl.BlockSpec((depth, block), lambda i: (0, i))],
+        out_specs=(out_spec, out_spec),
+        scratch_shapes=[pltpu.VMEM((2 * tile, depth), jnp.bfloat16)],
         compiler_params=params(52, ("arbitrary",)),
     )(half, recv, weight)
 
@@ -302,7 +299,14 @@
 def head_kernel(
     place_ref, counts_ref, own_ref, other_ref, residual_ref, modulate_ref, final_ref, noise_ref,
     near_ref, far_ref, velocity_ref, parts_ref, total_ref, normed_ref, inverse_ref, grad_ref,
+    own_here, other_here, semaphores,
 ):
+    copies = [
+        pltpu.make_async_copy(own_ref, own_here, semaphores.at[0]),
+        pltpu.make_async_copy(other_ref, other_here, semaphores.at[1]),
+    ]
+    for copy in copies:
+        copy.start()
     tile, width = residual_ref.shape
     lat = final_ref.shape[0]
     first, used_rows = layout(place_ref, counts_ref, tile)
@@ -312,7 +316,9 @@
         total += note[1:2, 0:1] * 128.0 + note[2:3, 0:1]
     total_ref[...] = jnp.broadcast_to(total, total_ref.shape)
     gate, shift, scale = (pick_rows(first, modulate_ref, at, width) for at in range(3))
-    projected = own_ref[...] + other_ref[...].astype(jnp.float32)
+    for copy in copies:
+        copy.wait()
+    projected = own_here[...] + other_here[...].astype(jnp.float32)
     hidden = residual_ref[...].astype(jnp.float32) + gate * projected
     centered = hidden - row_mean(hidden)
     inverse = lax.rsqrt(row_mean(centered * centered) + EPSILON)
@@ -350,9 +356,14 @@
             jax.ShapeDtypeStruct((tile, LANES), jnp.float32),
             jax.ShapeDtypeStruct((lat, tile), jnp.float32),
         ),
-        in_specs=[SMEM] * 2 + [VMEM] * 8,
+        in_specs=[SMEM] * 2 + [HBM] * 2 + [VMEM] * 6,
         out_specs=(VMEM,) * 6,
-        compiler_params=params(20),
+        scratch_shapes=[
+            pltpu.VMEM(own.shape, own.dtype),
+            pltpu.VMEM(other.shape, other.dtype),
+            pltpu.SemaphoreType.DMA((2,)),
+        ],
+        compiler_params=params(52),
     )(place, counts, own, other, residual, modulate, final_columns, noise, near, far)
 
 
@@ -524,6 +535,7 @@
     heads, held = lax.optimization_barrier((heads, held))
     attended = exchange(heads, "seqt", halves)
     mine, other = land(held, tagged.shape[0], ranks)
+    attended, mine, other = lax.optimization_barrier((attended, mine, other))
     final_columns = final_weight.T
     own, across = project(half, attended, gathered, tile)
     across = swap(across, sources, per_half, "seqt")
@@ -538,16 +550,17 @@
     share = blocks * lat_width // sources
     loss_row = (blocks - 1) * lat_width - (sources - 1) * share
     last = (column_index == sources - 1).astype(jnp.int32).reshape(1)
+    partner_grad = swap(grad_projected, sources, per_half, "seqt")
+    own_grad, across_grad = back(grad_projected, partner_grad, gathered)
+    swapped_grad = swap(across_grad, sources, per_half, "seqt")
     sums = exchange(parts.reshape(blocks * lat_width, LANES), "seqt")
-    sums, grad_projected = lax.optimization_barrier((sums, grad_projected))
-    partner_grad = swap(grad_projected, sources, per_half, "seqt")
+    sums, _ = lax.optimization_barrier((sums, grad_projected))
     sums = exchange(sum_out(sums, sources, near, loss_row, last), "dp", near_groups)
-    sums, partner_grad = lax.optimization_barrier((sums, partner_grad))
-    own_grad, across_grad = back(grad_projected, partner_grad, gathered)
+    sums, _ = lax.optimization_barrier((sums, partner_grad))
     sums = exchange(sum_out(sums, near, far, loss_row, last), "dp", far_groups)
-    sums, own_grad, across_grad = lax.optimization_barrier((sums, own_grad, across_grad))
-    attention_grad = join(half, own_grad, swap(across_grad, sources, per_half, "seqt"))
+    sums, _ = lax.optimization_barrier((sums, across_grad))
     sums = exchange(sum_out(sums, far, sources, loss_row, last), "seqt")
+    attention_grad = join(half, own_grad, swapped_grad)
     final_sums, loss = unpack(sums.reshape(blocks, lat_width, LANES), total, width)
     return velocity[None], attention_grad, final_sums.T, loss[0, 0]
 

time: 182 us -> 178 us (0.978)
  blocking collectives: 20.9 us -> 0 us
  starting transfers between devices: 58.9 us -> 73.9 us
  Pallas kernels: 29.4 us -> 31.6 us
  local copies, waits for them, and re-layouts: 6.16 us -> 4.26 us
    all_to_all x1 -> x0, blocking collectives: 20.9 us -> none  [exchange(): lax.all_to_all(array, axis, split_axis=0, concat_axis=0, axis_index_group...]
    all_to_all x5 -> x6, starting transfers between devices: 31.3 us -> 44.1 us  [exchange(): lax.all_to_all(array, axis, split_axis=0, concat_axis=0, axis_index_group...]
    ppermute x8, waiting for transfers between devices: 25.6 us -> 33.1 us  [swap(): lax.ppermute(array, axis, [(rank, rank ^ step) for rank in range(ranks)])]
    all_to_all x5 -> x6, waiting for transfers between devices: 24.4 us -> 18.5 us  [exchange(): lax.all_to_all(array, axis, split_axis=0, concat_axis=0, axis_index_group...]
    ppermute x8, starting transfers between devices: 27.5 us -> 29.7 us  [swap(): lax.ppermute(array, axis, [(rank, rank ^ step) for rank in range(ranks)])]
    pallas_call x1, Pallas kernels: 2.45 us -> 4.7 us  [head(): pl.pallas_call(head_kernel, out_shape=(jax.ShapeDtypeStruct((lat, tile),...]
    unnamed x26 -> x20, local copies, waits for them, and re-layouts: 5.64 us -> 3.74 us
  transfers between devices with their start and end apart: 14 -> 15, of which waited for: 9 -> 13; matrix products, arithmetic and copies ran while one was open for 0% -> 0% of each run, Pallas kernels for 10% -> 10%
where the time goes in v5:
time: 178 us; the launch traced here: 177 us
  starting transfers between devices  73.9 us (42%)
  waiting for transfers between devices  52.3 us (29%)
  Pallas kernels  31.6 us (18%)
  between operations  14.9 us (8%)
  local copies, waits for them, and re-layouts  4.26 us (2%)
    all_to_all x6, starting transfers between devices, exchange(): lax.all_to_all(array, axis, split_axis=0, concat_axis=0, axis_index_group...  44.1 us
    ppermute x8, waiting for transfers between devices, swap(): lax.ppermute(array, axis, [(rank, rank ^ step) for rank in range(ranks)])  33.1 us
    ppermute x8, starting transfers between devices, swap(): lax.ppermute(array, axis, [(rank, rank ^ step) for rank in range(ranks)])  29.7 us
    all_to_all x6, waiting for transfers between devices, exchange(): lax.all_to_all(array, axis, split_axis=0, concat_axis=0, axis_index_group...  18.5 us
    pallas_call x1, Pallas kernels, attention(): pl.pallas_call(functools.partial(attention_kernel, sources, tile, text_ro...  9.57 us
    pallas_call x1, Pallas kernels, project(): pl.pallas_call(project_kernel, grid=(pl.cdiv(width, block),), out_shape=(...  6.05 us
    pallas_call x1, Pallas kernels, head(): pl.pallas_call(head_kernel, out_shape=(jax.ShapeDtypeStruct((lat, tile),...  4.7 us
    unnamed x20, local copies, waits for them, and re-layouts  3.74 us
  transfers between devices with their start and end apart: 15, of which 13 were waited for; matrix products, arithmetic and copies ran while one was open for 0% of the time, Pallas kernels for 10%

profile of v5, /device:TPU:1, one launch (start us, length us, event | category | flops | bytes accessed | tf_op | source)
XLA Modules:
  0.0 177.2 jit_solution(4675010128435324357)
XLA Ops:
  7.2 0.0 all-gather.2.cloned.1.call-start
  7.2 0.7 all-gather.2.cloned.1.call-update
  8.5 3.6 %shard_map.183 = (bf16[6656,128]{1,0:T(8,128)(2,1)}, bf16[80,128]{1,0:T(8,128)(2,1)}) custom-call(s32[1]{0:T(128)S(6)} %copy.20.route_ref, s32[1,2]{1,0:T(1,128)} %counts_ref.7, bf16[1,64,128]{2,1,0:T(8,128)(2,1)} %tile_ref.1, bf16[128,2048]{1,0:T(8,128)(2,1)} %refs_0_.1, bf16[128,2048]{1,0:T(8,128)(2,1)} %refs_1_.1, bf16[128,2048]{1,0:T(8,128)(2,1)} %refs_2_.1, ...), custom_call_target="tpu_custom_call" | custom-call | tf_op jit(solution)/shard_map/pallas_call | solution.py:62
  12.2 0.0 copy-start.7
  12.2 0.0 copy-start.8
  12.2 0.0 copy-start.5
  12.3 10.5 %all-to-all-start = ((bf16[16,416,128]{2,1,0:T(8,128)(2,1)}), bf16[16,416,128]{2,1,0:T(8,128)(2,1)S(1)}, u32[]{:S(2)}, u32[]{:S(2)}) async-start(bf16[16,416,128]{2,1,0:T(8,128)(2,1)} %bitcast.35), calls=%async_computation | async-start | bytes 3407872 | tf_op jit(solution)/shard_map/all_to_all | solution.py:499
  22.8 7.1 %collective-permute-start = (bf16[80,128]{1,0:T(8,128)(2,1)S(1)}, bf16[80,128]{1,0:T(8,128)(2,1)S(1)}, u32[]{:S(2)}, u32[]{:S(2)}) collective-permute-start(bf16[80,128]{1,0:T(8,128)(2,1)S(1)} %copy-done.7), channel_id=1, source_target_pairs={{0,64},{16,80},{32,96},{48,112},{64,0},{80,16},{96,32},{112,48},{1... | collective-permute-start | bytes 61448 | tf_op jit(solution)/shard_map/ppermute | solution.py:123
  29.9 1.4 collective-permute-done
  31.3 3.8 %collective-permute-start.1 = (bf16[160,128]{1,0:T(8,128)(2,1)S(1)}, bf16[160,128]{1,0:T(8,128)(2,1)S(1)}, u32[]{:S(2)}, u32[]{:S(2)}) collective-permute-start(bf16[160,128]{1,0:T(8,128)(2,1)S(1)} %pad_maximum_fusion.3), channel_id=1, source_target_pairs={{0,32},{16,48},{32,0},{48,16},{64,96},{80,112},{96,64},{112,80},{1... | collective-permute-start | bytes 122888 | tf_op jit(solution)/shard_map/ppermute | solution.py:123
  35.1 2.2 %collective-permute-done.1 = bf16[160,128]{1,0:T(8,128)(2,1)S(1)} collective-permute-done((bf16[160,128]{1,0:T(8,128)(2,1)S(1)}, bf16[160,128]{1,0:T(8,128)(2,1)S(1)}, u32[]{:S(2)}, u32[]{:S(2)}) %collective-permute-start.1) | collective-permute-done | bytes 40992 | tf_op jit(solution)/shard_map/ppermute | solution.py:123
  37.2 2.8 %collective-permute-start.2 = (bf16[320,128]{1,0:T(8,128)(2,1)S(1)}, bf16[320,128]{1,0:T(8,128)(2,1)S(1)}, u32[]{:S(2)}, u32[]{:S(2)}) collective-permute-start(bf16[320,128]{1,0:T(8,128)(2,1)S(1)} %pad_maximum_fusion.2), channel_id=1, source_target_pairs={{0,16},{16,0},{32,48},{48,32},{64,80},{80,64},{96,112},{112,96},{1... | collective-permute-start | bytes 245768 | tf_op jit(solution)/shard_map/ppermute | solution.py:123
  40.1 0.1 maximum_bitcast_fusion
  40.2 2.6 %collective-permute-done.2 = bf16[320,128]{1,0:T(8,128)(2,1)S(1)} collective-permute-done((bf16[320,128]{1,0:T(8,128)(2,1)S(1)}, bf16[320,128]{1,0:T(8,128)(2,1)S(1)}, u32[]{:S(2)}, u32[]{:S(2)}) %collective-permute-start.2) | collective-permute-done | bytes 81952 | tf_op jit(solution)/shard_map/ppermute | solution.py:123
  42.8 6.3 %all-to-all-done = bf16[16,416,128]{2,1,0:T(8,128)(2,1)S(1)} async-done(((bf16[16,416,128]{2,1,0:T(8,128)(2,1)}), bf16[16,416,128]{2,1,0:T(8,128)(2,1)S(1)}, u32[]{:S(2)}, u32[]{:S(2)}) %all-to-all-start) | async-done | bytes 1703968 | tf_op jit(solution)/shard_map/all_to_all | solution.py:499
  49.2 1.9 %collective-permute-start.3 = (bf16[640,128]{1,0:T(8,128)(2,1)S(1)}, bf16[640,128]{1,0:T(8,128)(2,1)S(1)}, u32[]{:S(2)}, u32[]{:S(2)}) collective-permute-start(bf16[640,128]{1,0:T(8,128)(2,1)S(1)} %pad_maximum_fusion.1), channel_id=1, source_target_pairs={{0,128},{16,144},{32,160},{48,176},{64,192},{80,208},{96,224},{112... | collective-permute-start | bytes 491528 | tf_op jit(solution)/shard_map/ppermute | solution.py:123
  51.1 9.6 %shard_map.184 = bf16[2048,128]{1,0:T(8,128)(2,1)} custom-call(s32[1,2]{1,0:T(1,128)S(1)} %copy-done.5, s32[1,2]{1,0:T(1,128)S(1)} %copy-done.6, bf16[6656,128]{1,0:T(8,128)(2,1)S(1)} %bitcast.27, f32[1,128]{1,0:T(1,128)S(1)} %get-tuple-element.54.query_gain_ref, f32[1,128]{1,0:T(1,128)S(1)} %get-tuple-element.55.key_gain_ref), custom_call_target="tpu_custom_call" | custom-call | flops 4831838208 | bytes 4194304 | tf_op jit(solution)/shard_map/pallas_call | solution.py:221
  60.7 0.4 collective-permute-done.3
  61.1 4.2 %all-to-all-start.1 = ((bf16[8,256,128]{2,1,0:T(8,128)(2,1)}), bf16[8,256,128]{2,1,0:T(8,128)(2,1)S(1)}, u32[]{:S(2)}, u32[]{:S(2)}) async-start(bf16[8,256,128]{2,1,0:T(8,128)(2,1)} %bitcast.6), calls=%async_computation.1 | async-start | bytes 1048576 | tf_op jit(solution)/shard_map/all_to_all | solution.py:499
  65.4 0.1 shard_map.185
  65.5 4.2 %collective-permute-start.4 = (bf16[80,128]{1,0:T(8,128)(2,1)S(1)}, bf16[80,128]{1,0:T(8,128)(2,1)S(1)}, u32[]{:S(2)}, u32[]{:S(2)}) collective-permute-start(bf16[80,128]{1,0:T(8,128)(2,1)S(1)} %get-tuple-element.52), channel_id=1, source_target_pairs={{0,256},{16,272},{32,288},{48,304},{64,320},{80,336},{96,352},{112... | collective-permute-start | bytes 61448 | tf_op jit(solution)/shard_map/ppermute | solution.py:123
  69.8 4.2 %collective-permute-done.4.far_ref = bf16[80,128]{1,0:T(8,128)(2,1)S(1)} collective-permute-done((bf16[80,128]{1,0:T(8,128)(2,1)S(1)}, bf16[80,128]{1,0:T(8,128)(2,1)S(1)}, u32[]{:S(2)}, u32[]{:S(2)}) %collective-permute-start.4) | collective-permute-done | bytes 20512 | tf_op jit(solution)/shard_map/ppermute | solution.py:123
  74.0 0.9 all-to-all-done.1
  74.9 6.1 %shard_map.186 = (f32[128,2432]{1,0:T(8,128)}, bf16[128,2432]{1,0:T(8,128)(2,1)S(1)}) custom-call(s32[1]{0:T(128)} %bitcast.1.half_ref, bf16[2048,128]{1,0:T(8,128)(2,1)S(1)} %bitcast.26, bf16[1024,2432]{1,0:T(8,128)(2,1)} %all-gather.2.cloned.1.call-done.weight_ref), custom_call_target="tpu_custom_call" | custom-call | tf_op jit(solution)/shard_map/pallas_call | solution.py:285
  80.9 3.3 %collective-permute-start.5 = (bf16[128,2432]{1,0:T(8,128)(2,1)S(1)}, bf16[128,2432]{1,0:T(8,128)(2,1)S(1)}, u32[]{:S(2)}, u32[]{:S(2)}) collective-permute-start(bf16[128,2432]{1,0:T(8,128)(2,1)S(1)} %get-tuple-element.36), channel_id=1, source_target_pairs={{0,8},{1,9},{2,10},{3,11},{4,12},{5,13},{6,14},{7,15},{8,0},{9,1},... | collective-permute-start | bytes 1867784 | tf_op jit(solution)/shard_map/ppermute | solution.py:123
  84.2 13.2 %collective-permute-done.5.other_ref = bf16[128,2432]{1,0:T(8,128)(2,1)S(1)} collective-permute-done((bf16[128,2432]{1,0:T(8,128)(2,1)S(1)}, bf16[128,2432]{1,0:T(8,128)(2,1)S(1)}, u32[]{:S(2)}, u32[]{:S(2)}) %collective-permute-start.5) | collective-permute-done | bytes 622624 | tf_op jit(solution)/shard_map/ppermute | solution.py:123
  97.5 4.7 %shard_map.187 = (f32[64,128]{1,0:T(8,128)}, bf16[20,64,128]{2,1,0:T(8,128)(2,1)}, f32[8,128]{1,0:T(8,128)S(1)}, f32[128,2432]{1,0:T(8,128)}, f32[128,128]{1,0:T(8,128)S(1)}, /*index=5*/f32[64,128]{1,0:T(8,128)S(1)}) custom-call(s32[1]{0:T(128)} %bitcast.place_ref, s32[1,2]{1,0:T(1,128)S(1)} %copy-done.5, f32[128,2432]{1,0:T(8,128)} %get-tuple-element.35.own_ref, ...), custom_call_target="tpu_custom_call" | custom-call | tf_op jit(solution)/shard_map/pallas_call | solution.py:349
  102.2 6.5 %all-to-all-start.2 = ((bf16[16,80,128]{2,1,0:T(8,128)(2,1)}), bf16[16,80,128]{2,1,0:T(8,128)(2,1)S(1)}, u32[]{:S(2)}, u32[]{:S(2)}) async-start(bf16[16,80,128]{2,1,0:T(8,128)(2,1)} %bitcast.15), calls=%async_computation.2 | async-start | bytes 655360 | tf_op jit(solution)/shard_map/all_to_all | solution.py:499
  108.7 1.3 copy-done.1
  110.0 1.4 shard_map.188.own_ref
  111.4 3.3 %collective-permute-start.6 = (bf16[128,2432]{1,0:T(8,128)(2,1)S(1)}, bf16[128,2432]{1,0:T(8,128)(2,1)S(1)}, u32[]{:S(2)}, u32[]{:S(2)}) collective-permute-start(bf16[128,2432]{1,0:T(8,128)(2,1)S(1)} %shard_map.188.own_ref), channel_id=1, source_target_pairs={{0,8},{1,9},{2,10},{3,11},{4,12},{5,13},{6,14},{7,15},{8,0},{9,1},... | collective-permute-start | bytes 1867784 | tf_op jit(solution)/shard_map/ppermute | solution.py:123
  114.7 1.7 all-to-all-done.2
  116.4 0.7 shard_map.191
  117.1 10.9 %all-to-all-start.3 = ((bf16[8,80,128]{2,1,0:T(8,128)(2,1)}), bf16[8,80,128]{2,1,0:T(8,128)(2,1)S(1)}, u32[]{:S(2)}, u32[]{:S(2)}) async-start(bf16[8,80,128]{2,1,0:T(8,128)(2,1)} %shard_map.191), calls=%async_computation.3 | async-start | bytes 327680 | tf_op jit(solution)/shard_map/all_to_all | solution.py:499
  128.0 0.9 collective-permute-done.6.other_ref
  128.8 7.4 %all-to-all-done.3 = bf16[8,80,128]{2,1,0:T(8,128)(2,1)S(1)} async-done(((bf16[8,80,128]{2,1,0:T(8,128)(2,1)}), bf16[8,80,128]{2,1,0:T(8,128)(2,1)S(1)}, u32[]{:S(2)}, u32[]{:S(2)}) %all-to-all-start.3) | async-done | bytes 163872 | tf_op jit(solution)/shard_map/all_to_all | solution.py:499
  136.2 0.7 shard_map.192
  136.9 4.5 %all-to-all-start.4 = ((bf16[4,80,128]{2,1,0:T(8,128)(2,1)}), bf16[4,80,128]{2,1,0:T(8,128)(2,1)S(1)}, u32[]{:S(2)}, u32[]{:S(2)}) async-start(bf16[4,80,128]{2,1,0:T(8,128)(2,1)} %shard_map.192), calls=%async_computation.4 | async-start | bytes 163840 | tf_op jit(solution)/shard_map/all_to_all | solution.py:499
  141.4 2.4 %copy-done = bf16[1024,2432]{1,0:T(8,128)(2,1)S(1)} copy-done((bf16[1024,2432]{1,0:T(8,128)(2,1)S(1)}, bf16[1024,2432]{1,0:T(8,128)(2,1)}, u32[]{:S(2)}) %copy-start) | copy-done | bytes 4980760
  143.8 2.3 %shard_map.189 = (bf16[128,1024]{1,0:T(8,128)(2,1)S(1)}, bf16[128,1024]{1,0:T(8,128)(2,1)S(1)}) custom-call(bf16[128,2432]{1,0:T(8,128)(2,1)S(1)} %shard_map.188.own_ref, bf16[128,2432]{1,0:T(8,128)(2,1)S(1)} %collective-permute-done.6.other_ref, bf16[1024,2432]{1,0:T(8,128)(2,1)S(1)} %copy-done), custom_call_target="tpu_custom_call" | custom-call | flops 1275068416 | bytes 4980736 | tf_op jit(solution)/shard_map/pallas_call | solution.py:413
  146.1 2.2 %all-to-all-done.4 = bf16[4,80,128]{2,1,0:T(8,128)(2,1)S(1)} async-done(((bf16[4,80,128]{2,1,0:T(8,128)(2,1)}), bf16[4,80,128]{2,1,0:T(8,128)(2,1)S(1)}, u32[]{:S(2)}, u32[]{:S(2)}) %all-to-all-start.4) | async-done | bytes 81952 | tf_op jit(solution)/shard_map/all_to_all | solution.py:499
  148.3 0.8 shard_map.193
  149.1 7.5 %all-to-all-start.5 = ((bf16[16,80,128]{2,1,0:T(8,128)(2,1)}), bf16[16,80,128]{2,1,0:T(8,128)(2,1)S(1)}, u32[]{:S(2)}, u32[]{:S(2)}) async-start(bf16[16,80,128]{2,1,0:T(8,128)(2,1)} %shard_map.193), calls=%async_computation.5 | async-start | bytes 655360 | tf_op jit(solution)/shard_map/all_to_all | solution.py:499
  156.6 3.3 %collective-permute-start.7 = (bf16[128,1024]{1,0:T(8,128)(2,1)S(1)}, bf16[128,1024]{1,0:T(8,128)(2,1)S(1)}, u32[]{:S(2)}, u32[]{:S(2)}) collective-permute-start(bf16[128,1024]{1,0:T(8,128)(2,1)S(1)} %get-tuple-element.44), channel_id=1, source_target_pairs={{0,8},{1,9},{2,10},{3,11},{4,12},{5,13},{6,14},{7,15},{8,0},{9,1},... | collective-permute-start | bytes 786440 | tf_op jit(solution)/shard_map/ppermute | solution.py:123
  159.9 8.2 %collective-permute-done.7.other_ref = bf16[128,1024]{1,0:T(8,128)(2,1)S(1)} collective-permute-done((bf16[128,1024]{1,0:T(8,128)(2,1)S(1)}, bf16[128,1024]{1,0:T(8,128)(2,1)S(1)}, u32[]{:S(2)}, u32[]{:S(2)}) %collective-permute-start.7) | collective-permute-done | bytes 262176 | tf_op jit(solution)/shard_map/ppermute | solution.py:123
  168.1 0.8 shard_map.190
  168.9 0.9 shard_map.194
  169.8 0.5 slice.11
  (22 shorter events, 0.1 us)
Async XLA Ops:
  7.2 67.7 %all-gather.2.cloned.1.call-start = ((), (), s32[]{:S(2)}) async-start(), calls=%async_computation.6 | async-start | bytes 5603328 | tf_op jit(solution)/shard_map/all_gather | solution.py:523
  12.2 10.6 %copy-start.7 = (bf16[80,128]{1,0:T(8,128)(2,1)S(1)}, bf16[80,128]{1,0:T(8,128)(2,1)}, u32[]{:S(2)}) copy-start(bf16[80,128]{1,0:T(8,128)(2,1)} %get-tuple-element.29) | copy-start | bytes 61444
  12.2 27.9 %copy-start.8 = (f32[64]{0:T(128)S(1)}, f32[64]{0:T(128)}, u32[]{:S(2)}) copy-start(f32[64]{0:T(128)} %param.25) | copy-start | bytes 772
  12.2 27.9 %copy-start.9 = (f32[64]{0:T(128)S(1)}, f32[64]{0:T(128)}, u32[]{:S(2)}) copy-start(f32[64]{0:T(128)} %param.26) | copy-start | bytes 772
  12.2 38.8 %copy-start.5 = (s32[1,2]{1,0:T(1,128)S(1)}, s32[1,2]{1,0:T(1,128)}, u32[]{:S(2)}) copy-start(s32[1,2]{1,0:T(1,128)} %counts_ref.7) | copy-start | bytes 28
  12.2 38.8 %copy-start.6 = (s32[1,2]{1,0:T(1,128)S(1)}, s32[1,2]{1,0:T(1,128)}, u32[]{:S(2)}) copy-start(s32[1,2]{1,0:T(1,128)} %lengths_ref.1) | copy-start | bytes 28
  12.3 36.9 %all-to-all-start = ((bf16[16,416,128]{2,1,0:T(8,128)(2,1)}), bf16[16,416,128]{2,1,0:T(8,128)(2,1)S(1)}, u32[]{:S(2)}, u32[]{:S(2)}) async-start(bf16[16,416,128]{2,1,0:T(8,128)(2,1)} %bitcast.35), calls=%async_computation | async-start | bytes 3407872 | tf_op jit(solution)/shard_map/all_to_all | solution.py:499
  22.8 8.5 %collective-permute-start = (bf16[80,128]{1,0:T(8,128)(2,1)S(1)}, bf16[80,128]{1,0:T(8,128)(2,1)S(1)}, u32[]{:S(2)}, u32[]{:S(2)}) collective-permute-start(bf16[80,128]{1,0:T(8,128)(2,1)S(1)} %copy-done.7), channel_id=1, source_target_pairs={{0,64},{16,80},{32,96},{48,112},{64,0},{80,16},{96,32},{112,48},{1... | collective-permute-start | bytes 61448 | tf_op jit(solution)/shard_map/ppermute | solution.py:123
  31.3 5.9 %collective-permute-start.1 = (bf16[160,128]{1,0:T(8,128)(2,1)S(1)}, bf16[160,128]{1,0:T(8,128)(2,1)S(1)}, u32[]{:S(2)}, u32[]{:S(2)}) collective-permute-start(bf16[160,128]{1,0:T(8,128)(2,1)S(1)} %pad_maximum_fusion.3), channel_id=1, source_target_pairs={{0,32},{16,48},{32,0},{48,16},{64,96},{80,112},{96,64},{112,80},{1... | collective-permute-start | bytes 122888 | tf_op jit(solution)/shard_map/ppermute | solution.py:123
  37.2 5.6 %collective-permute-start.2 = (bf16[320,128]{1,0:T(8,128)(2,1)S(1)}, bf16[320,128]{1,0:T(8,128)(2,1)S(1)}, u32[]{:S(2)}, u32[]{:S(2)}) collective-permute-start(bf16[320,128]{1,0:T(8,128)(2,1)S(1)} %pad_maximum_fusion.2), channel_id=1, source_target_pairs={{0,16},{16,0},{32,48},{48,32},{64,80},{80,64},{96,112},{112,96},{1... | collective-permute-start | bytes 245768 | tf_op jit(solution)/shard_map/ppermute | solution.py:123
  49.2 11.9 %collective-permute-start.3 = (bf16[640,128]{1,0:T(8,128)(2,1)S(1)}, bf16[640,128]{1,0:T(8,128)(2,1)S(1)}, u32[]{:S(2)}, u32[]{:S(2)}) collective-permute-start(bf16[640,128]{1,0:T(8,128)(2,1)S(1)} %pad_maximum_fusion.1), channel_id=1, source_target_pairs={{0,128},{16,144},{32,160},{48,176},{64,192},{80,208},{96,224},{112... | collective-permute-start | bytes 491528 | tf_op jit(solution)/shard_map/ppermute | solution.py:123
  61.1 13.7 %all-to-all-start.1 = ((bf16[8,256,128]{2,1,0:T(8,128)(2,1)}), bf16[8,256,128]{2,1,0:T(8,128)(2,1)S(1)}, u32[]{:S(2)}, u32[]{:S(2)}) async-start(bf16[8,256,128]{2,1,0:T(8,128)(2,1)} %bitcast.6), calls=%async_computation.1 | async-start | bytes 1048576 | tf_op jit(solution)/shard_map/all_to_all | solution.py:499
  65.5 8.4 %collective-permute-start.4 = (bf16[80,128]{1,0:T(8,128)(2,1)S(1)}, bf16[80,128]{1,0:T(8,128)(2,1)S(1)}, u32[]{:S(2)}, u32[]{:S(2)}) collective-permute-start(bf16[80,128]{1,0:T(8,128)(2,1)S(1)} %get-tuple-element.52), channel_id=1, source_target_pairs={{0,256},{16,272},{32,288},{48,304},{64,320},{80,336},{96,352},{112... | collective-permute-start | bytes 61448 | tf_op jit(solution)/shard_map/ppermute | solution.py:123
  74.8 22.6 %copy-start.2 = (bf16[2432,64]{0,1:T(8,128)(2,1)S(1)}, bf16[2432,64]{0,1:T(8,128)(2,1)}, u32[]{:S(2)}) copy-start(bf16[2432,64]{0,1:T(8,128)(2,1)} %param.30) | copy-start | bytes 933892
  74.8 22.6 %copy-start.3 = (f32[2,7296]{1,0:T(2,128)S(1)}, f32[2,7296]{1,0:T(2,128)}, u32[]{:S(2)}) copy-start(f32[2,7296]{1,0:T(2,128)} %modulate_ref.3) | copy-start | bytes 175108
  74.8 22.6 %copy-start.4 = (bf16[1,64,128]{2,1,0:T(8,128)(2,1)S(1)}, bf16[1,64,128]{2,1,0:T(8,128)(2,1)}, u32[]{:S(2)}) copy-start(bf16[1,64,128]{2,1,0:T(8,128)(2,1)} %param.31) | copy-start | bytes 49156
  80.9 16.6 %collective-permute-start.5 = (bf16[128,2432]{1,0:T(8,128)(2,1)S(1)}, bf16[128,2432]{1,0:T(8,128)(2,1)S(1)}, u32[]{:S(2)}, u32[]{:S(2)}) collective-permute-start(bf16[128,2432]{1,0:T(8,128)(2,1)S(1)} %get-tuple-element.36), channel_id=1, source_target_pairs={{0,8},{1,9},{2,10},{3,11},{4,12},{5,13},{6,14},{7,15},{8,0},{9,1},... | collective-permute-start | bytes 1867784 | tf_op jit(solution)/shard_map/ppermute | solution.py:123
  102.2 14.2 %all-to-all-start.2 = ((bf16[16,80,128]{2,1,0:T(8,128)(2,1)}), bf16[16,80,128]{2,1,0:T(8,128)(2,1)S(1)}, u32[]{:S(2)}, u32[]{:S(2)}) async-start(bf16[16,80,128]{2,1,0:T(8,128)(2,1)} %bitcast.15), calls=%async_computation.2 | async-start | bytes 655360 | tf_op jit(solution)/shard_map/all_to_all | solution.py:499
  108.7 1.3 copy-start.1
  111.4 17.5 %collective-permute-start.6 = (bf16[128,2432]{1,0:T(8,128)(2,1)S(1)}, bf16[128,2432]{1,0:T(8,128)(2,1)S(1)}, u32[]{:S(2)}, u32[]{:S(2)}) collective-permute-start(bf16[128,2432]{1,0:T(8,128)(2,1)S(1)} %shard_map.188.own_ref), channel_id=1, source_target_pairs={{0,8},{1,9},{2,10},{3,11},{4,12},{5,13},{6,14},{7,15},{8,0},{9,1},... | collective-permute-start | bytes 1867784 | tf_op jit(solution)/shard_map/ppermute | solution.py:123
  117.1 19.1 %all-to-all-start.3 = ((bf16[8,80,128]{2,1,0:T(8,128)(2,1)}), bf16[8,80,128]{2,1,0:T(8,128)(2,1)S(1)}, u32[]{:S(2)}, u32[]{:S(2)}) async-start(bf16[8,80,128]{2,1,0:T(8,128)(2,1)} %shard_map.191), calls=%async_computation.3 | async-start | bytes 327680 | tf_op jit(solution)/shard_map/all_to_all | solution.py:499
  136.9 11.5 %all-to-all-start.4 = ((bf16[4,80,128]{2,1,0:T(8,128)(2,1)}), bf16[4,80,128]{2,1,0:T(8,128)(2,1)S(1)}, u32[]{:S(2)}, u32[]{:S(2)}) async-start(bf16[4,80,128]{2,1,0:T(8,128)(2,1)} %shard_map.192), calls=%async_computation.4 | async-start | bytes 163840 | tf_op jit(solution)/shard_map/all_to_all | solution.py:499
  141.4 2.4 %copy-start = (bf16[1024,2432]{1,0:T(8,128)(2,1)S(1)}, bf16[1024,2432]{1,0:T(8,128)(2,1)}, u32[]{:S(2)}) copy-start(bf16[1024,2432]{1,0:T(8,128)(2,1)} %all-gather.2.cloned.1.call-done.weight_ref) | copy-start | bytes 14942212
  149.1 19.8 %all-to-all-start.5 = ((bf16[16,80,128]{2,1,0:T(8,128)(2,1)}), bf16[16,80,128]{2,1,0:T(8,128)(2,1)S(1)}, u32[]{:S(2)}, u32[]{:S(2)}) async-start(bf16[16,80,128]{2,1,0:T(8,128)(2,1)} %shard_map.193), calls=%async_computation.5 | async-start | bytes 655360 | tf_op jit(solution)/shard_map/all_to_all | solution.py:499
  156.6 11.5 %collective-permute-start.7 = (bf16[128,1024]{1,0:T(8,128)(2,1)S(1)}, bf16[128,1024]{1,0:T(8,128)(2,1)S(1)}, u32[]{:S(2)}, u32[]{:S(2)}) collective-permute-start(bf16[128,1024]{1,0:T(8,128)(2,1)S(1)} %get-tuple-element.44), channel_id=1, source_target_pairs={{0,8},{1,9},{2,10},{3,11},{4,12},{5,13},{6,14},{7,15},{8,0},{9,1},... | collective-permute-start | bytes 786440 | tf_op jit(solution)/shard_map/ppermute | solution.py:123
Sparse Core Ops, SparseCore 0:
  10.1 56.9 all-gather.1

commit v6 on v5

--- a/solution.py
+++ b/solution.py
@@ -263,47 +263,70 @@
     return first, jnp.where(first, counts_ref[0, 0], border + counts_ref[0, 1]) - place
 
 
-def project_kernel(half_ref, rows_ref, weight_ref, own_ref, other_ref, lined_ref):
-    tile = own_ref.shape[0]
-
-    @pl.when(pl.program_id(0) == 0)
-    def _():
-        for at in range(lined_ref.shape[1] // LANES):
-            rows = rows_ref[at * 2 * tile : (at + 1) * 2 * tile, :]
-            lined_ref[:, at * LANES : (at + 1) * LANES] = rows
-
-    product = jnp.dot(lined_ref[...], weight_ref[...], preferred_element_type=jnp.float32)
+def project_kernel(
+    block, half_ref, rows_ref, weight_ref, own_ref, other_ref, lined_ref, here_ref, semaphores
+):
+    tile, width = own_ref.shape
+    whole = width // block
+
+    def landing(at, size):
+        columns = pl.ds(pl.multiple_of(at * block, block), size)
+        return pltpu.make_async_copy(
+            weight_ref.at[:, columns], here_ref.at[:, columns], semaphores.at[at]
+        )
+
+    sizes = [block] * whole + ([width % block] if width % block else [])
+    for at, size in enumerate(sizes):
+        landing(at, size).start()
+    for at in range(lined_ref.shape[1] // LANES):
+        rows = rows_ref[at * 2 * tile : (at + 1) * 2 * tile, :]
+        lined_ref[:, at * LANES : (at + 1) * LANES] = rows
     first = half_ref[0] == 0
-    own_ref[...] = jnp.where(first, product[:tile], product[tile:])
-    other_ref[...] = jnp.where(first, product[tile:], product[:tile]).astype(jnp.bfloat16)
+
+    def multiply(at, size):
+        landing(at, size).wait()
+        columns = pl.ds(pl.multiple_of(at * block, block), size)
+        product = jnp.dot(lined_ref[...], here_ref[:, columns], preferred_element_type=jnp.float32)
+        own_ref[:, columns] = jnp.where(first, product[:tile], product[tile:])
+        other = jnp.where(first, product[tile:], product[:tile])
+        other_ref[:, columns] = other.astype(jnp.bfloat16)
+
+    @pl.loop(0, whole)
+    def _(at):
+        multiply(at, block)
+
+    if width % block:
+        multiply(whole, width % block)
 
 
 def project(half, recv, weight, tile):
     depth, width = weight.shape
     block = 4 * LANES
-    out_spec = pl.BlockSpec((tile, block), lambda i: (0, i))
-    return pl.pallas_call(
-        project_kernel,
-        grid=(pl.cdiv(width, block),),
+    return pl.pallas_call(
+        functools.partial(project_kernel, block),
         out_shape=(
             jax.ShapeDtypeStruct((tile, width), jnp.float32),
             jax.ShapeDtypeStruct((tile, width), jnp.bfloat16),
         ),
-        in_specs=[SMEM, VMEM, pl.BlockSpec((depth, block), lambda i: (0, i))],
-        out_specs=(out_spec, out_spec),
-        scratch_shapes=[pltpu.VMEM((2 * tile, depth), jnp.bfloat16)],
-        compiler_params=params(52, ("arbitrary",)),
+        in_specs=[SMEM, VMEM, HBM],
+        out_specs=(VMEM, VMEM),
+        scratch_shapes=[
+            pltpu.VMEM((2 * tile, depth), jnp.bfloat16),
+            pltpu.VMEM((depth, width), jnp.bfloat16),
+            pltpu.SemaphoreType.DMA((pl.cdiv(width, block),)),
+        ],
+        compiler_params=params(52),
     )(half, recv, weight)
 
 
 def head_kernel(
     place_ref, counts_ref, own_ref, other_ref, residual_ref, modulate_ref, final_ref, noise_ref,
     near_ref, far_ref, velocity_ref, parts_ref, total_ref, normed_ref, inverse_ref, grad_ref,
-    own_here, other_here, semaphores,
+    own_here, other_here, residual_here, semaphores,
 ):
+    pairs = ((own_ref, own_here), (residual_ref, residual_here), (other_ref, other_here))
     copies = [
-        pltpu.make_async_copy(own_ref, own_here, semaphores.at[0]),
-        pltpu.make_async_copy(other_ref, other_here, semaphores.at[1]),
+        pltpu.make_async_copy(there, here, semaphores.at[at]) for at, (there, here) in enumerate(pairs)
     ]
     for copy in copies:
         copy.start()
@@ -319,7 +342,7 @@
     for copy in copies:
         copy.wait()
     projected = own_here[...] + other_here[...].astype(jnp.float32)
-    hidden = residual_ref[...].astype(jnp.float32) + gate * projected
+    hidden = residual_here[...].astype(jnp.float32) + gate * projected
     centered = hidden - row_mean(hidden)
     inverse = lax.rsqrt(row_mean(centered * centered) + EPSILON)
     normed = centered * inverse
@@ -356,12 +379,13 @@
             jax.ShapeDtypeStruct((tile, LANES), jnp.float32),
             jax.ShapeDtypeStruct((lat, tile), jnp.float32),
         ),
-        in_specs=[SMEM] * 2 + [HBM] * 2 + [VMEM] * 6,
+        in_specs=[SMEM] * 2 + [HBM] * 3 + [VMEM] * 5,
         out_specs=(VMEM,) * 6,
         scratch_shapes=[
             pltpu.VMEM(own.shape, own.dtype),
             pltpu.VMEM(other.shape, other.dtype),
-            pltpu.SemaphoreType.DMA((2,)),
+            pltpu.VMEM(residual.shape, residual.dtype),
+            pltpu.SemaphoreType.DMA((3,)),
         ],
         compiler_params=params(52),
     )(place, counts, own, other, residual, modulate, final_columns, noise, near, far)
@@ -527,7 +551,7 @@
     recv = exchange(sent, "seqt")
     bits = [1 << at for at in range(ranks.bit_length() - 1)]
     held = gather(tagged, ranks, [bit for bit in reversed(bits) if bit < near])
-    recv, held = lax.optimization_barrier((recv, held))
+    recv, _ = lax.optimization_barrier((recv, held))
     held = gather(held, ranks, [bit for bit in bits[:-1] if bit >= near])
     heads = attention(
         recv, image_tokens, text_lengths, query_gain, key_gain, sources, tile, text_rows
@@ -556,7 +580,6 @@
     sums = exchange(parts.reshape(blocks * lat_width, LANES), "seqt")
     sums, _ = lax.optimization_barrier((sums, grad_projected))
     sums = exchange(sum_out(sums, sources, near, loss_row, last), "dp", near_groups)
-    sums, _ = lax.optimization_barrier((sums, partner_grad))
     sums = exchange(sum_out(sums, near, far, loss_row, last), "dp", far_groups)
     sums, _ = lax.optimization_barrier((sums, across_grad))
     sums = exchange(sum_out(sums, far, sources, loss_row, last), "seqt")

time: 178 us -> 177 us (level)
  blocking collectives: 0 us -> 14.9 us
  waiting for transfers between devices: 52.3 us -> 43.5 us
  starting transfers between devices: 73.9 us -> 68.4 us
    all_to_all x0 -> x1, blocking collectives: none -> 14.9 us  [exchange(): lax.all_to_all(array, axis, split_axis=0, concat_axis=0, axis_index_group...]
    all_to_all x6 -> x5, waiting for transfers between devices: 18.5 us -> 4.84 us  [exchange(): lax.all_to_all(array, axis, split_axis=0, concat_axis=0, axis_index_group...]
    all_to_all x6 -> x5, starting transfers between devices: 44.1 us -> 34.4 us  [exchange(): lax.all_to_all(array, axis, split_axis=0, concat_axis=0, axis_index_group...]
    ppermute x8, waiting for transfers between devices: 33.1 us -> 37.9 us  [swap(): lax.ppermute(array, axis, [(rank, rank ^ step) for rank in range(ranks)])]
    ppermute x8, starting transfers between devices: 29.7 us -> 34 us  [swap(): lax.ppermute(array, axis, [(rank, rank ^ step) for rank in range(ranks)])]
    unnamed x20 -> x24, local copies, waits for them, and re-layouts: 3.74 us -> 3.81 us
  transfers between devices with their start and end apart: 15 -> 14, of which waited for: 13 -> 10; matrix products, arithmetic and copies ran while one was open for 0% -> 0% of each run, Pallas kernels for 10% -> 11%
where the time goes in v6:
time: 177 us; the launch traced here: 176 us
  starting transfers between devices  68.4 us (39%)
  waiting for transfers between devices  43.5 us (25%)
  Pallas kernels  30 us (17%)
  blocking collectives  14.9 us (8%)
  between operations  14.9 us (8%)
  local copies, waits for them, and re-layouts  4.35 us (2%)
    ppermute x8, waiting for transfers between devices, swap(): lax.ppermute(array, axis, [(rank, rank ^ step) for rank in range(ranks)])  37.9 us
    all_to_all x5, starting transfers between devices, exchange(): lax.all_to_all(array, axis, split_axis=0, concat_axis=0, axis_index_group...  34.4 us
    ppermute x8, starting transfers between devices, swap(): lax.ppermute(array, axis, [(rank, rank ^ step) for rank in range(ranks)])  34 us
    all_to_all x1, blocking collectives, exchange(): lax.all_to_all(array, axis, split_axis=0, concat_axis=0, axis_index_group...  14.9 us
    pallas_call x1, Pallas kernels, attention(): pl.pallas_call(functools.partial(attention_kernel, sources, tile, text_ro...  10.4 us
    all_to_all x5, waiting for transfers between devices, exchange(): lax.all_to_all(array, axis, split_axis=0, concat_axis=0, axis_index_group...  4.84 us
    pallas_call x1, Pallas kernels, project(): pl.pallas_call(functools.partial(project_kernel, block), out_shape=(jax.S...  4.6 us
    pallas_call x1, Pallas kernels, head(): pl.pallas_call(head_kernel, out_shape=(jax.ShapeDtypeStruct((lat, tile),...  4.34 us
  transfers between devices with their start and end apart: 14, of which 10 were waited for; matrix products, arithmetic and copies ran while one was open for 0% of the time, Pallas kernels for 11%

profile of v6, /device:TPU:1, one launch (start us, length us, event | category | flops | bytes accessed | tf_op | source)
XLA Modules:
  0.0 176.2 jit_solution(6865791291915279338)
XLA Ops:
  7.2 0.0 all-gather.2.cloned.1.call-start
  7.2 0.7 all-gather.2.cloned.1.call-update
  8.5 3.6 %shard_map.183 = (bf16[6656,128]{1,0:T(8,128)(2,1)}, bf16[80,128]{1,0:T(8,128)(2,1)}) custom-call(s32[1]{0:T(128)S(6)} %copy.27.route_ref, s32[1,2]{1,0:T(1,128)} %counts_ref.7, bf16[1,64,128]{2,1,0:T(8,128)(2,1)} %tile_ref.1, bf16[128,2048]{1,0:T(8,128)(2,1)} %refs_0_.1, bf16[128,2048]{1,0:T(8,128)(2,1)} %refs_1_.1, bf16[128,2048]{1,0:T(8,128)(2,1)} %refs_2_.1, ...), custom_call_target="tpu_custom_call" | custom-call | tf_op jit(solution)/shard_map/pallas_call | solution.py:62
  12.2 0.0 copy-start.7
  12.2 0.0 copy-start.8
  12.2 0.0 copy-start.9
  12.2 0.0 copy-start.5
  12.2 0.0 copy-start.6
  12.3 10.5 %all-to-all-start = ((bf16[16,416,128]{2,1,0:T(8,128)(2,1)}), bf16[16,416,128]{2,1,0:T(8,128)(2,1)S(1)}, u32[]{:S(2)}, u32[]{:S(2)}) async-start(bf16[16,416,128]{2,1,0:T(8,128)(2,1)} %bitcast.35), calls=%async_computation | async-start | bytes 3407872 | tf_op jit(solution)/shard_map/all_to_all | solution.py:523
  22.8 7.1 %collective-permute-start = (bf16[80,128]{1,0:T(8,128)(2,1)S(1)}, bf16[80,128]{1,0:T(8,128)(2,1)S(1)}, u32[]{:S(2)}, u32[]{:S(2)}) collective-permute-start(bf16[80,128]{1,0:T(8,128)(2,1)S(1)} %copy-done.7), channel_id=1, source_target_pairs={{0,64},{16,80},{32,96},{48,112},{64,0},{80,16},{96,32},{112,48},{1... | collective-permute-start | bytes 61448 | tf_op jit(solution)/shard_map/ppermute | solution.py:123
  29.9 1.4 collective-permute-done
  31.3 3.8 %collective-permute-start.1 = (bf16[160,128]{1,0:T(8,128)(2,1)S(1)}, bf16[160,128]{1,0:T(8,128)(2,1)S(1)}, u32[]{:S(2)}, u32[]{:S(2)}) collective-permute-start(bf16[160,128]{1,0:T(8,128)(2,1)S(1)} %pad_maximum_fusion.1), channel_id=1, source_target_pairs={{0,32},{16,48},{32,0},{48,16},{64,96},{80,112},{96,64},{112,80},{1... | collective-permute-start | bytes 122888 | tf_op jit(solution)/shard_map/ppermute | solution.py:123
  35.1 2.1 %collective-permute-done.1 = bf16[160,128]{1,0:T(8,128)(2,1)S(1)} collective-permute-done((bf16[160,128]{1,0:T(8,128)(2,1)S(1)}, bf16[160,128]{1,0:T(8,128)(2,1)S(1)}, u32[]{:S(2)}, u32[]{:S(2)}) %collective-permute-start.1) | collective-permute-done | bytes 40992 | tf_op jit(solution)/shard_map/ppermute | solution.py:123
  37.2 2.8 %collective-permute-start.2 = (bf16[320,128]{1,0:T(8,128)(2,1)S(1)}, bf16[320,128]{1,0:T(8,128)(2,1)S(1)}, u32[]{:S(2)}, u32[]{:S(2)}) collective-permute-start(bf16[320,128]{1,0:T(8,128)(2,1)S(1)} %pad_maximum_fusion), channel_id=1, source_target_pairs={{0,16},{16,0},{32,48},{48,32},{64,80},{80,64},{96,112},{112,96},{1... | collective-permute-start | bytes 245768 | tf_op jit(solution)/shard_map/ppermute | solution.py:123
  40.1 2.7 %collective-permute-done.2 = bf16[320,128]{1,0:T(8,128)(2,1)S(1)} collective-permute-done((bf16[320,128]{1,0:T(8,128)(2,1)S(1)}, bf16[320,128]{1,0:T(8,128)(2,1)S(1)}, u32[]{:S(2)}, u32[]{:S(2)}) %collective-permute-start.2) | collective-permute-done | bytes 81952 | tf_op jit(solution)/shard_map/ppermute | solution.py:123
  42.8 5.2 %collective-permute-start.3 = (bf16[640,128]{1,0:T(8,128)(2,1)S(1)}, bf16[640,128]{1,0:T(8,128)(2,1)S(1)}, u32[]{:S(2)}, u32[]{:S(2)}) collective-permute-start(bf16[640,128]{1,0:T(8,128)(2,1)S(1)} %get-tuple-element.49), channel_id=1, source_target_pairs={{0,128},{16,144},{32,160},{48,176},{64,192},{80,208},{96,224},{112... | collective-permute-start | bytes 491528 | tf_op jit(solution)/shard_map/ppermute | solution.py:123
  48.0 0.1 maximum_bitcast_fusion
  48.1 7.1 %collective-permute-done.3 = bf16[640,128]{1,0:T(8,128)(2,1)S(1)} collective-permute-done((bf16[640,128]{1,0:T(8,128)(2,1)S(1)}, bf16[640,128]{1,0:T(8,128)(2,1)S(1)}, u32[]{:S(2)}, u32[]{:S(2)}) %collective-permute-start.3) | collective-permute-done | bytes 163872 | tf_op jit(solution)/shard_map/ppermute | solution.py:123
  55.2 0.0 all-to-all-done
  55.2 10.4 %shard_map.184 = bf16[2048,128]{1,0:T(8,128)(2,1)} custom-call(s32[1,2]{1,0:T(1,128)S(1)} %copy-done.5, s32[1,2]{1,0:T(1,128)S(1)} %copy-done.6, bf16[6656,128]{1,0:T(8,128)(2,1)S(1)} %bitcast.27, f32[1,128]{1,0:T(1,128)S(1)} %get-tuple-element.58.query_gain_ref, f32[1,128]{1,0:T(1,128)S(1)} %get-tuple-element.59.key_gain_ref), custom_call_target="tpu_custom_call" | custom-call | flops 4831838208 | bytes 4194304 | tf_op jit(solution)/shard_map/pallas_call | solution.py:221
  65.7 5.0 %all-to-all-start.1 = ((bf16[8,256,128]{2,1,0:T(8,128)(2,1)}), bf16[8,256,128]{2,1,0:T(8,128)(2,1)S(1)}, u32[]{:S(2)}, u32[]{:S(2)}) async-start(bf16[8,256,128]{2,1,0:T(8,128)(2,1)} %bitcast.6), calls=%async_computation.1 | async-start | bytes 1048576 | tf_op jit(solution)/shard_map/all_to_all | solution.py:523
  70.7 0.1 shard_map.185
  70.9 6.5 %collective-permute-start.4 = (bf16[80,128]{1,0:T(8,128)(2,1)S(1)}, bf16[80,128]{1,0:T(8,128)(2,1)S(1)}, u32[]{:S(2)}, u32[]{:S(2)}) collective-permute-start(bf16[80,128]{1,0:T(8,128)(2,1)S(1)} %get-tuple-element.50), channel_id=1, source_target_pairs={{0,256},{16,272},{32,288},{48,304},{64,320},{80,336},{96,352},{112... | collective-permute-start | bytes 61448 | tf_op jit(solution)/shard_map/ppermute | solution.py:123
  77.4 1.9 %collective-permute-done.4.far_ref = bf16[80,128]{1,0:T(8,128)(2,1)S(1)} collective-permute-done((bf16[80,128]{1,0:T(8,128)(2,1)S(1)}, bf16[80,128]{1,0:T(8,128)(2,1)S(1)}, u32[]{:S(2)}, u32[]{:S(2)}) %collective-permute-start.4) | collective-permute-done | bytes 20512 | tf_op jit(solution)/shard_map/ppermute | solution.py:123
  79.3 0.9 all-to-all-done.1
  80.2 4.6 %shard_map.186 = (f32[128,2432]{1,0:T(8,128)}, bf16[128,2432]{1,0:T(8,128)(2,1)S(1)}) custom-call(s32[1]{0:T(128)} %bitcast.1.half_ref, bf16[2048,128]{1,0:T(8,128)(2,1)S(1)} %bitcast.26, bf16[1024,2432]{1,0:T(8,128)(2,1)} %all-gather.2.cloned.1.call-done.weight_ref), custom_call_target="tpu_custom_call" | custom-call | tf_op jit(solution)/shard_map/pallas_call | solution.py:305
  84.8 2.0 %collective-permute-start.5 = (bf16[128,2432]{1,0:T(8,128)(2,1)S(1)}, bf16[128,2432]{1,0:T(8,128)(2,1)S(1)}, u32[]{:S(2)}, u32[]{:S(2)}) collective-permute-start(bf16[128,2432]{1,0:T(8,128)(2,1)S(1)} %get-tuple-element.33), channel_id=1, source_target_pairs={{0,8},{1,9},{2,10},{3,11},{4,12},{5,13},{6,14},{7,15},{8,0},{9,1},... | collective-permute-start | bytes 1867784 | tf_op jit(solution)/shard_map/ppermute | solution.py:123
  86.9 14.5 %collective-permute-done.5.other_ref = bf16[128,2432]{1,0:T(8,128)(2,1)S(1)} collective-permute-done((bf16[128,2432]{1,0:T(8,128)(2,1)S(1)}, bf16[128,2432]{1,0:T(8,128)(2,1)S(1)}, u32[]{:S(2)}, u32[]{:S(2)}) %collective-permute-start.5) | collective-permute-done | bytes 622624 | tf_op jit(solution)/shard_map/ppermute | solution.py:123
  101.4 4.3 %shard_map.187 = (f32[64,128]{1,0:T(8,128)}, bf16[20,64,128]{2,1,0:T(8,128)(2,1)}, f32[8,128]{1,0:T(8,128)S(1)}, f32[128,2432]{1,0:T(8,128)}, f32[128,128]{1,0:T(8,128)S(1)}, /*index=5*/f32[64,128]{1,0:T(8,128)S(1)}) custom-call(s32[1]{0:T(128)} %bitcast.place_ref, s32[1,2]{1,0:T(1,128)S(1)} %copy-done.5, f32[128,2432]{1,0:T(8,128)} %get-tuple-element.32.own_ref, ...), custom_call_target="tpu_custom_call" | custom-call | tf_op jit(solution)/shard_map/pallas_call | solution.py:372
  105.7 5.4 %all-to-all-start.2 = ((bf16[16,80,128]{2,1,0:T(8,128)(2,1)}), bf16[16,80,128]{2,1,0:T(8,128)(2,1)S(1)}, u32[]{:S(2)}, u32[]{:S(2)}) async-start(bf16[16,80,128]{2,1,0:T(8,128)(2,1)} %bitcast.15), calls=%async_computation.2 | async-start | bytes 655360 | tf_op jit(solution)/shard_map/all_to_all | solution.py:523
  111.1 1.3 copy-done.1
  112.4 1.4 shard_map.188.own_ref
  113.8 3.3 %collective-permute-start.6 = (bf16[128,2432]{1,0:T(8,128)(2,1)S(1)}, bf16[128,2432]{1,0:T(8,128)(2,1)S(1)}, u32[]{:S(2)}, u32[]{:S(2)}) collective-permute-start(bf16[128,2432]{1,0:T(8,128)(2,1)S(1)} %shard_map.188.own_ref), channel_id=1, source_target_pairs={{0,8},{1,9},{2,10},{3,11},{4,12},{5,13},{6,14},{7,15},{8,0},{9,1},... | collective-permute-start | bytes 1867784 | tf_op jit(solution)/shard_map/ppermute | solution.py:123
  117.1 1.7 all-to-all-done.2
  118.8 0.1 shard_map.191
  118.9 14.9 %all_to_all.59 = bf16[8,80,128]{2,1,0:T(8,128)(2,1)S(1)} all-to-all(bf16[8,80,128]{2,1,0:T(8,128)(2,1)S(1)} %shard_map.191), channel_id=1, replica_groups={{0,16,32,48,64,80,96,112},{128,144,160,176,192,208,224,240},{256,272,28..., dimensions={0} | all-to-all | bytes 327680 | tf_op jit(solution)/shard_map/all_to_all | solution.py:523
  133.8 0.7 shard_map.192
  134.4 6.0 %all-to-all-start.4 = ((bf16[4,80,128]{2,1,0:T(8,128)(2,1)}), bf16[4,80,128]{2,1,0:T(8,128)(2,1)S(1)}, u32[]{:S(2)}, u32[]{:S(2)}) async-start(bf16[4,80,128]{2,1,0:T(8,128)(2,1)} %shard_map.192), calls=%async_computation.4 | async-start | bytes 163840 | tf_op jit(solution)/shard_map/all_to_all | solution.py:523
  140.4 2.4 %copy-done = bf16[1024,2432]{1,0:T(8,128)(2,1)S(1)} copy-done((bf16[1024,2432]{1,0:T(8,128)(2,1)S(1)}, bf16[1024,2432]{1,0:T(8,128)(2,1)}, u32[]{:S(2)}) %copy-start) | copy-done | bytes 4980760
  142.8 2.3 %shard_map.189 = (bf16[128,1024]{1,0:T(8,128)(2,1)S(1)}, bf16[128,1024]{1,0:T(8,128)(2,1)S(1)}) custom-call(bf16[128,2432]{1,0:T(8,128)(2,1)S(1)} %shard_map.188.own_ref, bf16[128,2432]{1,0:T(8,128)(2,1)S(1)} %collective-permute-done.6.other_ref, bf16[1024,2432]{1,0:T(8,128)(2,1)S(1)} %copy-done), custom_call_target="tpu_custom_call" | custom-call | flops 1275068416 | bytes 4980736 | tf_op jit(solution)/shard_map/pallas_call | solution.py:437
  145.1 2.2 %all-to-all-done.4 = bf16[4,80,128]{2,1,0:T(8,128)(2,1)S(1)} async-done(((bf16[4,80,128]{2,1,0:T(8,128)(2,1)}), bf16[4,80,128]{2,1,0:T(8,128)(2,1)S(1)}, u32[]{:S(2)}, u32[]{:S(2)}) %all-to-all-start.4) | async-done | bytes 81952 | tf_op jit(solution)/shard_map/all_to_all | solution.py:523
  147.4 0.8 shard_map.193
  148.1 7.5 %all-to-all-start.5 = ((bf16[16,80,128]{2,1,0:T(8,128)(2,1)}), bf16[16,80,128]{2,1,0:T(8,128)(2,1)S(1)}, u32[]{:S(2)}, u32[]{:S(2)}) async-start(bf16[16,80,128]{2,1,0:T(8,128)(2,1)} %shard_map.193), calls=%async_computation.5 | async-start | bytes 655360 | tf_op jit(solution)/shard_map/all_to_all | solution.py:523
  155.6 3.3 %collective-permute-start.7 = (bf16[128,1024]{1,0:T(8,128)(2,1)S(1)}, bf16[128,1024]{1,0:T(8,128)(2,1)S(1)}, u32[]{:S(2)}, u32[]{:S(2)}) collective-permute-start(bf16[128,1024]{1,0:T(8,128)(2,1)S(1)} %get-tuple-element.41), channel_id=1, source_target_pairs={{0,8},{1,9},{2,10},{3,11},{4,12},{5,13},{6,14},{7,15},{8,0},{9,1},... | collective-permute-start | bytes 786440 | tf_op jit(solution)/shard_map/ppermute | solution.py:123
  158.9 8.2 %collective-permute-done.7.other_ref = bf16[128,1024]{1,0:T(8,128)(2,1)S(1)} collective-permute-done((bf16[128,1024]{1,0:T(8,128)(2,1)S(1)}, bf16[128,1024]{1,0:T(8,128)(2,1)S(1)}, u32[]{:S(2)}, u32[]{:S(2)}) %collective-permute-start.7) | collective-permute-done | bytes 262176 | tf_op jit(solution)/shard_map/ppermute | solution.py:123
  167.1 0.8 shard_map.190
  168.0 0.9 shard_map.194
  168.8 0.5 slice.11
  (24 shorter events, 0.1 us)
Async XLA Ops:
  7.2 73.0 %all-gather.2.cloned.1.call-start = ((), (), s32[]{:S(2)}) async-start(), calls=%async_computation.6 | async-start | bytes 5603328 | tf_op jit(solution)/shard_map/all_gather | solution.py:547
  12.2 10.6 %copy-start.7 = (bf16[80,128]{1,0:T(8,128)(2,1)S(1)}, bf16[80,128]{1,0:T(8,128)(2,1)}, u32[]{:S(2)}) copy-start(bf16[80,128]{1,0:T(8,128)(2,1)} %get-tuple-element.27) | copy-start | bytes 61444
  12.2 35.8 %copy-start.8 = (f32[64]{0:T(128)S(1)}, f32[64]{0:T(128)}, u32[]{:S(2)}) copy-start(f32[64]{0:T(128)} %param.25) | copy-start | bytes 772
  12.2 35.8 %copy-start.9 = (f32[64]{0:T(128)S(1)}, f32[64]{0:T(128)}, u32[]{:S(2)}) copy-start(f32[64]{0:T(128)} %param.26) | copy-start | bytes 772
  12.2 43.0 %copy-start.5 = (s32[1,2]{1,0:T(1,128)S(1)}, s32[1,2]{1,0:T(1,128)}, u32[]{:S(2)}) copy-start(s32[1,2]{1,0:T(1,128)} %counts_ref.7) | copy-start | bytes 28
  12.2 43.0 %copy-start.6 = (s32[1,2]{1,0:T(1,128)S(1)}, s32[1,2]{1,0:T(1,128)}, u32[]{:S(2)}) copy-start(s32[1,2]{1,0:T(1,128)} %lengths_ref.1) | copy-start | bytes 28
  12.3 43.0 %all-to-all-start = ((bf16[16,416,128]{2,1,0:T(8,128)(2,1)}), bf16[16,416,128]{2,1,0:T(8,128)(2,1)S(1)}, u32[]{:S(2)}, u32[]{:S(2)}) async-start(bf16[16,416,128]{2,1,0:T(8,128)(2,1)} %bitcast.35), calls=%async_computation | async-start | bytes 3407872 | tf_op jit(solution)/shard_map/all_to_all | solution.py:523
  22.8 8.5 %collective-permute-start = (bf16[80,128]{1,0:T(8,128)(2,1)S(1)}, bf16[80,128]{1,0:T(8,128)(2,1)S(1)}, u32[]{:S(2)}, u32[]{:S(2)}) collective-permute-start(bf16[80,128]{1,0:T(8,128)(2,1)S(1)} %copy-done.7), channel_id=1, source_target_pairs={{0,64},{16,80},{32,96},{48,112},{64,0},{80,16},{96,32},{112,48},{1... | collective-permute-start | bytes 61448 | tf_op jit(solution)/shard_map/ppermute | solution.py:123
  31.3 5.9 %collective-permute-start.1 = (bf16[160,128]{1,0:T(8,128)(2,1)S(1)}, bf16[160,128]{1,0:T(8,128)(2,1)S(1)}, u32[]{:S(2)}, u32[]{:S(2)}) collective-permute-start(bf16[160,128]{1,0:T(8,128)(2,1)S(1)} %pad_maximum_fusion.1), channel_id=1, source_target_pairs={{0,32},{16,48},{32,0},{48,16},{64,96},{80,112},{96,64},{112,80},{1... | collective-permute-start | bytes 122888 | tf_op jit(solution)/shard_map/ppermute | solution.py:123
  37.2 5.6 %collective-permute-start.2 = (bf16[320,128]{1,0:T(8,128)(2,1)S(1)}, bf16[320,128]{1,0:T(8,128)(2,1)S(1)}, u32[]{:S(2)}, u32[]{:S(2)}) collective-permute-start(bf16[320,128]{1,0:T(8,128)(2,1)S(1)} %pad_maximum_fusion), channel_id=1, source_target_pairs={{0,16},{16,0},{32,48},{48,32},{64,80},{80,64},{96,112},{112,96},{1... | collective-permute-start | bytes 245768 | tf_op jit(solution)/shard_map/ppermute | solution.py:123
  42.8 12.3 %collective-permute-start.3 = (bf16[640,128]{1,0:T(8,128)(2,1)S(1)}, bf16[640,128]{1,0:T(8,128)(2,1)S(1)}, u32[]{:S(2)}, u32[]{:S(2)}) collective-permute-start(bf16[640,128]{1,0:T(8,128)(2,1)S(1)} %get-tuple-element.49), channel_id=1, source_target_pairs={{0,128},{16,144},{32,160},{48,176},{64,192},{80,208},{96,224},{112... | collective-permute-start | bytes 491528 | tf_op jit(solution)/shard_map/ppermute | solution.py:123
  65.7 14.5 %all-to-all-start.1 = ((bf16[8,256,128]{2,1,0:T(8,128)(2,1)}), bf16[8,256,128]{2,1,0:T(8,128)(2,1)S(1)}, u32[]{:S(2)}, u32[]{:S(2)}) async-start(bf16[8,256,128]{2,1,0:T(8,128)(2,1)} %bitcast.6), calls=%async_computation.1 | async-start | bytes 1048576 | tf_op jit(solution)/shard_map/all_to_all | solution.py:523
  70.9 8.4 %collective-permute-start.4 = (bf16[80,128]{1,0:T(8,128)(2,1)S(1)}, bf16[80,128]{1,0:T(8,128)(2,1)S(1)}, u32[]{:S(2)}, u32[]{:S(2)}) collective-permute-start(bf16[80,128]{1,0:T(8,128)(2,1)S(1)} %get-tuple-element.50), channel_id=1, source_target_pairs={{0,256},{16,272},{32,288},{48,304},{64,320},{80,336},{96,352},{112... | collective-permute-start | bytes 61448 | tf_op jit(solution)/shard_map/ppermute | solution.py:123
  80.2 21.2 %copy-start.2 = (bf16[2432,64]{0,1:T(8,128)(2,1)S(1)}, bf16[2432,64]{0,1:T(8,128)(2,1)}, u32[]{:S(2)}) copy-start(bf16[2432,64]{0,1:T(8,128)(2,1)} %param.30) | copy-start | bytes 933892
  80.2 21.2 %copy-start.3 = (f32[2,7296]{1,0:T(2,128)S(1)}, f32[2,7296]{1,0:T(2,128)}, u32[]{:S(2)}) copy-start(f32[2,7296]{1,0:T(2,128)} %modulate_ref.3) | copy-start | bytes 175108
  80.2 21.2 %copy-start.4 = (bf16[1,64,128]{2,1,0:T(8,128)(2,1)S(1)}, bf16[1,64,128]{2,1,0:T(8,128)(2,1)}, u32[]{:S(2)}) copy-start(bf16[1,64,128]{2,1,0:T(8,128)(2,1)} %param.31) | copy-start | bytes 49156
  84.8 16.6 %collective-permute-start.5 = (bf16[128,2432]{1,0:T(8,128)(2,1)S(1)}, bf16[128,2432]{1,0:T(8,128)(2,1)S(1)}, u32[]{:S(2)}, u32[]{:S(2)}) collective-permute-start(bf16[128,2432]{1,0:T(8,128)(2,1)S(1)} %get-tuple-element.33), channel_id=1, source_target_pairs={{0,8},{1,9},{2,10},{3,11},{4,12},{5,13},{6,14},{7,15},{8,0},{9,1},... | collective-permute-start | bytes 1867784 | tf_op jit(solution)/shard_map/ppermute | solution.py:123
  105.7 13.1 %all-to-all-start.2 = ((bf16[16,80,128]{2,1,0:T(8,128)(2,1)}), bf16[16,80,128]{2,1,0:T(8,128)(2,1)S(1)}, u32[]{:S(2)}, u32[]{:S(2)}) async-start(bf16[16,80,128]{2,1,0:T(8,128)(2,1)} %bitcast.15), calls=%async_computation.2 | async-start | bytes 655360 | tf_op jit(solution)/shard_map/all_to_all | solution.py:523
  111.1 1.3 copy-start.1
  113.8 26.6 %collective-permute-start.6 = (bf16[128,2432]{1,0:T(8,128)(2,1)S(1)}, bf16[128,2432]{1,0:T(8,128)(2,1)S(1)}, u32[]{:S(2)}, u32[]{:S(2)}) collective-permute-start(bf16[128,2432]{1,0:T(8,128)(2,1)S(1)} %shard_map.188.own_ref), channel_id=1, source_target_pairs={{0,8},{1,9},{2,10},{3,11},{4,12},{5,13},{6,14},{7,15},{8,0},{9,1},... | collective-permute-start | bytes 1867784 | tf_op jit(solution)/shard_map/ppermute | solution.py:123
  134.4 12.9 %all-to-all-start.4 = ((bf16[4,80,128]{2,1,0:T(8,128)(2,1)}), bf16[4,80,128]{2,1,0:T(8,128)(2,1)S(1)}, u32[]{:S(2)}, u32[]{:S(2)}) async-start(bf16[4,80,128]{2,1,0:T(8,128)(2,1)} %shard_map.192), calls=%async_computation.4 | async-start | bytes 163840 | tf_op jit(solution)/shard_map/all_to_all | solution.py:523
  140.4 2.4 %copy-start = (bf16[1024,2432]{1,0:T(8,128)(2,1)S(1)}, bf16[1024,2432]{1,0:T(8,128)(2,1)}, u32[]{:S(2)}) copy-start(bf16[1024,2432]{1,0:T(8,128)(2,1)} %all-gather.2.cloned.1.call-done.weight_ref) | copy-start | bytes 14942212
  148.1 19.8 %all-to-all-start.5 = ((bf16[16,80,128]{2,1,0:T(8,128)(2,1)}), bf16[16,80,128]{2,1,0:T(8,128)(2,1)S(1)}, u32[]{:S(2)}, u32[]{:S(2)}) async-start(bf16[16,80,128]{2,1,0:T(8,128)(2,1)} %shard_map.193), calls=%async_computation.5 | async-start | bytes 655360 | tf_op jit(solution)/shard_map/all_to_all | solution.py:523
  155.6 11.5 %collective-permute-start.7 = (bf16[128,1024]{1,0:T(8,128)(2,1)S(1)}, bf16[128,1024]{1,0:T(8,128)(2,1)S(1)}, u32[]{:S(2)}, u32[]{:S(2)}) collective-permute-start(bf16[128,1024]{1,0:T(8,128)(2,1)S(1)} %get-tuple-element.41), channel_id=1, source_target_pairs={{0,8},{1,9},{2,10},{3,11},{4,12},{5,13},{6,14},{7,15},{8,0},{9,1},... | collective-permute-start | bytes 786440 | tf_op jit(solution)/shard_map/ppermute | solution.py:123
Sparse Core Ops, SparseCore 0:
  10.1 56.9 all-gather.1

commit v7 on v6

--- a/solution.py
+++ b/solution.py
@@ -264,16 +264,15 @@
 
 
 def project_kernel(
-    block, half_ref, rows_ref, weight_ref, own_ref, other_ref, lined_ref, here_ref, semaphores
+    block, begin, half_ref, rows_ref, weight_ref, own_ref, other_ref, lined_ref, here_ref, semaphores
 ):
     tile, width = own_ref.shape
     whole = width // block
 
     def landing(at, size):
-        columns = pl.ds(pl.multiple_of(at * block, block), size)
-        return pltpu.make_async_copy(
-            weight_ref.at[:, columns], here_ref.at[:, columns], semaphores.at[at]
-        )
+        there = pl.ds(pl.multiple_of(begin + at * block, LANES), size)
+        here = pl.ds(pl.multiple_of(at * block, LANES), size)
+        return pltpu.make_async_copy(weight_ref.at[:, there], here_ref.at[:, here], semaphores.at[at])
 
     sizes = [block] * whole + ([width % block] if width % block else [])
     for at, size in enumerate(sizes):
@@ -299,11 +298,11 @@
         multiply(whole, width % block)
 
 
-def project(half, recv, weight, tile):
-    depth, width = weight.shape
+def project(half, recv, weight, tile, begin, width):
+    depth = weight.shape[0]
     block = 4 * LANES
     return pl.pallas_call(
-        functools.partial(project_kernel, block),
+        functools.partial(project_kernel, block, begin),
         out_shape=(
             jax.ShapeDtypeStruct((tile, width), jnp.float32),
             jax.ShapeDtypeStruct((tile, width), jnp.bfloat16),
@@ -316,15 +315,26 @@
             pltpu.SemaphoreType.DMA((pl.cdiv(width, block),)),
         ],
         compiler_params=params(52),
+        cost_estimate=pl.CostEstimate(
+            flops=4 * tile * depth * width, bytes_accessed=2 * depth * width, transcendentals=0
+        ),
     )(half, recv, weight)
 
 
 def head_kernel(
-    place_ref, counts_ref, own_ref, other_ref, residual_ref, modulate_ref, final_ref, noise_ref,
-    near_ref, far_ref, velocity_ref, parts_ref, total_ref, normed_ref, inverse_ref, grad_ref,
+    place_ref, counts_ref, own_left_ref, own_right_ref, other_left_ref, other_right_ref,
+    residual_ref, modulate_ref, final_ref, noise_ref, near_ref, far_ref, velocity_ref, parts_ref, total_ref, normed_ref, inverse_ref, grad_ref,
     own_here, other_here, residual_here, semaphores,
 ):
-    pairs = ((own_ref, own_here), (residual_ref, residual_here), (other_ref, other_here))
+    left = pl.ds(0, own_left_ref.shape[1])
+    right = pl.ds(own_left_ref.shape[1], own_right_ref.shape[1])
+    pairs = (
+        (own_left_ref, own_here.at[:, left]),
+        (own_right_ref, own_here.at[:, right]),
+        (residual_ref, residual_here),
+        (other_left_ref, other_here.at[:, left]),
+        (other_right_ref, other_here.at[:, right]),
+    )
     copies = [
         pltpu.make_async_copy(there, here, semaphores.at[at]) for at, (there, here) in enumerate(pairs)
     ]
@@ -379,16 +389,16 @@
             jax.ShapeDtypeStruct((tile, LANES), jnp.float32),
             jax.ShapeDtypeStruct((lat, tile), jnp.float32),
         ),
-        in_specs=[SMEM] * 2 + [HBM] * 3 + [VMEM] * 5,
+        in_specs=[SMEM] * 2 + [pl.BlockSpec(memory_space=pl.ANY)] * 5 + [VMEM] * 5,
         out_specs=(VMEM,) * 6,
         scratch_shapes=[
-            pltpu.VMEM(own.shape, own.dtype),
-            pltpu.VMEM(other.shape, other.dtype),
+            pltpu.VMEM(residual.shape, own[0].dtype),
+            pltpu.VMEM(residual.shape, other[0].dtype),
             pltpu.VMEM(residual.shape, residual.dtype),
-            pltpu.SemaphoreType.DMA((3,)),
+            pltpu.SemaphoreType.DMA((5,)),
         ],
         compiler_params=params(52),
-    )(place, counts, own, other, residual, modulate, final_columns, noise, near, far)
+    )(place, counts, *own, *other, residual, modulate, final_columns, noise, near, far)
 
 
 def grad_kernel(
@@ -561,8 +571,12 @@
     mine, other = land(held, tagged.shape[0], ranks)
     attended, mine, other = lax.optimization_barrier((attended, mine, other))
     final_columns = final_weight.T
-    own, across = project(half, attended, gathered, tile)
-    across = swap(across, sources, per_half, "seqt")
+    left = pl.cdiv(width, 2 * LANES) * LANES
+    own, across = [], []
+    for begin, size in ((0, left), (left, width - left)):
+        here, there = project(half, attended, gathered, tile, begin, size)
+        own.append(here)
+        across.append(swap(there, sources, per_half, "seqt"))
     velocity, parts, total, normed, inverse, grad_columns = head(
         place, image_tokens, own, across, residual, modulation, final_columns, noise_tiles[0],
         mine, other,
@@ -580,8 +594,9 @@
     sums = exchange(parts.reshape(blocks * lat_width, LANES), "seqt")
     sums, _ = lax.optimization_barrier((sums, grad_projected))
     sums = exchange(sum_out(sums, sources, near, loss_row, last), "dp", near_groups)
+    sums, _ = lax.optimization_barrier((sums, across_grad))
     sums = exchange(sum_out(sums, near, far, loss_row, last), "dp", far_groups)
-    sums, _ = lax.optimization_barrier((sums, across_grad))
+    sums, _ = lax.optimization_barrier((sums, swapped_grad))
     sums = exchange(sum_out(sums, far, sources, loss_row, last), "seqt")
     attention_grad = join(half, own_grad, swapped_grad)
     final_sums, loss = unpack(sums.reshape(blocks, lat_width, LANES), total, width)

time: 177 us -> 176 us (level)
  blocking collectives: 14.9 us -> 0 us
  starting transfers between devices: 68.4 us -> 76.6 us
  waiting for transfers between devices: 43.5 us -> 46 us
    all_to_all x1 -> x0, blocking collectives: 14.9 us -> none  [exchange(): lax.all_to_all(array, axis, split_axis=0, concat_axis=0, axis_index_group...]
    all_to_all x5 -> x6, waiting for transfers between devices: 4.84 us -> 16.2 us  [exchange(): lax.all_to_all(array, axis, split_axis=0, concat_axis=0, axis_index_group...]
    ppermute x8 -> x9, waiting for transfers between devices: 37.9 us -> 29.1 us  [swap(): lax.ppermute(array, axis, [(rank, rank ^ step) for rank in range(ranks)])]
    all_to_all x5 -> x6, starting transfers between devices: 34.4 us -> 40.5 us  [exchange(): lax.all_to_all(array, axis, split_axis=0, concat_axis=0, axis_index_group...]
    ppermute x8 -> x9, starting transfers between devices: 34 us -> 36.1 us  [swap(): lax.ppermute(array, axis, [(rank, rank ^ step) for rank in range(ranks)])]
    unnamed x24 -> x28, local copies, waits for them, and re-layouts: 3.81 us -> 5.44 us
    pallas_call x1 -> x2, Pallas kernels: 4.6 us -> 4.89 us  [project(): pl.pallas_call(functools.partial(project_kernel, block, begin), out_shape...]
  transfers between devices with their start and end apart: 14 -> 16, of which waited for: 10 -> 12; matrix products, arithmetic and copies ran while one was open for 0% -> 0% of each run, Pallas kernels for 11% -> 13%
where the time goes in v7:
time: 176 us; the launch traced here: 175 us
  starting transfers between devices  76.6 us (44%)
  waiting for transfers between devices  46 us (26%)
  Pallas kernels  31 us (18%)
  between operations  15 us (9%)
  local copies, waits for them, and re-layouts  5.98 us (3%)
    all_to_all x6, starting transfers between devices, exchange(): lax.all_to_all(array, axis, split_axis=0, concat_axis=0, axis_index_group...  40.5 us
    ppermute x9, starting transfers between devices, swap(): lax.ppermute(array, axis, [(rank, rank ^ step) for rank in range(ranks)])  36.1 us
    ppermute x9, waiting for transfers between devices, swap(): lax.ppermute(array, axis, [(rank, rank ^ step) for rank in range(ranks)])  29.1 us
    all_to_all x6, waiting for transfers between devices, exchange(): lax.all_to_all(array, axis, split_axis=0, concat_axis=0, axis_index_group...  16.2 us
    pallas_call x1, Pallas kernels, attention(): pl.pallas_call(functools.partial(attention_kernel, sources, tile, text_ro...  10.4 us
    unnamed x28, local copies, waits for them, and re-layouts  5.44 us
    pallas_call x2, Pallas kernels, project(): pl.pallas_call(functools.partial(project_kernel, block, begin), out_shape...  4.89 us
    pallas_call x1, Pallas kernels, head(): pl.pallas_call(head_kernel, out_shape=(jax.ShapeDtypeStruct((lat, tile),...  4.39 us
  transfers between devices with their start and end apart: 16, of which 12 were waited for; matrix products, arithmetic and copies ran while one was open for 0% of the time, Pallas kernels for 13%

profile of v7, /device:TPU:1, one launch (start us, length us, event | category | flops | bytes accessed | tf_op | source)
XLA Modules:
  0.0 174.7 jit_solution(16557534343007269566)
XLA Ops:
  7.2 0.0 all-gather.2.cloned.1.call-start
  7.2 0.7 all-gather.2.cloned.1.call-update
  8.5 3.6 %shard_map.183 = (bf16[6656,128]{1,0:T(8,128)(2,1)}, bf16[80,128]{1,0:T(8,128)(2,1)}) custom-call(s32[1]{0:T(128)S(6)} %copy.27.route_ref, s32[1,2]{1,0:T(1,128)} %counts_ref.7, bf16[1,64,128]{2,1,0:T(8,128)(2,1)} %tile_ref.1, bf16[128,2048]{1,0:T(8,128)(2,1)} %refs_0_.1, bf16[128,2048]{1,0:T(8,128)(2,1)} %refs_1_.1, bf16[128,2048]{1,0:T(8,128)(2,1)} %refs_2_.1, ...), custom_call_target="tpu_custom_call" | custom-call | tf_op jit(solution)/shard_map/pallas_call | solution.py:62
  12.2 10.5 %all-to-all-start = ((bf16[16,416,128]{2,1,0:T(8,128)(2,1)}), bf16[16,416,128]{2,1,0:T(8,128)(2,1)S(1)}, u32[]{:S(2)}, u32[]{:S(2)}) async-start(bf16[16,416,128]{2,1,0:T(8,128)(2,1)} %bitcast.36), calls=%async_computation | async-start | bytes 3407872 | tf_op jit(solution)/shard_map/all_to_all | solution.py:533
  22.8 7.1 %collective-permute-start = (bf16[80,128]{1,0:T(8,128)(2,1)S(1)}, bf16[80,128]{1,0:T(8,128)(2,1)S(1)}, u32[]{:S(2)}, u32[]{:S(2)}) collective-permute-start(bf16[80,128]{1,0:T(8,128)(2,1)S(1)} %copy-done.9), channel_id=1, source_target_pairs={{0,64},{16,80},{32,96},{48,112},{64,0},{80,16},{96,32},{112,48},{1... | collective-permute-start | bytes 61448 | tf_op jit(solution)/shard_map/ppermute | solution.py:123
  29.9 1.4 collective-permute-done
  31.3 3.8 %collective-permute-start.1 = (bf16[160,128]{1,0:T(8,128)(2,1)S(1)}, bf16[160,128]{1,0:T(8,128)(2,1)S(1)}, u32[]{:S(2)}, u32[]{:S(2)}) collective-permute-start(bf16[160,128]{1,0:T(8,128)(2,1)S(1)} %pad_maximum_fusion.1), channel_id=1, source_target_pairs={{0,32},{16,48},{32,0},{48,16},{64,96},{80,112},{96,64},{112,80},{1... | collective-permute-start | bytes 122888 | tf_op jit(solution)/shard_map/ppermute | solution.py:123
  35.1 2.1 %collective-permute-done.1 = bf16[160,128]{1,0:T(8,128)(2,1)S(1)} collective-permute-done((bf16[160,128]{1,0:T(8,128)(2,1)S(1)}, bf16[160,128]{1,0:T(8,128)(2,1)S(1)}, u32[]{:S(2)}, u32[]{:S(2)}) %collective-permute-start.1) | collective-permute-done | bytes 40992 | tf_op jit(solution)/shard_map/ppermute | solution.py:123
  37.2 2.8 %collective-permute-start.2 = (bf16[320,128]{1,0:T(8,128)(2,1)S(1)}, bf16[320,128]{1,0:T(8,128)(2,1)S(1)}, u32[]{:S(2)}, u32[]{:S(2)}) collective-permute-start(bf16[320,128]{1,0:T(8,128)(2,1)S(1)} %pad_maximum_fusion), channel_id=1, source_target_pairs={{0,16},{16,0},{32,48},{48,32},{64,80},{80,64},{96,112},{112,96},{1... | collective-permute-start | bytes 245768 | tf_op jit(solution)/shard_map/ppermute | solution.py:123
  40.1 2.7 %collective-permute-done.2 = bf16[320,128]{1,0:T(8,128)(2,1)S(1)} collective-permute-done((bf16[320,128]{1,0:T(8,128)(2,1)S(1)}, bf16[320,128]{1,0:T(8,128)(2,1)S(1)}, u32[]{:S(2)}, u32[]{:S(2)}) %collective-permute-start.2) | collective-permute-done | bytes 81952 | tf_op jit(solution)/shard_map/ppermute | solution.py:123
  42.8 5.2 %collective-permute-start.3 = (bf16[640,128]{1,0:T(8,128)(2,1)S(1)}, bf16[640,128]{1,0:T(8,128)(2,1)S(1)}, u32[]{:S(2)}, u32[]{:S(2)}) collective-permute-start(bf16[640,128]{1,0:T(8,128)(2,1)S(1)} %get-tuple-element.55), channel_id=1, source_target_pairs={{0,128},{16,144},{32,160},{48,176},{64,192},{80,208},{96,224},{112... | collective-permute-start | bytes 491528 | tf_op jit(solution)/shard_map/ppermute | solution.py:123
  48.0 0.1 maximum_bitcast_fusion
  48.1 7.1 %collective-permute-done.3 = bf16[640,128]{1,0:T(8,128)(2,1)S(1)} collective-permute-done((bf16[640,128]{1,0:T(8,128)(2,1)S(1)}, bf16[640,128]{1,0:T(8,128)(2,1)S(1)}, u32[]{:S(2)}, u32[]{:S(2)}) %collective-permute-start.3) | collective-permute-done | bytes 163872 | tf_op jit(solution)/shard_map/ppermute | solution.py:123
  55.2 10.4 %shard_map.184 = bf16[2048,128]{1,0:T(8,128)(2,1)} custom-call(s32[1,2]{1,0:T(1,128)S(1)} %copy-done.7, s32[1,2]{1,0:T(1,128)S(1)} %copy-done.8, bf16[6656,128]{1,0:T(8,128)(2,1)S(1)} %bitcast.28, f32[1,128]{1,0:T(1,128)S(1)} %get-tuple-element.64.query_gain_ref, f32[1,128]{1,0:T(1,128)S(1)} %get-tuple-element.65.key_gain_ref), custom_call_target="tpu_custom_call" | custom-call | flops 4831838208 | bytes 4194304 | tf_op jit(solution)/shard_map/pallas_call | solution.py:221
  65.7 5.0 %all-to-all-start.1 = ((bf16[8,256,128]{2,1,0:T(8,128)(2,1)}), bf16[8,256,128]{2,1,0:T(8,128)(2,1)S(1)}, u32[]{:S(2)}, u32[]{:S(2)}) async-start(bf16[8,256,128]{2,1,0:T(8,128)(2,1)} %bitcast.6), calls=%async_computation.1 | async-start | bytes 1048576 | tf_op jit(solution)/shard_map/all_to_all | solution.py:533
  70.7 0.1 shard_map.185
  70.9 5.6 %collective-permute-start.4 = (bf16[80,128]{1,0:T(8,128)(2,1)S(1)}, bf16[80,128]{1,0:T(8,128)(2,1)S(1)}, u32[]{:S(2)}, u32[]{:S(2)}) collective-permute-start(bf16[80,128]{1,0:T(8,128)(2,1)S(1)} %get-tuple-element.56), channel_id=1, source_target_pairs={{0,256},{16,272},{32,288},{48,304},{64,320},{80,336},{96,352},{112... | collective-permute-start | bytes 61448 | tf_op jit(solution)/shard_map/ppermute | solution.py:123
  76.5 2.8 %collective-permute-done.4.far_ref = bf16[80,128]{1,0:T(8,128)(2,1)S(1)} collective-permute-done((bf16[80,128]{1,0:T(8,128)(2,1)S(1)}, bf16[80,128]{1,0:T(8,128)(2,1)S(1)}, u32[]{:S(2)}, u32[]{:S(2)}) %collective-permute-start.4) | collective-permute-done | bytes 20512 | tf_op jit(solution)/shard_map/ppermute | solution.py:123
  79.3 0.9 all-to-all-done.1
  80.2 2.5 %shard_map.186 = (f32[128,1280]{1,0:T(8,128)S(1)}, bf16[128,1280]{1,0:T(8,128)(2,1)S(1)}) custom-call(s32[1]{0:T(128)} %bitcast.1.half_ref, bf16[2048,128]{1,0:T(8,128)(2,1)S(1)} %bitcast.26, bf16[1024,2432]{1,0:T(8,128)(2,1)} %all-gather.2.cloned.1.call-done.weight_ref), custom_call_target="tpu_custom_call" | custom-call | flops 671088640 | bytes 2621440 | tf_op jit(solution)/shard_map/pallas_call | solution.py:304
  82.6 0.8 copy-done.3
  83.5 2.1 %collective-permute-start.5 = (bf16[128,1280]{1,0:T(8,128)(2,1)S(1)}, bf16[128,1280]{1,0:T(8,128)(2,1)S(1)}, u32[]{:S(2)}, u32[]{:S(2)}) collective-permute-start(bf16[128,1280]{1,0:T(8,128)(2,1)S(1)} %get-tuple-element.37), channel_id=1, source_target_pairs={{0,8},{1,9},{2,10},{3,11},{4,12},{5,13},{6,14},{7,15},{8,0},{9,1},... | collective-permute-start | bytes 983048 | tf_op jit(solution)/shard_map/ppermute | solution.py:123
  85.6 2.4 %shard_map.187 = (f32[128,1152]{1,0:T(8,128)S(1)}, bf16[128,1152]{1,0:T(8,128)(2,1)S(1)}) custom-call(s32[1]{0:T(128)} %bitcast.1.half_ref, bf16[2048,128]{1,0:T(8,128)(2,1)S(1)} %bitcast.27, bf16[1024,2432]{1,0:T(8,128)(2,1)} %all-gather.2.cloned.1.call-done.weight_ref), custom_call_target="tpu_custom_call" | custom-call | flops 603979776 | bytes 2359296 | tf_op jit(solution)/shard_map/pallas_call | solution.py:304
  88.1 0.8 copy-done.4
  88.9 3.2 %collective-permute-start.6 = (bf16[128,1152]{1,0:T(8,128)(2,1)S(1)}, bf16[128,1152]{1,0:T(8,128)(2,1)S(1)}, u32[]{:S(2)}, u32[]{:S(2)}) collective-permute-start(bf16[128,1152]{1,0:T(8,128)(2,1)S(1)} %get-tuple-element.38), channel_id=1, source_target_pairs={{0,8},{1,9},{2,10},{3,11},{4,12},{5,13},{6,14},{7,15},{8,0},{9,1},... | collective-permute-start | bytes 884744 | tf_op jit(solution)/shard_map/ppermute | solution.py:123
  92.1 8.0 %collective-permute-done.6.other_right_ref = bf16[128,1152]{1,0:T(8,128)(2,1)S(1)} collective-permute-done((bf16[128,1152]{1,0:T(8,128)(2,1)S(1)}, bf16[128,1152]{1,0:T(8,128)(2,1)S(1)}, u32[]{:S(2)}, u32[]{:S(2)}) %collective-permute-start.6) | collective-permute-done | bytes 294944 | tf_op jit(solution)/shard_map/ppermute | solution.py:123
  100.2 4.4 %shard_map.188 = (f32[64,128]{1,0:T(8,128)}, bf16[20,64,128]{2,1,0:T(8,128)(2,1)}, f32[8,128]{1,0:T(8,128)S(1)}, f32[128,2432]{1,0:T(8,128)}, f32[128,128]{1,0:T(8,128)S(1)}, /*index=5*/f32[64,128]{1,0:T(8,128)S(1)}) custom-call(s32[1]{0:T(128)} %bitcast.place_ref, s32[1,2]{1,0:T(1,128)S(1)} %copy-done.7, f32[128,1280]{1,0:T(8,128)} %copy-done.3, ...), custom_call_target="tpu_custom_call" | custom-call | tf_op jit(solution)/shard_map/pallas_call | solution.py:382
  104.6 5.3 %all-to-all-start.2 = ((bf16[16,80,128]{2,1,0:T(8,128)(2,1)}), bf16[16,80,128]{2,1,0:T(8,128)(2,1)S(1)}, u32[]{:S(2)}, u32[]{:S(2)}) async-start(bf16[16,80,128]{2,1,0:T(8,128)(2,1)} %bitcast.15), calls=%async_computation.2 | async-start | bytes 655360 | tf_op jit(solution)/shard_map/all_to_all | solution.py:533
  109.9 1.3 copy-done.1
  111.2 1.4 shard_map.189.own_ref
  112.6 3.3 %collective-permute-start.7 = (bf16[128,2432]{1,0:T(8,128)(2,1)S(1)}, bf16[128,2432]{1,0:T(8,128)(2,1)S(1)}, u32[]{:S(2)}, u32[]{:S(2)}) collective-permute-start(bf16[128,2432]{1,0:T(8,128)(2,1)S(1)} %shard_map.189.own_ref), channel_id=1, source_target_pairs={{0,8},{1,9},{2,10},{3,11},{4,12},{5,13},{6,14},{7,15},{8,0},{9,1},... | collective-permute-start | bytes 1867784 | tf_op jit(solution)/shard_map/ppermute | solution.py:123
  115.9 1.7 all-to-all-done.2
  117.6 0.7 shard_map.192
  118.3 7.0 %all-to-all-start.3 = ((bf16[8,80,128]{2,1,0:T(8,128)(2,1)}), bf16[8,80,128]{2,1,0:T(8,128)(2,1)S(1)}, u32[]{:S(2)}, u32[]{:S(2)}) async-start(bf16[8,80,128]{2,1,0:T(8,128)(2,1)} %shard_map.192), calls=%async_computation.3 | async-start | bytes 327680 | tf_op jit(solution)/shard_map/all_to_all | solution.py:533
  125.3 4.7 %collective-permute-done.7.other_ref = bf16[128,2432]{1,0:T(8,128)(2,1)S(1)} collective-permute-done((bf16[128,2432]{1,0:T(8,128)(2,1)S(1)}, bf16[128,2432]{1,0:T(8,128)(2,1)S(1)}, u32[]{:S(2)}, u32[]{:S(2)}) %collective-permute-start.7) | collective-permute-done | bytes 622624 | tf_op jit(solution)/shard_map/ppermute | solution.py:123
  130.1 2.4 %copy-done = bf16[1024,2432]{1,0:T(8,128)(2,1)S(1)} copy-done((bf16[1024,2432]{1,0:T(8,128)(2,1)S(1)}, bf16[1024,2432]{1,0:T(8,128)(2,1)}, u32[]{:S(2)}) %copy-start) | copy-done | bytes 4980760
  132.5 2.3 %shard_map.190 = (bf16[128,1024]{1,0:T(8,128)(2,1)S(1)}, bf16[128,1024]{1,0:T(8,128)(2,1)S(1)}) custom-call(bf16[128,2432]{1,0:T(8,128)(2,1)S(1)} %shard_map.189.own_ref, bf16[128,2432]{1,0:T(8,128)(2,1)S(1)} %collective-permute-done.7.other_ref, bf16[1024,2432]{1,0:T(8,128)(2,1)S(1)} %copy-done), custom_call_target="tpu_custom_call" | custom-call | flops 1275068416 | bytes 4980736 | tf_op jit(solution)/shard_map/pallas_call | solution.py:447
  134.8 3.0 %collective-permute-start.8 = (bf16[128,1024]{1,0:T(8,128)(2,1)S(1)}, bf16[128,1024]{1,0:T(8,128)(2,1)S(1)}, u32[]{:S(2)}, u32[]{:S(2)}) collective-permute-start(bf16[128,1024]{1,0:T(8,128)(2,1)S(1)} %get-tuple-element.46), channel_id=1, source_target_pairs={{0,8},{1,9},{2,10},{3,11},{4,12},{5,13},{6,14},{7,15},{8,0},{9,1},... | collective-permute-start | bytes 786440 | tf_op jit(solution)/shard_map/ppermute | solution.py:123
  137.8 0.7 shard_map.193
  138.5 5.0 %all-to-all-start.4 = ((bf16[4,80,128]{2,1,0:T(8,128)(2,1)}), bf16[4,80,128]{2,1,0:T(8,128)(2,1)S(1)}, u32[]{:S(2)}, u32[]{:S(2)}) async-start(bf16[4,80,128]{2,1,0:T(8,128)(2,1)} %shard_map.193), calls=%async_computation.4 | async-start | bytes 163840 | tf_op jit(solution)/shard_map/all_to_all | solution.py:533
  143.4 0.2 collective-permute-done.8.other_ref
  143.7 6.7 %all-to-all-done.4 = bf16[4,80,128]{2,1,0:T(8,128)(2,1)S(1)} async-done(((bf16[4,80,128]{2,1,0:T(8,128)(2,1)}), bf16[4,80,128]{2,1,0:T(8,128)(2,1)S(1)}, u32[]{:S(2)}, u32[]{:S(2)}) %all-to-all-start.4) | async-done | bytes 81952 | tf_op jit(solution)/shard_map/all_to_all | solution.py:533
  150.4 0.8 shard_map.194
  151.2 7.6 %all-to-all-start.5 = ((bf16[16,80,128]{2,1,0:T(8,128)(2,1)}), bf16[16,80,128]{2,1,0:T(8,128)(2,1)S(1)}, u32[]{:S(2)}, u32[]{:S(2)}) async-start(bf16[16,80,128]{2,1,0:T(8,128)(2,1)} %shard_map.194), calls=%async_computation.5 | async-start | bytes 655360 | tf_op jit(solution)/shard_map/all_to_all | solution.py:533
  158.7 0.8 shard_map.191
  159.6 6.9 %all-to-all-done.5 = bf16[16,80,128]{2,1,0:T(8,128)(2,1)S(1)} async-done(((bf16[16,80,128]{2,1,0:T(8,128)(2,1)}), bf16[16,80,128]{2,1,0:T(8,128)(2,1)S(1)}, u32[]{:S(2)}, u32[]{:S(2)}) %all-to-all-start.5) | async-done | bytes 327712 | tf_op jit(solution)/shard_map/all_to_all | solution.py:533
  166.4 0.9 shard_map.195
  167.3 0.5 slice.11
  (32 shorter events, 0.2 us)
Async XLA Ops:
  7.2 73.0 %all-gather.2.cloned.1.call-start = ((), (), s32[]{:S(2)}) async-start(), calls=%async_computation.6 | async-start | bytes 5603328 | tf_op jit(solution)/shard_map/all_gather | solution.py:557
  12.2 10.6 %copy-start.9 = (bf16[80,128]{1,0:T(8,128)(2,1)S(1)}, bf16[80,128]{1,0:T(8,128)(2,1)}, u32[]{:S(2)}) copy-start(bf16[80,128]{1,0:T(8,128)(2,1)} %get-tuple-element.30) | copy-start | bytes 61444
  12.2 35.8 %copy-start.10 = (f32[64]{0:T(128)S(1)}, f32[64]{0:T(128)}, u32[]{:S(2)}) copy-start(f32[64]{0:T(128)} %param.25) | copy-start | bytes 772
  12.2 35.8 %copy-start.11 = (f32[64]{0:T(128)S(1)}, f32[64]{0:T(128)}, u32[]{:S(2)}) copy-start(f32[64]{0:T(128)} %param.26) | copy-start | bytes 772
  12.2 43.0 %copy-start.7 = (s32[1,2]{1,0:T(1,128)S(1)}, s32[1,2]{1,0:T(1,128)}, u32[]{:S(2)}) copy-start(s32[1,2]{1,0:T(1,128)} %counts_ref.7) | copy-start | bytes 28
  12.2 43.0 %copy-start.8 = (s32[1,2]{1,0:T(1,128)S(1)}, s32[1,2]{1,0:T(1,128)}, u32[]{:S(2)}) copy-start(s32[1,2]{1,0:T(1,128)} %lengths_ref.1) | copy-start | bytes 28
  12.2 43.0 %all-to-all-start = ((bf16[16,416,128]{2,1,0:T(8,128)(2,1)}), bf16[16,416,128]{2,1,0:T(8,128)(2,1)S(1)}, u32[]{:S(2)}, u32[]{:S(2)}) async-start(bf16[16,416,128]{2,1,0:T(8,128)(2,1)} %bitcast.36), calls=%async_computation | async-start | bytes 3407872 | tf_op jit(solution)/shard_map/all_to_all | solution.py:533
  22.8 8.5 %collective-permute-start = (bf16[80,128]{1,0:T(8,128)(2,1)S(1)}, bf16[80,128]{1,0:T(8,128)(2,1)S(1)}, u32[]{:S(2)}, u32[]{:S(2)}) collective-permute-start(bf16[80,128]{1,0:T(8,128)(2,1)S(1)} %copy-done.9), channel_id=1, source_target_pairs={{0,64},{16,80},{32,96},{48,112},{64,0},{80,16},{96,32},{112,48},{1... | collective-permute-start | bytes 61448 | tf_op jit(solution)/shard_map/ppermute | solution.py:123
  31.3 5.9 %collective-permute-start.1 = (bf16[160,128]{1,0:T(8,128)(2,1)S(1)}, bf16[160,128]{1,0:T(8,128)(2,1)S(1)}, u32[]{:S(2)}, u32[]{:S(2)}) collective-permute-start(bf16[160,128]{1,0:T(8,128)(2,1)S(1)} %pad_maximum_fusion.1), channel_id=1, source_target_pairs={{0,32},{16,48},{32,0},{48,16},{64,96},{80,112},{96,64},{112,80},{1... | collective-permute-start | bytes 122888 | tf_op jit(solution)/shard_map/ppermute | solution.py:123
  37.2 5.6 %collective-permute-start.2 = (bf16[320,128]{1,0:T(8,128)(2,1)S(1)}, bf16[320,128]{1,0:T(8,128)(2,1)S(1)}, u32[]{:S(2)}, u32[]{:S(2)}) collective-permute-start(bf16[320,128]{1,0:T(8,128)(2,1)S(1)} %pad_maximum_fusion), channel_id=1, source_target_pairs={{0,16},{16,0},{32,48},{48,32},{64,80},{80,64},{96,112},{112,96},{1... | collective-permute-start | bytes 245768 | tf_op jit(solution)/shard_map/ppermute | solution.py:123
  42.8 12.3 %collective-permute-start.3 = (bf16[640,128]{1,0:T(8,128)(2,1)S(1)}, bf16[640,128]{1,0:T(8,128)(2,1)S(1)}, u32[]{:S(2)}, u32[]{:S(2)}) collective-permute-start(bf16[640,128]{1,0:T(8,128)(2,1)S(1)} %get-tuple-element.55), channel_id=1, source_target_pairs={{0,128},{16,144},{32,160},{48,176},{64,192},{80,208},{96,224},{112... | collective-permute-start | bytes 491528 | tf_op jit(solution)/shard_map/ppermute | solution.py:123
  65.7 14.5 %all-to-all-start.1 = ((bf16[8,256,128]{2,1,0:T(8,128)(2,1)}), bf16[8,256,128]{2,1,0:T(8,128)(2,1)S(1)}, u32[]{:S(2)}, u32[]{:S(2)}) async-start(bf16[8,256,128]{2,1,0:T(8,128)(2,1)} %bitcast.6), calls=%async_computation.1 | async-start | bytes 1048576 | tf_op jit(solution)/shard_map/all_to_all | solution.py:533
  70.9 8.4 %collective-permute-start.4 = (bf16[80,128]{1,0:T(8,128)(2,1)S(1)}, bf16[80,128]{1,0:T(8,128)(2,1)S(1)}, u32[]{:S(2)}, u32[]{:S(2)}) collective-permute-start(bf16[80,128]{1,0:T(8,128)(2,1)S(1)} %get-tuple-element.56), channel_id=1, source_target_pairs={{0,256},{16,272},{32,288},{48,304},{64,320},{80,336},{96,352},{112... | collective-permute-start | bytes 61448 | tf_op jit(solution)/shard_map/ppermute | solution.py:123
  82.6 0.8 copy-start.3
  83.5 16.7 %copy-start.2 = (bf16[2432,64]{0,1:T(8,128)(2,1)S(1)}, bf16[2432,64]{0,1:T(8,128)(2,1)}, u32[]{:S(2)}) copy-start(bf16[2432,64]{0,1:T(8,128)(2,1)} %param.30) | copy-start | bytes 933892
  83.5 16.7 %copy-start.5 = (f32[2,7296]{1,0:T(2,128)S(1)}, f32[2,7296]{1,0:T(2,128)}, u32[]{:S(2)}) copy-start(f32[2,7296]{1,0:T(2,128)} %modulate_ref.3) | copy-start | bytes 175108
  83.5 16.7 %copy-start.6 = (bf16[1,64,128]{2,1,0:T(8,128)(2,1)S(1)}, bf16[1,64,128]{2,1,0:T(8,128)(2,1)}, u32[]{:S(2)}) copy-start(bf16[1,64,128]{2,1,0:T(8,128)(2,1)} %param.31) | copy-start | bytes 49156
  83.5 16.7 %collective-permute-start.5 = (bf16[128,1280]{1,0:T(8,128)(2,1)S(1)}, bf16[128,1280]{1,0:T(8,128)(2,1)S(1)}, u32[]{:S(2)}, u32[]{:S(2)}) collective-permute-start(bf16[128,1280]{1,0:T(8,128)(2,1)S(1)} %get-tuple-element.37), channel_id=1, source_target_pairs={{0,8},{1,9},{2,10},{3,11},{4,12},{5,13},{6,14},{7,15},{8,0},{9,1},... | collective-permute-start | bytes 983048 | tf_op jit(solution)/shard_map/ppermute | solution.py:123
  88.1 0.8 copy-start.4
  88.9 11.3 %collective-permute-start.6 = (bf16[128,1152]{1,0:T(8,128)(2,1)S(1)}, bf16[128,1152]{1,0:T(8,128)(2,1)S(1)}, u32[]{:S(2)}, u32[]{:S(2)}) collective-permute-start(bf16[128,1152]{1,0:T(8,128)(2,1)S(1)} %get-tuple-element.38), channel_id=1, source_target_pairs={{0,8},{1,9},{2,10},{3,11},{4,12},{5,13},{6,14},{7,15},{8,0},{9,1},... | collective-permute-start | bytes 884744 | tf_op jit(solution)/shard_map/ppermute | solution.py:123
  104.6 13.0 %all-to-all-start.2 = ((bf16[16,80,128]{2,1,0:T(8,128)(2,1)}), bf16[16,80,128]{2,1,0:T(8,128)(2,1)S(1)}, u32[]{:S(2)}, u32[]{:S(2)}) async-start(bf16[16,80,128]{2,1,0:T(8,128)(2,1)} %bitcast.15), calls=%async_computation.2 | async-start | bytes 655360 | tf_op jit(solution)/shard_map/all_to_all | solution.py:533
  109.9 1.3 copy-start.1
  112.6 17.5 %collective-permute-start.7 = (bf16[128,2432]{1,0:T(8,128)(2,1)S(1)}, bf16[128,2432]{1,0:T(8,128)(2,1)S(1)}, u32[]{:S(2)}, u32[]{:S(2)}) collective-permute-start(bf16[128,2432]{1,0:T(8,128)(2,1)S(1)} %shard_map.189.own_ref), channel_id=1, source_target_pairs={{0,8},{1,9},{2,10},{3,11},{4,12},{5,13},{6,14},{7,15},{8,0},{9,1},... | collective-permute-start | bytes 1867784 | tf_op jit(solution)/shard_map/ppermute | solution.py:123
  118.3 19.5 %all-to-all-start.3 = ((bf16[8,80,128]{2,1,0:T(8,128)(2,1)}), bf16[8,80,128]{2,1,0:T(8,128)(2,1)S(1)}, u32[]{:S(2)}, u32[]{:S(2)}) async-start(bf16[8,80,128]{2,1,0:T(8,128)(2,1)} %shard_map.192), calls=%async_computation.3 | async-start | bytes 327680 | tf_op jit(solution)/shard_map/all_to_all | solution.py:533
  130.1 2.4 %copy-start = (bf16[1024,2432]{1,0:T(8,128)(2,1)S(1)}, bf16[1024,2432]{1,0:T(8,128)(2,1)}, u32[]{:S(2)}) copy-start(bf16[1024,2432]{1,0:T(8,128)(2,1)} %all-gather.2.cloned.1.call-done.weight_ref) | copy-start | bytes 14942212
  134.8 8.8 %collective-permute-start.8 = (bf16[128,1024]{1,0:T(8,128)(2,1)S(1)}, bf16[128,1024]{1,0:T(8,128)(2,1)S(1)}, u32[]{:S(2)}, u32[]{:S(2)}) collective-permute-start(bf16[128,1024]{1,0:T(8,128)(2,1)S(1)} %get-tuple-element.46), channel_id=1, source_target_pairs={{0,8},{1,9},{2,10},{3,11},{4,12},{5,13},{6,14},{7,15},{8,0},{9,1},... | collective-permute-start | bytes 786440 | tf_op jit(solution)/shard_map/ppermute | solution.py:123
  138.5 11.9 %all-to-all-start.4 = ((bf16[4,80,128]{2,1,0:T(8,128)(2,1)}), bf16[4,80,128]{2,1,0:T(8,128)(2,1)S(1)}, u32[]{:S(2)}, u32[]{:S(2)}) async-start(bf16[4,80,128]{2,1,0:T(8,128)(2,1)} %shard_map.193), calls=%async_computation.4 | async-start | bytes 163840 | tf_op jit(solution)/shard_map/all_to_all | solution.py:533
  151.2 15.3 %all-to-all-start.5 = ((bf16[16,80,128]{2,1,0:T(8,128)(2,1)}), bf16[16,80,128]{2,1,0:T(8,128)(2,1)S(1)}, u32[]{:S(2)}, u32[]{:S(2)}) async-start(bf16[16,80,128]{2,1,0:T(8,128)(2,1)} %shard_map.194), calls=%async_computation.5 | async-start | bytes 655360 | tf_op jit(solution)/shard_map/all_to_all | solution.py:533
Sparse Core Ops, SparseCore 0:
  10.1 56.9 all-gather.1

commit v8 on v7

--- a/solution.py
+++ b/solution.py
@@ -426,38 +426,27 @@
     )(place, counts, grad_columns, normed, inverse, modulate, final_columns)
 
 
-def back_kernel(own_ref, other_ref, weight_ref, own_out_ref, other_out_ref, both_ref):
-    tile = own_ref.shape[0]
-
-    @pl.when(pl.program_id(0) == 0)
-    def _():
-        both_ref[:tile, :] = own_ref[...]
-        both_ref[tile:, :] = other_ref[...]
-
-    product = lax.dot_general(both_ref[...], weight_ref[...], NT, preferred_element_type=jnp.float32)
-    own_out_ref[...] = product[:tile].astype(jnp.bfloat16)
-    other_out_ref[...] = product[tile:].astype(jnp.bfloat16)
-
-
-def back(own, other, weight):
-    tile, width = own.shape
+def back_kernel(grad_ref, weight_ref, out_ref):
+    product = lax.dot_general(grad_ref[...], weight_ref[...], NT, preferred_element_type=jnp.float32)
+    out_ref[...] = product.astype(jnp.bfloat16)
+
+
+def back(grad, weight):
+    tile, width = grad.shape
     depth = 2 * LANES
-    out = jax.ShapeDtypeStruct((tile, weight.shape[0]), jnp.bfloat16)
-    out_spec = pl.BlockSpec((tile, depth), lambda i: (0, i))
     return pl.pallas_call(
         back_kernel,
         grid=(weight.shape[0] // depth,),
-        out_shape=(out, out),
-        in_specs=[VMEM, VMEM, pl.BlockSpec((depth, width), lambda i: (i, 0))],
-        out_specs=(out_spec, out_spec),
-        scratch_shapes=[pltpu.VMEM((2 * tile, width), jnp.bfloat16)],
+        out_shape=jax.ShapeDtypeStruct((tile, weight.shape[0]), jnp.bfloat16),
+        in_specs=[VMEM, pl.BlockSpec((depth, width), lambda i: (i, 0))],
+        out_specs=pl.BlockSpec((tile, depth), lambda i: (0, i)),
         compiler_params=params(24, ("arbitrary",)),
         cost_estimate=pl.CostEstimate(
-            flops=4 * tile * width * weight.shape[0],
+            flops=2 * tile * width * weight.shape[0],
             bytes_accessed=2 * width * weight.shape[0],
             transcendentals=0,
         ),
-    )(own, other, weight)
+    )(grad, weight)
 
 
 def join_kernel(half_ref, own_ref, other_ref, out_ref):
@@ -589,7 +578,9 @@
     loss_row = (blocks - 1) * lat_width - (sources - 1) * share
     last = (column_index == sources - 1).astype(jnp.int32).reshape(1)
     partner_grad = swap(grad_projected, sources, per_half, "seqt")
-    own_grad, across_grad = back(grad_projected, partner_grad, gathered)
+    own_grad = back(grad_projected, gathered)
+    own_grad, partner_grad = lax.optimization_barrier((own_grad, partner_grad))
+    across_grad = back(partner_grad, gathered)
     swapped_grad = swap(across_grad, sources, per_half, "seqt")
     sums = exchange(parts.reshape(blocks * lat_width, LANES), "seqt")
     sums, _ = lax.optimization_barrier((sums, grad_projected))

time: 176 us -> 174 us (0.989)
  waiting for transfers between devices: 46 us -> 41.7 us
  Pallas kernels: 31 us -> 33.1 us
    ppermute x9, waiting for transfers between devices: 29.1 us -> 24.4 us  [swap(): lax.ppermute(array, axis, [(rank, rank ^ step) for rank in range(ranks)])]
    pallas_call x1 -> x2, Pallas kernels: 2.31 us -> 4.47 us  [back(): pl.pallas_call(back_kernel, grid=(weight.shape[0] // depth,), out_shape=j...]
  transfers between devices with their start and end apart: 16 -> 16, of which waited for: 12 -> 11; matrix products, arithmetic and copies ran while one was open for 0% -> 0% of each run, Pallas kernels for 13% -> 14%
where the time goes in v8:
time: 174 us; the launch traced here: 172 us
  starting transfers between devices  76.3 us (44%)
  waiting for transfers between devices  41.7 us (24%)
  Pallas kernels  33.1 us (19%)
  between operations  15 us (9%)
  local copies, waits for them, and re-layouts  5.96 us (3%)
    all_to_all x6, starting transfers between devices, exchange(): lax.all_to_all(array, axis, split_axis=0, concat_axis=0, axis_index_group...  40.1 us
    ppermute x9, starting transfers between devices, swap(): lax.ppermute(array, axis, [(rank, rank ^ step) for rank in range(ranks)])  36.2 us
    ppermute x9, waiting for transfers between devices, swap(): lax.ppermute(array, axis, [(rank, rank ^ step) for rank in range(ranks)])  24.4 us
    all_to_all x6, waiting for transfers between devices, exchange(): lax.all_to_all(array, axis, split_axis=0, concat_axis=0, axis_index_group...  16.6 us
    pallas_call x1, Pallas kernels, attention(): pl.pallas_call(functools.partial(attention_kernel, sources, tile, text_ro...  10.4 us
    unnamed x28, local copies, waits for them, and re-layouts  5.42 us
    pallas_call x2, Pallas kernels, project(): pl.pallas_call(functools.partial(project_kernel, block, begin), out_shape...  4.89 us
    pallas_call x2, Pallas kernels, back(): pl.pallas_call(back_kernel, grid=(weight.shape[0] // depth,), out_shape=j...  4.47 us
  transfers between devices with their start and end apart: 16, of which 11 were waited for; matrix products, arithmetic and copies ran while one was open for 0% of the time, Pallas kernels for 14%

profile of v8, /device:TPU:1, one launch (start us, length us, event | category | flops | bytes accessed | tf_op | source)
XLA Modules:
  0.0 172.2 jit_solution(17823317030415309580)
XLA Ops:
  7.2 0.0 all-gather.2.cloned.1.call-start
  7.2 0.7 all-gather.2.cloned.1.call-update
  8.5 3.6 %shard_map.183 = (bf16[6656,128]{1,0:T(8,128)(2,1)}, bf16[80,128]{1,0:T(8,128)(2,1)}) custom-call(s32[1]{0:T(128)S(6)} %copy.27.route_ref, s32[1,2]{1,0:T(1,128)} %counts_ref.7, bf16[1,64,128]{2,1,0:T(8,128)(2,1)} %tile_ref.1, bf16[128,2048]{1,0:T(8,128)(2,1)} %refs_0_.1, bf16[128,2048]{1,0:T(8,128)(2,1)} %refs_1_.1, bf16[128,2048]{1,0:T(8,128)(2,1)} %refs_2_.1, ...), custom_call_target="tpu_custom_call" | custom-call | tf_op jit(solution)/shard_map/pallas_call | solution.py:62
  12.3 10.5 %all-to-all-start = ((bf16[16,416,128]{2,1,0:T(8,128)(2,1)}), bf16[16,416,128]{2,1,0:T(8,128)(2,1)S(1)}, u32[]{:S(2)}, u32[]{:S(2)}) async-start(bf16[16,416,128]{2,1,0:T(8,128)(2,1)} %bitcast.36), calls=%async_computation | async-start | bytes 3407872 | tf_op jit(solution)/shard_map/all_to_all | solution.py:522
  22.8 7.1 %collective-permute-start = (bf16[80,128]{1,0:T(8,128)(2,1)S(1)}, bf16[80,128]{1,0:T(8,128)(2,1)S(1)}, u32[]{:S(2)}, u32[]{:S(2)}) collective-permute-start(bf16[80,128]{1,0:T(8,128)(2,1)S(1)} %copy-done.9), channel_id=1, source_target_pairs={{0,64},{16,80},{32,96},{48,112},{64,0},{80,16},{96,32},{112,48},{1... | collective-permute-start | bytes 61448 | tf_op jit(solution)/shard_map/ppermute | solution.py:123
  29.9 1.4 collective-permute-done
  31.3 3.8 %collective-permute-start.1 = (bf16[160,128]{1,0:T(8,128)(2,1)S(1)}, bf16[160,128]{1,0:T(8,128)(2,1)S(1)}, u32[]{:S(2)}, u32[]{:S(2)}) collective-permute-start(bf16[160,128]{1,0:T(8,128)(2,1)S(1)} %pad_maximum_fusion.1), channel_id=1, source_target_pairs={{0,32},{16,48},{32,0},{48,16},{64,96},{80,112},{96,64},{112,80},{1... | collective-permute-start | bytes 122888 | tf_op jit(solution)/shard_map/ppermute | solution.py:123
  35.1 2.1 %collective-permute-done.1 = bf16[160,128]{1,0:T(8,128)(2,1)S(1)} collective-permute-done((bf16[160,128]{1,0:T(8,128)(2,1)S(1)}, bf16[160,128]{1,0:T(8,128)(2,1)S(1)}, u32[]{:S(2)}, u32[]{:S(2)}) %collective-permute-start.1) | collective-permute-done | bytes 40992 | tf_op jit(solution)/shard_map/ppermute | solution.py:123
  37.2 2.8 %collective-permute-start.2 = (bf16[320,128]{1,0:T(8,128)(2,1)S(1)}, bf16[320,128]{1,0:T(8,128)(2,1)S(1)}, u32[]{:S(2)}, u32[]{:S(2)}) collective-permute-start(bf16[320,128]{1,0:T(8,128)(2,1)S(1)} %pad_maximum_fusion), channel_id=1, source_target_pairs={{0,16},{16,0},{32,48},{48,32},{64,80},{80,64},{96,112},{112,96},{1... | collective-permute-start | bytes 245768 | tf_op jit(solution)/shard_map/ppermute | solution.py:123
  40.1 2.7 %collective-permute-done.2 = bf16[320,128]{1,0:T(8,128)(2,1)S(1)} collective-permute-done((bf16[320,128]{1,0:T(8,128)(2,1)S(1)}, bf16[320,128]{1,0:T(8,128)(2,1)S(1)}, u32[]{:S(2)}, u32[]{:S(2)}) %collective-permute-start.2) | collective-permute-done | bytes 81952 | tf_op jit(solution)/shard_map/ppermute | solution.py:123
  42.8 5.2 %collective-permute-start.3 = (bf16[640,128]{1,0:T(8,128)(2,1)S(1)}, bf16[640,128]{1,0:T(8,128)(2,1)S(1)}, u32[]{:S(2)}, u32[]{:S(2)}) collective-permute-start(bf16[640,128]{1,0:T(8,128)(2,1)S(1)} %get-tuple-element.55), channel_id=1, source_target_pairs={{0,128},{16,144},{32,160},{48,176},{64,192},{80,208},{96,224},{112... | collective-permute-start | bytes 491528 | tf_op jit(solution)/shard_map/ppermute | solution.py:123
  48.0 0.1 maximum_bitcast_fusion
  48.1 7.1 %collective-permute-done.3 = bf16[640,128]{1,0:T(8,128)(2,1)S(1)} collective-permute-done((bf16[640,128]{1,0:T(8,128)(2,1)S(1)}, bf16[640,128]{1,0:T(8,128)(2,1)S(1)}, u32[]{:S(2)}, u32[]{:S(2)}) %collective-permute-start.3) | collective-permute-done | bytes 163872 | tf_op jit(solution)/shard_map/ppermute | solution.py:123
  55.2 10.4 %shard_map.184 = bf16[2048,128]{1,0:T(8,128)(2,1)} custom-call(s32[1,2]{1,0:T(1,128)S(1)} %copy-done.7, s32[1,2]{1,0:T(1,128)S(1)} %copy-done.8, bf16[6656,128]{1,0:T(8,128)(2,1)S(1)} %bitcast.28, f32[1,128]{1,0:T(1,128)S(1)} %get-tuple-element.64.query_gain_ref, f32[1,128]{1,0:T(1,128)S(1)} %get-tuple-element.65.key_gain_ref), custom_call_target="tpu_custom_call" | custom-call | flops 4831838208 | bytes 4194304 | tf_op jit(solution)/shard_map/pallas_call | solution.py:221
  65.7 5.0 %all-to-all-start.1 = ((bf16[8,256,128]{2,1,0:T(8,128)(2,1)}), bf16[8,256,128]{2,1,0:T(8,128)(2,1)S(1)}, u32[]{:S(2)}, u32[]{:S(2)}) async-start(bf16[8,256,128]{2,1,0:T(8,128)(2,1)} %bitcast.6), calls=%async_computation.1 | async-start | bytes 1048576 | tf_op jit(solution)/shard_map/all_to_all | solution.py:522
  70.7 0.1 shard_map.185
  70.9 5.6 %collective-permute-start.4 = (bf16[80,128]{1,0:T(8,128)(2,1)S(1)}, bf16[80,128]{1,0:T(8,128)(2,1)S(1)}, u32[]{:S(2)}, u32[]{:S(2)}) collective-permute-start(bf16[80,128]{1,0:T(8,128)(2,1)S(1)} %get-tuple-element.56), channel_id=1, source_target_pairs={{0,256},{16,272},{32,288},{48,304},{64,320},{80,336},{96,352},{112... | collective-permute-start | bytes 61448 | tf_op jit(solution)/shard_map/ppermute | solution.py:123
  76.5 2.8 %collective-permute-done.4.far_ref = bf16[80,128]{1,0:T(8,128)(2,1)S(1)} collective-permute-done((bf16[80,128]{1,0:T(8,128)(2,1)S(1)}, bf16[80,128]{1,0:T(8,128)(2,1)S(1)}, u32[]{:S(2)}, u32[]{:S(2)}) %collective-permute-start.4) | collective-permute-done | bytes 20512 | tf_op jit(solution)/shard_map/ppermute | solution.py:123
  79.3 0.9 all-to-all-done.1
  80.2 2.5 %shard_map.186 = (f32[128,1280]{1,0:T(8,128)S(1)}, bf16[128,1280]{1,0:T(8,128)(2,1)S(1)}) custom-call(s32[1]{0:T(128)} %bitcast.1.half_ref, bf16[2048,128]{1,0:T(8,128)(2,1)S(1)} %bitcast.26, bf16[1024,2432]{1,0:T(8,128)(2,1)} %all-gather.2.cloned.1.call-done.weight_ref), custom_call_target="tpu_custom_call" | custom-call | flops 671088640 | bytes 2621440 | tf_op jit(solution)/shard_map/pallas_call | solution.py:304
  82.7 0.8 copy-done.3
  83.5 2.2 %collective-permute-start.5 = (bf16[128,1280]{1,0:T(8,128)(2,1)S(1)}, bf16[128,1280]{1,0:T(8,128)(2,1)S(1)}, u32[]{:S(2)}, u32[]{:S(2)}) collective-permute-start(bf16[128,1280]{1,0:T(8,128)(2,1)S(1)} %get-tuple-element.37), channel_id=1, source_target_pairs={{0,8},{1,9},{2,10},{3,11},{4,12},{5,13},{6,14},{7,15},{8,0},{9,1},... | collective-permute-start | bytes 983048 | tf_op jit(solution)/shard_map/ppermute | solution.py:123
  85.6 2.4 %shard_map.187 = (f32[128,1152]{1,0:T(8,128)S(1)}, bf16[128,1152]{1,0:T(8,128)(2,1)S(1)}) custom-call(s32[1]{0:T(128)} %bitcast.1.half_ref, bf16[2048,128]{1,0:T(8,128)(2,1)S(1)} %bitcast.27, bf16[1024,2432]{1,0:T(8,128)(2,1)} %all-gather.2.cloned.1.call-done.weight_ref), custom_call_target="tpu_custom_call" | custom-call | flops 603979776 | bytes 2359296 | tf_op jit(solution)/shard_map/pallas_call | solution.py:304
  88.1 0.8 copy-done.4
  88.9 3.2 %collective-permute-start.6 = (bf16[128,1152]{1,0:T(8,128)(2,1)S(1)}, bf16[128,1152]{1,0:T(8,128)(2,1)S(1)}, u32[]{:S(2)}, u32[]{:S(2)}) collective-permute-start(bf16[128,1152]{1,0:T(8,128)(2,1)S(1)} %get-tuple-element.38), channel_id=1, source_target_pairs={{0,8},{1,9},{2,10},{3,11},{4,12},{5,13},{6,14},{7,15},{8,0},{9,1},... | collective-permute-start | bytes 884744 | tf_op jit(solution)/shard_map/ppermute | solution.py:123
  92.1 8.0 %collective-permute-done.6.other_right_ref = bf16[128,1152]{1,0:T(8,128)(2,1)S(1)} collective-permute-done((bf16[128,1152]{1,0:T(8,128)(2,1)S(1)}, bf16[128,1152]{1,0:T(8,128)(2,1)S(1)}, u32[]{:S(2)}, u32[]{:S(2)}) %collective-permute-start.6) | collective-permute-done | bytes 294944 | tf_op jit(solution)/shard_map/ppermute | solution.py:123
  100.2 4.4 %shard_map.188 = (f32[64,128]{1,0:T(8,128)}, bf16[20,64,128]{2,1,0:T(8,128)(2,1)}, f32[8,128]{1,0:T(8,128)S(1)}, f32[128,2432]{1,0:T(8,128)}, f32[128,128]{1,0:T(8,128)S(1)}, /*index=5*/f32[64,128]{1,0:T(8,128)S(1)}) custom-call(s32[1]{0:T(128)} %bitcast.place_ref, s32[1,2]{1,0:T(1,128)S(1)} %copy-done.7, f32[128,1280]{1,0:T(8,128)} %copy-done.3, ...), custom_call_target="tpu_custom_call" | custom-call | tf_op jit(solution)/shard_map/pallas_call | solution.py:382
  104.6 5.4 %all-to-all-start.2 = ((bf16[16,80,128]{2,1,0:T(8,128)(2,1)}), bf16[16,80,128]{2,1,0:T(8,128)(2,1)S(1)}, u32[]{:S(2)}, u32[]{:S(2)}) async-start(bf16[16,80,128]{2,1,0:T(8,128)(2,1)} %bitcast.15), calls=%async_computation.2 | async-start | bytes 655360 | tf_op jit(solution)/shard_map/all_to_all | solution.py:522
  109.9 1.3 copy-done.1
  111.2 1.4 shard_map.189.grad_ref
  112.6 3.3 %collective-permute-start.7 = (bf16[128,2432]{1,0:T(8,128)(2,1)S(1)}, bf16[128,2432]{1,0:T(8,128)(2,1)S(1)}, u32[]{:S(2)}, u32[]{:S(2)}) collective-permute-start(bf16[128,2432]{1,0:T(8,128)(2,1)S(1)} %shard_map.189.grad_ref), channel_id=1, source_target_pairs={{0,8},{1,9},{2,10},{3,11},{4,12},{5,13},{6,14},{7,15},{8,0},{9,1},... | collective-permute-start | bytes 1867784 | tf_op jit(solution)/shard_map/ppermute | solution.py:123
  115.9 1.7 all-to-all-done.2
  117.6 0.7 shard_map.193
  118.3 6.9 %all-to-all-start.3 = ((bf16[8,80,128]{2,1,0:T(8,128)(2,1)}), bf16[8,80,128]{2,1,0:T(8,128)(2,1)S(1)}, u32[]{:S(2)}, u32[]{:S(2)}) async-start(bf16[8,80,128]{2,1,0:T(8,128)(2,1)} %shard_map.193), calls=%async_computation.3 | async-start | bytes 327680 | tf_op jit(solution)/shard_map/all_to_all | solution.py:522
  125.2 2.4 %copy-done = bf16[1024,2432]{1,0:T(8,128)(2,1)S(1)} copy-done((bf16[1024,2432]{1,0:T(8,128)(2,1)S(1)}, bf16[1024,2432]{1,0:T(8,128)(2,1)}, u32[]{:S(2)}) %copy-start) | copy-done | bytes 4980760
  127.6 2.2 %shard_map.190.own_ref = bf16[128,1024]{1,0:T(8,128)(2,1)S(1)} custom-call(bf16[128,2432]{1,0:T(8,128)(2,1)S(1)} %shard_map.189.grad_ref, bf16[1024,2432]{1,0:T(8,128)(2,1)S(1)} %copy-done), custom_call_target="tpu_custom_call" | custom-call | flops 637534208 | bytes 4980736 | tf_op jit(solution)/shard_map/pallas_call | solution.py:437
  129.8 0.2 collective-permute-done.7.grad_ref
  130.1 2.2 %shard_map.191 = bf16[128,1024]{1,0:T(8,128)(2,1)S(1)} custom-call(bf16[128,2432]{1,0:T(8,128)(2,1)S(1)} %collective-permute-done.7.grad_ref, bf16[1024,2432]{1,0:T(8,128)(2,1)S(1)} %copy-done), custom_call_target="tpu_custom_call" | custom-call | flops 637534208 | bytes 4980736 | tf_op jit(solution)/shard_map/pallas_call | solution.py:437
  132.3 3.0 %collective-permute-start.8 = (bf16[128,1024]{1,0:T(8,128)(2,1)S(1)}, bf16[128,1024]{1,0:T(8,128)(2,1)S(1)}, u32[]{:S(2)}, u32[]{:S(2)}) collective-permute-start(bf16[128,1024]{1,0:T(8,128)(2,1)S(1)} %shard_map.191), channel_id=1, source_target_pairs={{0,8},{1,9},{2,10},{3,11},{4,12},{5,13},{6,14},{7,15},{8,0},{9,1},... | collective-permute-start | bytes 786440 | tf_op jit(solution)/shard_map/ppermute | solution.py:123
  135.3 0.7 shard_map.194
  136.0 5.8 %all-to-all-start.4 = ((bf16[4,80,128]{2,1,0:T(8,128)(2,1)}), bf16[4,80,128]{2,1,0:T(8,128)(2,1)S(1)}, u32[]{:S(2)}, u32[]{:S(2)}) async-start(bf16[4,80,128]{2,1,0:T(8,128)(2,1)} %shard_map.194), calls=%async_computation.4 | async-start | bytes 163840 | tf_op jit(solution)/shard_map/all_to_all | solution.py:522
  141.7 7.2 %all-to-all-done.4 = bf16[4,80,128]{2,1,0:T(8,128)(2,1)S(1)} async-done(((bf16[4,80,128]{2,1,0:T(8,128)(2,1)}), bf16[4,80,128]{2,1,0:T(8,128)(2,1)S(1)}, u32[]{:S(2)}, u32[]{:S(2)}) %all-to-all-start.4) | async-done | bytes 81952 | tf_op jit(solution)/shard_map/all_to_all | solution.py:522
  148.9 0.8 shard_map.195
  149.7 6.6 %all-to-all-start.5 = ((bf16[16,80,128]{2,1,0:T(8,128)(2,1)}), bf16[16,80,128]{2,1,0:T(8,128)(2,1)S(1)}, u32[]{:S(2)}, u32[]{:S(2)}) async-start(bf16[16,80,128]{2,1,0:T(8,128)(2,1)} %shard_map.195), calls=%async_computation.5 | async-start | bytes 655360 | tf_op jit(solution)/shard_map/all_to_all | solution.py:522
  156.3 0.8 shard_map.192
  157.1 6.9 %all-to-all-done.5 = bf16[16,80,128]{2,1,0:T(8,128)(2,1)S(1)} async-done(((bf16[16,80,128]{2,1,0:T(8,128)(2,1)}), bf16[16,80,128]{2,1,0:T(8,128)(2,1)S(1)}, u32[]{:S(2)}, u32[]{:S(2)}) %all-to-all-start.5) | async-done | bytes 327712 | tf_op jit(solution)/shard_map/all_to_all | solution.py:522
  164.0 0.9 shard_map.196
  164.8 0.5 slice.11
  (33 shorter events, 0.2 us)
Async XLA Ops:
  7.2 73.0 %all-gather.2.cloned.1.call-start = ((), (), s32[]{:S(2)}) async-start(), calls=%async_computation.6 | async-start | bytes 5603328 | tf_op jit(solution)/shard_map/all_gather | solution.py:546
  12.2 10.6 %copy-start.9 = (bf16[80,128]{1,0:T(8,128)(2,1)S(1)}, bf16[80,128]{1,0:T(8,128)(2,1)}, u32[]{:S(2)}) copy-start(bf16[80,128]{1,0:T(8,128)(2,1)} %get-tuple-element.30) | copy-start | bytes 61444
  12.2 35.8 %copy-start.10 = (f32[64]{0:T(128)S(1)}, f32[64]{0:T(128)}, u32[]{:S(2)}) copy-start(f32[64]{0:T(128)} %param.25) | copy-start | bytes 772
  12.2 35.8 %copy-start.11 = (f32[64]{0:T(128)S(1)}, f32[64]{0:T(128)}, u32[]{:S(2)}) copy-start(f32[64]{0:T(128)} %param.26) | copy-start | bytes 772
  12.2 43.0 %copy-start.7 = (s32[1,2]{1,0:T(1,128)S(1)}, s32[1,2]{1,0:T(1,128)}, u32[]{:S(2)}) copy-start(s32[1,2]{1,0:T(1,128)} %counts_ref.7) | copy-start | bytes 28
  12.2 43.0 %copy-start.8 = (s32[1,2]{1,0:T(1,128)S(1)}, s32[1,2]{1,0:T(1,128)}, u32[]{:S(2)}) copy-start(s32[1,2]{1,0:T(1,128)} %lengths_ref.1) | copy-start | bytes 28
  12.3 43.0 %all-to-all-start = ((bf16[16,416,128]{2,1,0:T(8,128)(2,1)}), bf16[16,416,128]{2,1,0:T(8,128)(2,1)S(1)}, u32[]{:S(2)}, u32[]{:S(2)}) async-start(bf16[16,416,128]{2,1,0:T(8,128)(2,1)} %bitcast.36), calls=%async_computation | async-start | bytes 3407872 | tf_op jit(solution)/shard_map/all_to_all | solution.py:522
  22.8 8.5 %collective-permute-start = (bf16[80,128]{1,0:T(8,128)(2,1)S(1)}, bf16[80,128]{1,0:T(8,128)(2,1)S(1)}, u32[]{:S(2)}, u32[]{:S(2)}) collective-permute-start(bf16[80,128]{1,0:T(8,128)(2,1)S(1)} %copy-done.9), channel_id=1, source_target_pairs={{0,64},{16,80},{32,96},{48,112},{64,0},{80,16},{96,32},{112,48},{1... | collective-permute-start | bytes 61448 | tf_op jit(solution)/shard_map/ppermute | solution.py:123
  31.3 5.9 %collective-permute-start.1 = (bf16[160,128]{1,0:T(8,128)(2,1)S(1)}, bf16[160,128]{1,0:T(8,128)(2,1)S(1)}, u32[]{:S(2)}, u32[]{:S(2)}) collective-permute-start(bf16[160,128]{1,0:T(8,128)(2,1)S(1)} %pad_maximum_fusion.1), channel_id=1, source_target_pairs={{0,32},{16,48},{32,0},{48,16},{64,96},{80,112},{96,64},{112,80},{1... | collective-permute-start | bytes 122888 | tf_op jit(solution)/shard_map/ppermute | solution.py:123
  37.2 5.6 %collective-permute-start.2 = (bf16[320,128]{1,0:T(8,128)(2,1)S(1)}, bf16[320,128]{1,0:T(8,128)(2,1)S(1)}, u32[]{:S(2)}, u32[]{:S(2)}) collective-permute-start(bf16[320,128]{1,0:T(8,128)(2,1)S(1)} %pad_maximum_fusion), channel_id=1, source_target_pairs={{0,16},{16,0},{32,48},{48,32},{64,80},{80,64},{96,112},{112,96},{1... | collective-permute-start | bytes 245768 | tf_op jit(solution)/shard_map/ppermute | solution.py:123
  42.8 12.3 %collective-permute-start.3 = (bf16[640,128]{1,0:T(8,128)(2,1)S(1)}, bf16[640,128]{1,0:T(8,128)(2,1)S(1)}, u32[]{:S(2)}, u32[]{:S(2)}) collective-permute-start(bf16[640,128]{1,0:T(8,128)(2,1)S(1)} %get-tuple-element.55), channel_id=1, source_target_pairs={{0,128},{16,144},{32,160},{48,176},{64,192},{80,208},{96,224},{112... | collective-permute-start | bytes 491528 | tf_op jit(solution)/shard_map/ppermute | solution.py:123
  65.7 14.5 %all-to-all-start.1 = ((bf16[8,256,128]{2,1,0:T(8,128)(2,1)}), bf16[8,256,128]{2,1,0:T(8,128)(2,1)S(1)}, u32[]{:S(2)}, u32[]{:S(2)}) async-start(bf16[8,256,128]{2,1,0:T(8,128)(2,1)} %bitcast.6), calls=%async_computation.1 | async-start | bytes 1048576 | tf_op jit(solution)/shard_map/all_to_all | solution.py:522
  70.9 8.4 %collective-permute-start.4 = (bf16[80,128]{1,0:T(8,128)(2,1)S(1)}, bf16[80,128]{1,0:T(8,128)(2,1)S(1)}, u32[]{:S(2)}, u32[]{:S(2)}) collective-permute-start(bf16[80,128]{1,0:T(8,128)(2,1)S(1)} %get-tuple-element.56), channel_id=1, source_target_pairs={{0,256},{16,272},{32,288},{48,304},{64,320},{80,336},{96,352},{112... | collective-permute-start | bytes 61448 | tf_op jit(solution)/shard_map/ppermute | solution.py:123
  82.6 0.8 copy-start.3
  83.5 16.7 %copy-start.2 = (bf16[2432,64]{0,1:T(8,128)(2,1)S(1)}, bf16[2432,64]{0,1:T(8,128)(2,1)}, u32[]{:S(2)}) copy-start(bf16[2432,64]{0,1:T(8,128)(2,1)} %param.30) | copy-start | bytes 933892
  83.5 16.7 %copy-start.5 = (f32[2,7296]{1,0:T(2,128)S(1)}, f32[2,7296]{1,0:T(2,128)}, u32[]{:S(2)}) copy-start(f32[2,7296]{1,0:T(2,128)} %modulate_ref.3) | copy-start | bytes 175108
  83.5 16.7 %copy-start.6 = (bf16[1,64,128]{2,1,0:T(8,128)(2,1)S(1)}, bf16[1,64,128]{2,1,0:T(8,128)(2,1)}, u32[]{:S(2)}) copy-start(bf16[1,64,128]{2,1,0:T(8,128)(2,1)} %param.31) | copy-start | bytes 49156
  83.5 16.7 %collective-permute-start.5 = (bf16[128,1280]{1,0:T(8,128)(2,1)S(1)}, bf16[128,1280]{1,0:T(8,128)(2,1)S(1)}, u32[]{:S(2)}, u32[]{:S(2)}) collective-permute-start(bf16[128,1280]{1,0:T(8,128)(2,1)S(1)} %get-tuple-element.37), channel_id=1, source_target_pairs={{0,8},{1,9},{2,10},{3,11},{4,12},{5,13},{6,14},{7,15},{8,0},{9,1},... | collective-permute-start | bytes 983048 | tf_op jit(solution)/shard_map/ppermute | solution.py:123
  88.1 0.8 copy-start.4
  88.9 11.3 %collective-permute-start.6 = (bf16[128,1152]{1,0:T(8,128)(2,1)S(1)}, bf16[128,1152]{1,0:T(8,128)(2,1)S(1)}, u32[]{:S(2)}, u32[]{:S(2)}) collective-permute-start(bf16[128,1152]{1,0:T(8,128)(2,1)S(1)} %get-tuple-element.38), channel_id=1, source_target_pairs={{0,8},{1,9},{2,10},{3,11},{4,12},{5,13},{6,14},{7,15},{8,0},{9,1},... | collective-permute-start | bytes 884744 | tf_op jit(solution)/shard_map/ppermute | solution.py:123
  104.6 13.0 %all-to-all-start.2 = ((bf16[16,80,128]{2,1,0:T(8,128)(2,1)}), bf16[16,80,128]{2,1,0:T(8,128)(2,1)S(1)}, u32[]{:S(2)}, u32[]{:S(2)}) async-start(bf16[16,80,128]{2,1,0:T(8,128)(2,1)} %bitcast.15), calls=%async_computation.2 | async-start | bytes 655360 | tf_op jit(solution)/shard_map/all_to_all | solution.py:522
  109.9 1.3 copy-start.1
  112.6 17.5 %collective-permute-start.7 = (bf16[128,2432]{1,0:T(8,128)(2,1)S(1)}, bf16[128,2432]{1,0:T(8,128)(2,1)S(1)}, u32[]{:S(2)}, u32[]{:S(2)}) collective-permute-start(bf16[128,2432]{1,0:T(8,128)(2,1)S(1)} %shard_map.189.grad_ref), channel_id=1, source_target_pairs={{0,8},{1,9},{2,10},{3,11},{4,12},{5,13},{6,14},{7,15},{8,0},{9,1},... | collective-permute-start | bytes 1867784 | tf_op jit(solution)/shard_map/ppermute | solution.py:123
  118.3 17.0 %all-to-all-start.3 = ((bf16[8,80,128]{2,1,0:T(8,128)(2,1)}), bf16[8,80,128]{2,1,0:T(8,128)(2,1)S(1)}, u32[]{:S(2)}, u32[]{:S(2)}) async-start(bf16[8,80,128]{2,1,0:T(8,128)(2,1)} %shard_map.193), calls=%async_computation.3 | async-start | bytes 327680 | tf_op jit(solution)/shard_map/all_to_all | solution.py:522
  125.2 2.4 %copy-start = (bf16[1024,2432]{1,0:T(8,128)(2,1)S(1)}, bf16[1024,2432]{1,0:T(8,128)(2,1)}, u32[]{:S(2)}) copy-start(bf16[1024,2432]{1,0:T(8,128)(2,1)} %all-gather.2.cloned.1.call-done.weight_ref) | copy-start | bytes 14942212
  132.3 9.4 %collective-permute-start.8 = (bf16[128,1024]{1,0:T(8,128)(2,1)S(1)}, bf16[128,1024]{1,0:T(8,128)(2,1)S(1)}, u32[]{:S(2)}, u32[]{:S(2)}) collective-permute-start(bf16[128,1024]{1,0:T(8,128)(2,1)S(1)} %shard_map.191), channel_id=1, source_target_pairs={{0,8},{1,9},{2,10},{3,11},{4,12},{5,13},{6,14},{7,15},{8,0},{9,1},... | collective-permute-start | bytes 786440 | tf_op jit(solution)/shard_map/ppermute | solution.py:123
  136.0 12.9 %all-to-all-start.4 = ((bf16[4,80,128]{2,1,0:T(8,128)(2,1)}), bf16[4,80,128]{2,1,0:T(8,128)(2,1)S(1)}, u32[]{:S(2)}, u32[]{:S(2)}) async-start(bf16[4,80,128]{2,1,0:T(8,128)(2,1)} %shard_map.194), calls=%async_computation.4 | async-start | bytes 163840 | tf_op jit(solution)/shard_map/all_to_all | solution.py:522
  149.7 14.3 %all-to-all-start.5 = ((bf16[16,80,128]{2,1,0:T(8,128)(2,1)}), bf16[16,80,128]{2,1,0:T(8,128)(2,1)S(1)}, u32[]{:S(2)}, u32[]{:S(2)}) async-start(bf16[16,80,128]{2,1,0:T(8,128)(2,1)} %shard_map.195), calls=%async_computation.5 | async-start | bytes 655360 | tf_op jit(solution)/shard_map/all_to_all | solution.py:522
Sparse Core Ops, SparseCore 0:
  10.1 56.9 all-gather.1
